TPU v7x, 32 devices: a whole 2x2x4 slice. The times are simulated.
32 devices in a mesh: dp: 8 (over y, x, core), table: 4 (over z).
Axes of the slice: x: 2, y: 2, z: 4, core: 2. Of those that a mesh axis runs over, the one named last changes fastest.
Arguments:
- features: bfloat16 [3, 8, 2048, 100], P(None, 'dp', 'table'), may hold values from -6 to 6
- feature_mask: int32 [3, 8, 100], P(None, 'dp'), may hold values 0 or 1
- support_count: int32 [3, 8], P(None, 'dp'), may hold values from 1537 to 2047
- embed_weight: bfloat16 [100, 512], P(None, 'dp'), may hold values from -0.625 to 0.625
- embed_bias: bfloat16 [512], P('dp'), may hold values from -3 to 3
- gain_first: bfloat16 [512], P('dp'), may hold values from 0.5 to 1.5
- shift_first: bfloat16 [512], P('dp'), may hold values from -2 to 2
- query_weight: bfloat16 [512, 512], P('dp'), may hold values from -0.375 to 0.375
- key_weight: bfloat16 [512, 512], P('dp'), may hold values from -0.375 to 0.375
- value_weight: bfloat16 [512, 512], P('dp'), may hold values from -0.25 to 0.25
- out_weight: bfloat16 [512, 512], P('dp'), may hold values from -1.5 to 1.5
- gain_second: bfloat16 [512], P('dp'), may hold values from 0.5 to 1.5
- shift_second: bfloat16 [512], P('dp'), may hold values from -2 to 2
- up_weight: bfloat16 [512, 2048], P('dp'), may hold values from -0.25 to 0.25
- up_bias: bfloat16 [2048], P('dp'), may hold values from -3 to 3
- down_weight: bfloat16 [2048, 512], P('dp'), may hold values from -0.125 to 0.125
- down_bias: bfloat16 [512], P('dp'), may hold values from -2 to 2
- cotangent: bfloat16 [3, 8, 2048, 512], P(None, 'dp', 'table'), may hold values from -6 to 6
Outputs:
- activations: bfloat16 [3, 8, 2048, 512], P(None, 'dp', 'table')
- input_grad: float32 [3, 8, 2048, 100], P(None, 'dp', 'table')
- grad_embed_weight: float32 [100, 512], P(None, 'dp')
- grad_embed_bias: float32 [512], P('dp')
- grad_gain_first: float32 [512], P('dp')
- grad_shift_first: float32 [512], P('dp')
- grad_query_weight: float32 [512, 512], P('dp')
- grad_key_weight: float32 [512, 512], P('dp')
- grad_value_weight: float32 [512, 512], P('dp')
- grad_out_weight: float32 [512, 512], P('dp')
- grad_gain_second: float32 [512], P('dp')
- grad_shift_second: float32 [512], P('dp')
- grad_up_weight: float32 [512, 2048], P('dp')
- grad_up_bias: float32 [2048], P('dp')
- grad_down_weight: float32 [2048, 512], P('dp')
- grad_down_bias: float32 [512], P('dp')
Inputs may be any that keep to these rules, and one draw needn't show every extreme that they name: A table's first support_count rows are its support rows; the other rows are queries. Every row attends to the support rows only.
All inputs are finite; a program needn't handle non-finite values. No bound on the sum of `feature_mask` on one device may be relied on, other than what follows from the above.
Results may differ from a plain program's by a relative error of at most 0.014.
Values may be sent and summed in bfloat16 or wider, within the bound.
A program may use at most 256 MiB of HBM per device.

v0:
```python
import jax
import jax.numpy as jnp
from jax import lax
from jax.sharding import PartitionSpec as P

HEADS = 4
HEAD_DIM = 128


epsilon = 1e-05
inv_sqrt_two = 0.7071067811865476
inv_sqrt_two_pi = 0.3989422804014327


def inner(left_side, right_side):
    return lax.dot_general(
        left_side, right_side, (((0,), (0,)), ((), ())), preferred_element_type=jnp.float32
    )


def times_back(left_side, right_side):
    return lax.dot_general(
        left_side, right_side, (((1,), (1,)), ((), ())), preferred_element_type=jnp.float32
    )


def norm_forward(values_in):
    row_mean = jnp.mean(values_in, axis=-1, keepdims=True)
    centred = values_in - row_mean
    inv_scale = lax.rsqrt(jnp.mean(centred * centred, axis=-1, keepdims=True) + epsilon)
    return (centred * inv_scale, inv_scale)


def norm_backward(grad_norm, unit_vals, inv_scale, gain_vec):
    scaled = grad_norm * gain_vec
    return inv_scale * (
        scaled
        - jnp.mean(scaled, axis=-1, keepdims=True)
        - unit_vals * jnp.mean(scaled * unit_vals, axis=-1, keepdims=True)
    )


def fetch_weights(shards):
    return (
        lax.all_gather(shards[0], "dp", axis=1, tiled=True),
        lax.all_gather(shards[1], "dp", axis=0, tiled=True),
        lax.all_gather(shards[2], "dp", axis=0, tiled=True),
        lax.all_gather(shards[3], "dp", axis=0, tiled=True),
        lax.all_gather(shards[4], "dp", axis=0, tiled=True),
        lax.all_gather(shards[5], "dp", axis=0, tiled=True),
        lax.all_gather(shards[6], "dp", axis=0, tiled=True),
        lax.all_gather(shards[7], "dp", axis=0, tiled=True),
        lax.all_gather(shards[8], "dp", axis=0, tiled=True),
        lax.all_gather(shards[9], "dp", axis=0, tiled=True),
        lax.all_gather(shards[10], "dp", axis=0, tiled=True),
        lax.all_gather(shards[11], "dp", axis=0, tiled=True),
        lax.all_gather(shards[12], "dp", axis=0, tiled=True),
        lax.all_gather(shards[13], "dp", axis=0, tiled=True),
    )


def add_grads(summed, adding):
    if summed is None:
        return adding
    return jax.tree.map(lambda carried, extra: carried + extra, summed, adding)


def body(
    features,
    feature_mask,
    support_count,
    embed_weight,
    embed_bias,
    gain_first,
    shift_first,
    query_weight,
    key_weight,
    value_weight,
    out_weight,
    gain_second,
    shift_second,
    up_weight,
    up_bias,
    down_weight,
    down_bias,
    cotangent,
):
    shards = (
        embed_weight,
        embed_bias,
        gain_first,
        shift_first,
        query_weight,
        key_weight,
        value_weight,
        out_weight,
        gain_second,
        shift_second,
        up_weight,
        up_bias,
        down_weight,
        down_bias,
    )
    micro_count = features.shape[0]
    rows_here = features.shape[2]
    width = query_weight.shape[1]
    score_scale = HEAD_DIM ** (-0.5)
    results = []
    feat_grads = []
    summed = None
    for batch_index in range(micro_count):
        gathered = fetch_weights(shards)
        (
            embed_all,
            ebias_all,
            gain_one,
            shift_one,
            query_all,
            key_all,
            value_all,
            out_all,
            gain_two,
            shift_two,
            up_all,
            ubias_all,
            down_all,
            dbias_all,
        ) = gathered
        mask_row = feature_mask[batch_index, 0]
        masked = features[batch_index, 0] * mask_row.astype(jnp.bfloat16)[None, :]
        embedded = jnp.dot(
            masked, embed_all, preferred_element_type=jnp.float32
        ) + ebias_all.astype(jnp.float32)
        unit_one, inv_one = norm_forward(embedded)
        gain_one_f = gain_one.astype(jnp.float32)
        normed = (unit_one * gain_one_f + shift_one.astype(jnp.float32)).astype(jnp.bfloat16)
        queries = jnp.dot(normed, query_all, preferred_element_type=jnp.float32).astype(
            jnp.bfloat16
        )
        key_here = jnp.dot(normed, key_all, preferred_element_type=jnp.float32).astype(jnp.bfloat16)
        value_here = jnp.dot(normed, value_all, preferred_element_type=jnp.float32).astype(
            jnp.bfloat16
        )
        all_keys, all_values = (
            lax.all_gather(key_here, "table", axis=0, tiled=True),
            lax.all_gather(value_here, "table", axis=0, tiled=True),
        )
        length = all_keys.shape[0]
        query_heads = queries.reshape(rows_here, HEADS, HEAD_DIM)
        key_heads = all_keys.reshape(length, HEADS, HEAD_DIM)
        value_heads = all_values.reshape(length, HEADS, HEAD_DIM)
        support_now = support_count[batch_index, 0]
        is_support = jnp.arange(length, dtype=jnp.int32) < support_now

        def scores_of():
            raw = jnp.einsum(
                "rhd,lhd->hrl", query_heads, key_heads, preferred_element_type=jnp.float32
            )
            return jnp.where(is_support[None, None, :], raw * score_scale, -1e30)

        scores = scores_of()
        row_max = jnp.max(scores, axis=-1, keepdims=True)
        log_total = row_max + jnp.log(jnp.sum(jnp.exp(scores - row_max), axis=-1, keepdims=True))
        attn_probs = jnp.exp(scores - log_total)
        mixed = (
            jnp.einsum(
                "hrl,lhd->rhd",
                attn_probs.astype(jnp.bfloat16),
                value_heads,
                preferred_element_type=jnp.float32,
            )
            .reshape(rows_here, width)
            .astype(jnp.bfloat16)
        )
        hidden = embedded + jnp.dot(mixed, out_all, preferred_element_type=jnp.float32)
        unit_two, inv_two = norm_forward(hidden)
        gain_two_f = gain_two.astype(jnp.float32)
        normed_two = (unit_two * gain_two_f + shift_two.astype(jnp.float32)).astype(jnp.bfloat16)
        pre_act = jnp.dot(
            normed_two, up_all, preferred_element_type=jnp.float32
        ) + ubias_all.astype(jnp.float32)
        activated = jax.nn.gelu(pre_act, approximate=False).astype(jnp.bfloat16)
        output = (
            hidden
            + jnp.dot(activated, down_all, preferred_element_type=jnp.float32)
            + dbias_all.astype(jnp.float32)
        )
        results.append(output.astype(jnp.bfloat16))
        gathered = (
            lax.all_gather(shards[0], "dp", axis=1, tiled=True),
            lax.all_gather(shards[1], "dp", axis=0, tiled=True),
            lax.all_gather(shards[2], "dp", axis=0, tiled=True),
            lax.all_gather(shards[3], "dp", axis=0, tiled=True),
            lax.all_gather(shards[4], "dp", axis=0, tiled=True),
            lax.all_gather(shards[5], "dp", axis=0, tiled=True),
            lax.all_gather(shards[6], "dp", axis=0, tiled=True),
            lax.all_gather(shards[7], "dp", axis=0, tiled=True),
            lax.all_gather(shards[8], "dp", axis=0, tiled=True),
            lax.all_gather(shards[9], "dp", axis=0, tiled=True),
            lax.all_gather(shards[10], "dp", axis=0, tiled=True),
            lax.all_gather(shards[11], "dp", axis=0, tiled=True),
            lax.all_gather(shards[12], "dp", axis=0, tiled=True),
            lax.all_gather(shards[13], "dp", axis=0, tiled=True),
        )
        (
            embed_all,
            ebias_all,
            gain_one,
            shift_one,
            query_all,
            key_all,
            value_all,
            out_all,
            gain_two,
            shift_two,
            up_all,
            ubias_all,
            down_all,
            dbias_all,
        ) = gathered
        grad_out = cotangent[batch_index, 0]
        grad_down_bias = jnp.sum(grad_out.astype(jnp.float32), axis=0)
        grad_down_weight = inner(activated, grad_out)
        grad_act = times_back(grad_out, down_all)
        normal_cdf = 0.5 * (1.0 + lax.erf(pre_act * inv_sqrt_two))
        normal_pdf = jnp.exp(-0.5 * pre_act * pre_act) * inv_sqrt_two_pi
        grad_pre = (grad_act * (normal_cdf + pre_act * normal_pdf)).astype(jnp.bfloat16)
        grad_up_bias = jnp.sum(grad_pre.astype(jnp.float32), axis=0)
        grad_up_weight = inner(normed_two, grad_pre)
        grad_norm_two = times_back(grad_pre, up_all)
        grad_gain_second = jnp.sum(grad_norm_two * unit_two, axis=0)
        grad_shift_second = jnp.sum(grad_norm_two, axis=0)
        grad_hidden = grad_out.astype(jnp.float32) + norm_backward(
            grad_norm_two, unit_two, inv_two, gain_two_f
        )
        grad_branch = grad_hidden.astype(jnp.bfloat16)
        grad_out_weight = inner(mixed, grad_branch)
        grad_mixed = (
            times_back(grad_branch, out_all)
            .astype(jnp.bfloat16)
            .reshape(rows_here, HEADS, HEAD_DIM)
        )
        attn_probs = jnp.exp(scores_of() - log_total)
        grad_probs = jnp.einsum(
            "rhd,lhd->hrl", grad_mixed, value_heads, preferred_element_type=jnp.float32
        )
        prob_dot = jnp.sum(attn_probs * grad_probs, axis=-1, keepdims=True)
        grad_scores = (attn_probs * (grad_probs - prob_dot)).astype(jnp.bfloat16)
        grad_queries = (
            (
                jnp.einsum(
                    "hrl,lhd->rhd", grad_scores, key_heads, preferred_element_type=jnp.float32
                )
                * score_scale
            )
            .reshape(rows_here, width)
            .astype(jnp.bfloat16)
        )
        grad_values = jnp.einsum(
            "hrl,rhd->lhd",
            attn_probs.astype(jnp.bfloat16),
            grad_mixed,
            preferred_element_type=jnp.float32,
        ).reshape(length, width)
        grad_keys = (
            jnp.einsum(
                "hrl,rhd->lhd", grad_scores, query_heads, preferred_element_type=jnp.float32
            ).reshape(length, width)
            * score_scale
        )
        key_back, value_back = (
            lax.psum_scatter(grad_keys, "table", scatter_dimension=0, tiled=True),
            lax.psum_scatter(grad_values, "table", scatter_dimension=0, tiled=True),
        )
        key_back = key_back.astype(jnp.bfloat16)
        value_back = value_back.astype(jnp.bfloat16)
        grad_query_weight = inner(normed, grad_queries)
        grad_key_weight = inner(normed, key_back)
        grad_value_weight = inner(normed, value_back)
        grad_normed = (
            times_back(grad_queries, query_all)
            + times_back(key_back, key_all)
            + times_back(value_back, value_all)
        )
        grad_gain_first = jnp.sum(grad_normed * unit_one, axis=0)
        grad_shift_first = jnp.sum(grad_normed, axis=0)
        grad_embedded = (
            grad_hidden + norm_backward(grad_normed, unit_one, inv_one, gain_one_f)
        ).astype(jnp.bfloat16)
        grad_embed_bias = jnp.sum(grad_embedded.astype(jnp.float32), axis=0)
        grad_embed_weight = inner(masked, grad_embedded)
        feat_grads.append(
            times_back(grad_embedded, embed_all) * mask_row.astype(jnp.float32)[None, :]
        )
        local_grads = (
            grad_embed_weight,
            grad_embed_bias,
            grad_gain_first,
            grad_shift_first,
            grad_query_weight,
            grad_key_weight,
            grad_value_weight,
            grad_out_weight,
            grad_gain_second,
            grad_shift_second,
            grad_up_weight,
            grad_up_bias,
            grad_down_weight,
            grad_down_bias,
        )
        owned = (
            lax.psum_scatter(local_grads[0], "dp", scatter_dimension=1, tiled=True),
            lax.psum_scatter(local_grads[1], "dp", scatter_dimension=0, tiled=True),
            lax.psum_scatter(local_grads[2], "dp", scatter_dimension=0, tiled=True),
            lax.psum_scatter(local_grads[3], "dp", scatter_dimension=0, tiled=True),
            lax.psum_scatter(local_grads[4], "dp", scatter_dimension=0, tiled=True),
            lax.psum_scatter(local_grads[5], "dp", scatter_dimension=0, tiled=True),
            lax.psum_scatter(local_grads[6], "dp", scatter_dimension=0, tiled=True),
            lax.psum_scatter(local_grads[7], "dp", scatter_dimension=0, tiled=True),
            lax.psum_scatter(local_grads[8], "dp", scatter_dimension=0, tiled=True),
            lax.psum_scatter(local_grads[9], "dp", scatter_dimension=0, tiled=True),
            lax.psum_scatter(local_grads[10], "dp", scatter_dimension=0, tiled=True),
            lax.psum_scatter(local_grads[11], "dp", scatter_dimension=0, tiled=True),
            lax.psum_scatter(local_grads[12], "dp", scatter_dimension=0, tiled=True),
            lax.psum_scatter(local_grads[13], "dp", scatter_dimension=0, tiled=True),
        )
        owned = (
            lax.psum(owned[0].astype(jnp.bfloat16), "table").astype(jnp.float32),
            lax.psum(owned[1].astype(jnp.bfloat16), "table").astype(jnp.float32),
            lax.psum(owned[2].astype(jnp.bfloat16), "table").astype(jnp.float32),
            lax.psum(owned[3].astype(jnp.bfloat16), "table").astype(jnp.float32),
            lax.psum(owned[4].astype(jnp.bfloat16), "table").astype(jnp.float32),
            lax.psum(owned[5].astype(jnp.bfloat16), "table").astype(jnp.float32),
            lax.psum(owned[6].astype(jnp.bfloat16), "table").astype(jnp.float32),
            lax.psum(owned[7].astype(jnp.bfloat16), "table").astype(jnp.float32),
            lax.psum(owned[8].astype(jnp.bfloat16), "table").astype(jnp.float32),
            lax.psum(owned[9].astype(jnp.bfloat16), "table").astype(jnp.float32),
            lax.psum(owned[10].astype(jnp.bfloat16), "table").astype(jnp.float32),
            lax.psum(owned[11].astype(jnp.bfloat16), "table").astype(jnp.float32),
            lax.psum(owned[12].astype(jnp.bfloat16), "table").astype(jnp.float32),
            lax.psum(owned[13].astype(jnp.bfloat16), "table").astype(jnp.float32),
        )
        summed = add_grads(summed, tuple(owned))
    activations = jnp.stack(results)[:, None]
    input_grad = jnp.stack(feat_grads)[:, None]
    return (
        activations,
        input_grad,
        summed[0],
        summed[1],
        summed[2],
        summed[3],
        summed[4],
        summed[5],
        summed[6],
        summed[7],
        summed[8],
        summed[9],
        summed[10],
        summed[11],
        summed[12],
        summed[13],
    )


def solution(mesh):
    return jax.shard_map(
        body,
        mesh=mesh,
        in_specs=(
            P(None, "dp", "table", None),
            P(None, "dp", None),
            P(None, "dp"),
            P(None, "dp"),
            P("dp"),
            P("dp"),
            P("dp"),
            P("dp", None),
            P("dp", None),
            P("dp", None),
            P("dp", None),
            P("dp"),
            P("dp"),
            P("dp", None),
            P("dp"),
            P("dp", None),
            P("dp"),
            P(None, "dp", "table", None),
        ),
        out_specs=(
            P(None, "dp", "table", None),
            P(None, "dp", "table", None),
            P(None, "dp"),
            P("dp"),
            P("dp"),
            P("dp"),
            P("dp", None),
            P("dp", None),
            P("dp", None),
            P("dp", None),
            P("dp"),
            P("dp"),
            P("dp", None),
            P("dp"),
            P("dp", None),
            P("dp"),
        ),
        check_vma=False,
    )
```

profile of v0, /device:TPU:0, one launch (start us, length us, event | category | flops | bytes accessed | tf_op | source)
XLA Modules:
  0.0 1981.7 jit_solution(3506439235125683923)
XLA Ops:
  14.3 16.0 all-reduce.28
  81.8 9.7 all_gather.46
  108.6 10.7 all_gather.49
  136.8 13.9 all-gather.22.cloned.1.call-done
  160.1 37.1 %all-gather.20.cloned.1.call-done = bf16[2048,512]{1,0:T(8,128)(2,1)} async-done(((bf16[512,512]{1,0:T(8,128)(2,1)}), bf16[2048,512]{1,0:T(8,128)(2,1)}) %all-gather.20.cloned.1.call-update) | async-done | bytes 2097168 | tf_op jit(solution)/shard_map/all_gather | solution.py:145
  211.6 32.0 %all-gather.18.cloned.1.call-done = bf16[2048,512]{1,0:T(8,128)(2,1)} async-done(((bf16[512,512]{1,0:T(8,128)(2,1)}), bf16[2048,512]{1,0:T(8,128)(2,1)}) %all-gather.18.cloned.1.call-update) | async-done | bytes 2097168 | tf_op jit(solution)/shard_map/all_gather | solution.py:146
  243.6 20.7 %fusion.84 = bf16[4,128,512]{2,1,0:T(8,128)(2,1)S(1)} fusion(f32[4,512,2048]{2,1,0:T(8,128)} %copy-done.2, f32[4,512]{1,0:T(4,128)S(1)} %log_add_fusion.1, pred[2048]{0:T(1024)(128)(4,1)S(1)} %iota_compare_fusion.1, bf16[2048,512]{1,0:T(8,128)(2,1)} %all-gather.18.cloned.1.call-done), kind=kOutput, calls=%fused_computation.158 | convolution fusion | flops 1090781184 | bytes 19408896 | tf_op jit(solution)/shard_map/hrl,lhd->rhd/dot_general | solution.py:166
  266.6 23.1 %all-gather.12.cloned.1.call-done = bf16[2048,512]{1,0:T(8,128)(2,1)} async-done(((bf16[512,512]{1,0:T(8,128)(2,1)}), bf16[2048,512]{1,0:T(8,128)(2,1)}) %all-gather.12.cloned.1.call-update) | async-done | bytes 2097168 | tf_op jit(solution)/shard_map/all_gather | solution.py:145
  304.6 31.2 %all-gather.10.cloned.1.call-done = bf16[2048,512]{1,0:T(8,128)(2,1)} async-done(((bf16[512,512]{1,0:T(8,128)(2,1)}), bf16[2048,512]{1,0:T(8,128)(2,1)}) %all-gather.10.cloned.1.call-update) | async-done | bytes 2097168 | tf_op jit(solution)/shard_map/all_gather | solution.py:146
  346.1 18.2 all-gather.14.cloned.1.call-done
  369.3 24.8 %all-gather.16.cloned.1.call-done = bf16[2048,512]{1,0:T(8,128)(2,1)} async-done(((bf16[256,512]{1,0:T(8,128)(2,1)}), bf16[2048,512]{1,0:T(8,128)(2,1)}) %all-gather.16.cloned.1.call-update) | async-done | bytes 2097168 | tf_op jit(solution)/shard_map/all_gather | solution.py:57
  416.6 32.6 %fusion.8 = (bf16[512,2048]{1,0:T(8,128)(2,1)}, bf16[512,2048]{1,0:T(8,128)(2,1)}, bf16[512,2048]{1,0:T(8,128)(2,1)}, f32[512,2048]{1,0:T(8,128)S(1)}) fusion(f32[2048]{0:T(1024)S(1)} %bitcast.330, f32[512,2048]{1,0:T(8,128)} %copy-done.72, f32[512,2048]{1,0:T(8,128)} %fusion.173, bf16[512,2048]{1,0:T(8,128)(2,1)} %all-gather.14.cloned.1.call-done, ...), kind=kOutput, calls=%fused_computation.29 | convolution fusion | flops 1282670592 | bytes 22036480 | tf_op jit(solution)/shard_map/dot_general | solution.py:179
  462.5 10.1 fusion.132
  479.8 10.1 fusion.138
  497.1 10.2 fusion.135
  507.4 12.9 multiply_reduce_fusion.1
  520.3 12.2 multiply_convert_fusion.1
  537.0 13.4 multiply_reduce_fusion.2
  550.4 12.8 multiply_convert_fusion.2
  567.8 12.9 multiply_reduce_fusion
  580.7 12.2 multiply_convert_fusion
  671.6 37.1 %reduce-scatter.34.cloned.1.call-done = f32[512,512]{0,1:T(8,128)} async-done(((f32[2048,512]{0,1:T(8,128)}), f32[512,512]{0,1:T(8,128)}) %reduce-scatter.34.cloned.1.call-update) | async-done | bytes 1048592 | tf_op jit(solution)/shard_map/reduce_scatter | solution.py:273
  711.6 76.6 %reduce-scatter.32.cloned.1.call-done = f32[512,512]{0,1:T(8,128)} async-done(((f32[2048,512]{0,1:T(8,128)}), f32[512,512]{0,1:T(8,128)}) %reduce-scatter.32.cloned.1.call-update) | async-done | bytes 1048592 | tf_op jit(solution)/shard_map/reduce_scatter | solution.py:272
  796.5 71.4 %reduce-scatter.28.cloned.1.call-done = f32[512,512]{0,1:T(8,128)} async-done(((f32[2048,512]{0,1:T(8,128)}), f32[512,512]{0,1:T(8,128)}) %reduce-scatter.28.cloned.1.call-update) | async-done | bytes 1048592 | tf_op jit(solution)/shard_map/reduce_scatter | solution.py:272
  877.4 70.0 %reduce-scatter.36.cloned.1.call-done = f32[512,512]{0,1:T(8,128)} async-done(((f32[2048,512]{0,1:T(8,128)}), f32[512,512]{0,1:T(8,128)}) %reduce-scatter.36.cloned.1.call-update) | async-done | bytes 1048592 | tf_op jit(solution)/shard_map/reduce_scatter | solution.py:272
  988.6 37.5 %reduce-scatter.64.cloned.1.call-done = f32[64,512]{1,0:T(8,128)} async-done(((f32[512,512]{1,0:T(8,128)}), f32[64,512]{1,0:T(8,128)}) %reduce-scatter.64.cloned.1.call-update) | async-done | bytes 131088 | tf_op jit(solution)/shard_map/reduce_scatter | solution.py:319
  1027.6 37.5 %reduce-scatter.68.cloned.1.call-done = f32[64,512]{1,0:T(8,128)} async-done(((f32[512,512]{1,0:T(8,128)}), f32[64,512]{1,0:T(8,128)}) %reduce-scatter.68.cloned.1.call-update) | async-done | bytes 131088 | tf_op jit(solution)/shard_map/reduce_scatter | solution.py:319
  1066.7 37.5 %reduce-scatter.48.cloned.1.call-done = f32[64,512]{1,0:T(8,128)} async-done(((f32[512,512]{1,0:T(8,128)}), f32[64,512]{1,0:T(8,128)}) %reduce-scatter.48.cloned.1.call-update) | async-done | bytes 131088 | tf_op jit(solution)/shard_map/reduce_scatter | solution.py:316
  1105.8 37.7 %reduce-scatter.46.cloned.1.call-done = f32[64,512]{1,0:T(8,128)} async-done(((f32[512,512]{1,0:T(8,128)}), f32[64,512]{1,0:T(8,128)}) %reduce-scatter.46.cloned.1.call-update) | async-done | bytes 131088 | tf_op jit(solution)/shard_map/reduce_scatter | solution.py:316
  1145.0 37.5 %reduce-scatter.50.cloned.1.call-done = f32[64,512]{1,0:T(8,128)} async-done(((f32[512,512]{1,0:T(8,128)}), f32[64,512]{1,0:T(8,128)}) %reduce-scatter.50.cloned.1.call-update) | async-done | bytes 131088 | tf_op jit(solution)/shard_map/reduce_scatter | solution.py:316
  1184.0 53.1 %reduce-scatter.74.cloned.1.call-done = f32[64,2048]{1,0:T(8,128)} async-done(((f32[512,2048]{1,0:T(8,128)}), f32[64,2048]{1,0:T(8,128)}) %reduce-scatter.74.cloned.1.call-update) | async-done | bytes 524304 | tf_op jit(solution)/shard_map/reduce_scatter | solution.py:322
  1239.0 53.3 %reduce-scatter.72.cloned.1.call-done = f32[64,2048]{1,0:T(8,128)} async-done(((f32[512,2048]{1,0:T(8,128)}), f32[64,2048]{1,0:T(8,128)}) %reduce-scatter.72.cloned.1.call-update) | async-done | bytes 524304 | tf_op jit(solution)/shard_map/reduce_scatter | solution.py:322
  1294.0 52.9 %reduce-scatter.70.cloned.1.call-done = f32[64,2048]{1,0:T(8,128)} async-done(((f32[512,2048]{1,0:T(8,128)}), f32[64,2048]{1,0:T(8,128)}) %reduce-scatter.70.cloned.1.call-update) | async-done | bytes 524304 | tf_op jit(solution)/shard_map/reduce_scatter | solution.py:322
  1348.8 53.2 %reduce-scatter.80.cloned.1.call-done = f32[256,512]{1,0:T(8,128)} async-done(((f32[2048,512]{1,0:T(8,128)}), f32[256,512]{1,0:T(8,128)}) %reduce-scatter.80.cloned.1.call-update) | async-done | bytes 524304 | tf_op jit(solution)/shard_map/reduce_scatter | solution.py:324
  1403.7 52.9 %reduce-scatter.78.cloned.1.call-done = f32[256,512]{1,0:T(8,128)} async-done(((f32[2048,512]{1,0:T(8,128)}), f32[256,512]{1,0:T(8,128)}) %reduce-scatter.78.cloned.1.call-update) | async-done | bytes 524304 | tf_op jit(solution)/shard_map/reduce_scatter | solution.py:324
  1458.4 53.2 %reduce-scatter.76.cloned.1.call-done = f32[256,512]{1,0:T(8,128)} async-done(((f32[2048,512]{1,0:T(8,128)}), f32[256,512]{1,0:T(8,128)}) %reduce-scatter.76.cloned.1.call-update) | async-done | bytes 524304 | tf_op jit(solution)/shard_map/reduce_scatter | solution.py:324
  1513.5 23.9 %all-reduce.27 = (bf16[512]{0:T(512)(128)(2,1)S(1)}, bf16[512]{0:T(512)(128)(2,1)S(1)}, bf16[512]{0:T(512)(128)(2,1)S(1)}, bf16[512]{0:T(512)(128)(2,1)S(1)}, bf...) all-reduce(f32[512]{0:T(512)S(1)} %get-tuple-element.173, ...), channel_id=13, replica_groups=mesh['dp'=8,'table'=4] {'dp'}, use_global_device_ids=true, to_apply=%region_52.53.clone | all-reduce | flops 15360 | bytes 92160
  1538.9 11.7 reduce-scatter.62.cloned.1.call-done
  1552.2 37.7 %reduce-scatter.58.cloned.1.call-done = f32[64,512]{1,0:T(8,128)} async-done(((f32[512,512]{1,0:T(8,128)}), f32[64,512]{1,0:T(8,128)}) %reduce-scatter.58.cloned.1.call-update) | async-done | bytes 131088 | tf_op jit(solution)/shard_map/reduce_scatter | solution.py:318
  1591.4 37.7 %reduce-scatter.60.cloned.1.call-done = f32[64,512]{1,0:T(8,128)} async-done(((f32[512,512]{1,0:T(8,128)}), f32[64,512]{1,0:T(8,128)}) %reduce-scatter.60.cloned.1.call-update) | async-done | bytes 131088 | tf_op jit(solution)/shard_map/reduce_scatter | solution.py:318
  1630.7 37.5 %reduce-scatter.54.cloned.1.call-done = f32[64,512]{1,0:T(8,128)} async-done(((f32[512,512]{1,0:T(8,128)}), f32[64,512]{1,0:T(8,128)}) %reduce-scatter.54.cloned.1.call-update) | async-done | bytes 131088 | tf_op jit(solution)/shard_map/reduce_scatter | solution.py:317
  1669.7 37.6 %reduce-scatter.52.cloned.1.call-done = f32[64,512]{1,0:T(8,128)} async-done(((f32[512,512]{1,0:T(8,128)}), f32[64,512]{1,0:T(8,128)}) %reduce-scatter.52.cloned.1.call-update) | async-done | bytes 131088 | tf_op jit(solution)/shard_map/reduce_scatter | solution.py:317
  1708.9 37.7 %reduce-scatter.56.cloned.1.call-done = f32[64,512]{1,0:T(8,128)} async-done(((f32[512,512]{1,0:T(8,128)}), f32[64,512]{1,0:T(8,128)}) %reduce-scatter.56.cloned.1.call-update) | async-done | bytes 131088 | tf_op jit(solution)/shard_map/reduce_scatter | solution.py:317
  1750.5 32.6 %reduce-scatter.42.cloned.1.call-done = f32[100,64]{0,1:T(8,128)} async-done(((f32[100,512]{0,1:T(8,128)}), f32[100,64]{0,1:T(8,128)}) %reduce-scatter.42.cloned.1.call-update) | async-done | bytes 25616 | tf_op jit(solution)/shard_map/reduce_scatter | solution.py:312
  1783.9 36.2 %reduce-scatter.44.cloned.1.call-done = f32[100,64]{0,1:T(8,128)} async-done(((f32[100,512]{0,1:T(8,128)}), f32[100,64]{0,1:T(8,128)}) %reduce-scatter.44.cloned.1.call-update) | async-done | bytes 25616 | tf_op jit(solution)/shard_map/reduce_scatter | solution.py:312
  1820.8 35.9 %reduce-scatter.40.cloned.1.call-done = f32[100,64]{0,1:T(8,128)} async-done(((f32[100,512]{0,1:T(8,128)}), f32[100,64]{0,1:T(8,128)}) %reduce-scatter.40.cloned.1.call-update) | async-done | bytes 25616 | tf_op jit(solution)/shard_map/reduce_scatter | solution.py:312
  1857.5 20.9 %all-reduce.29 = (bf16[100,64]{0,1:T(8,128)(2,1)S(1)}, bf16[100,64]{0,1:T(8,128)(2,1)S(1)}, bf16[100,64]{0,1:T(8,128)(2,1)S(1)}, bf16[64]{0:T(256)(128)(2,1)S(1)...) all-reduce(bf16[100,64]{0,1:T(8,128)(2,1)S(1)} %convert_element_typ, ...), channel_id=1, replica_groups=mesh['dp'=8,'table'=4] {'table'}, use_global_device_ids=true, to_apply=%region_44.45 | all-reduce | flops 21120 | bytes 84480 | tf_op jit(solution)/shard_map/psum | solution.py:328
  1882.6 81.8 %all-reduce.33.cloned.1.call-done = (bf16[64,512]{1,0:T(8,128)(2,1)}, bf16[64,512]{1,0:T(8,128)(2,1)}, bf16[64,512]{1,0:T(8,128)(2,1)}, bf16[64,512]{1,0:T(8,128...) async-done(((bf16[64,512]{1,0:T(8,128)(2,1)}, ...) | async-done | bytes 2359312 | tf_op jit(solution)/shard_map/psum | solution.py:332
  (574 shorter events, 393.8 us)
Async XLA Ops:
  7.2 115.4 %all-gather.24.cloned.1.call-start = ((), (), s32[]{:S(2)}) async-start(), calls=%async_computation.34 | async-start | bytes 2621440 | tf_op jit(solution)/shard_map/all_gather | solution.py:145
  58.1 92.7 %all-gather.22.cloned.1.call-start = ((), (), s32[]{:S(2)}) async-start(), calls=%async_computation.33 | async-start | bytes 2621440 | tf_op jit(solution)/shard_map/all_gather | solution.py:146
  70.6 126.6 %all-gather.20.cloned.1.call-start = ((), (), s32[]{:S(2)}) async-start(), calls=%async_computation.32 | async-start | bytes 2621440 | tf_op jit(solution)/shard_map/all_gather | solution.py:145
  73.0 170.6 %all-gather.18.cloned.1.call-start = ((), (), s32[]{:S(2)}) async-start(), calls=%async_computation.31 | async-start | bytes 2621440 | tf_op jit(solution)/shard_map/all_gather | solution.py:146
  75.4 214.3 %all-gather.12.cloned.1.call-start = ((), (), s32[]{:S(2)}) async-start(), calls=%async_computation.28 | async-start | bytes 2621440 | tf_op jit(solution)/shard_map/all_gather | solution.py:145
  77.9 257.9 %all-gather.10.cloned.1.call-start = ((), (), s32[]{:S(2)}) async-start(), calls=%async_computation.27 | async-start | bytes 2621440 | tf_op jit(solution)/shard_map/all_gather | solution.py:146
  80.3 284.0 %all-gather.14.cloned.1.call-start = ((), (), s32[]{:S(2)}) async-start(), calls=%async_computation.29 | async-start | bytes 2359296 | tf_op jit(solution)/shard_map/all_gather | solution.py:55
  81.0 313.1 %all-gather.16.cloned.1.call-start = ((), (), s32[]{:S(2)}) async-start(), calls=%async_computation.30 | async-start | bytes 2359296 | tf_op jit(solution)/shard_map/all_gather | solution.py:57
  81.8 583.3 %reduce-scatter.38.cloned.1.call-start = ((), (), s32[]{:S(2)}) async-start(), calls=%async_computation.40 | async-start | bytes 5242880 | tf_op jit(solution)/shard_map/reduce_scatter | solution.py:273
  472.7 196.2 %reduce-scatter.30.cloned.1.call-start = ((), (), s32[]{:S(2)}) async-start(), calls=%async_computation.36 | async-start | bytes 5242880 | tf_op jit(solution)/shard_map/reduce_scatter | solution.py:273
  490.0 218.7 %reduce-scatter.34.cloned.1.call-start = ((), (), s32[]{:S(2)}) async-start(), calls=%async_computation.38 | async-start | bytes 5242880 | tf_op jit(solution)/shard_map/reduce_scatter | solution.py:273
  507.3 281.0 %reduce-scatter.32.cloned.1.call-start = ((), (), s32[]{:S(2)}) async-start(), calls=%async_computation.37 | async-start | bytes 5242880 | tf_op jit(solution)/shard_map/reduce_scatter | solution.py:272
  537.0 330.9 %reduce-scatter.28.cloned.1.call-start = ((), (), s32[]{:S(2)}) async-start(), calls=%async_computation.35 | async-start | bytes 5242880 | tf_op jit(solution)/shard_map/reduce_scatter | solution.py:272
  567.8 379.7 %reduce-scatter.36.cloned.1.call-start = ((), (), s32[]{:S(2)}) async-start(), calls=%async_computation.39 | async-start | bytes 5242880 | tf_op jit(solution)/shard_map/reduce_scatter | solution.py:272
  597.5 389.6 %reduce-scatter.66.cloned.1.call-start = ((), (), s32[]{:S(2)}) async-start(), calls=%async_computation.54 | async-start | bytes 1179648 | tf_op jit(solution)/shard_map/reduce_scatter | solution.py:319
  600.5 425.6 %reduce-scatter.64.cloned.1.call-start = ((), (), s32[]{:S(2)}) async-start(), calls=%async_computation.53 | async-start | bytes 1179648 | tf_op jit(solution)/shard_map/reduce_scatter | solution.py:319
  603.4 461.7 %reduce-scatter.68.cloned.1.call-start = ((), (), s32[]{:S(2)}) async-start(), calls=%async_computation.55 | async-start | bytes 1179648 | tf_op jit(solution)/shard_map/reduce_scatter | solution.py:319
  606.6 497.6 %reduce-scatter.48.cloned.1.call-start = ((), (), s32[]{:S(2)}) async-start(), calls=%async_computation.45 | async-start | bytes 1179648 | tf_op jit(solution)/shard_map/reduce_scatter | solution.py:316
  615.9 527.5 %reduce-scatter.46.cloned.1.call-start = ((), (), s32[]{:S(2)}) async-start(), calls=%async_computation.44 | async-start | bytes 1179648 | tf_op jit(solution)/shard_map/reduce_scatter | solution.py:316
  625.4 557.1 %reduce-scatter.50.cloned.1.call-start = ((), (), s32[]{:S(2)}) async-start(), calls=%async_computation.46 | async-start | bytes 1179648 | tf_op jit(solution)/shard_map/reduce_scatter | solution.py:316
  634.8 602.4 %reduce-scatter.74.cloned.1.call-start = ((), (), s32[]{:S(2)}) async-start(), calls=%async_computation.58 | async-start | bytes 4718592 | tf_op jit(solution)/shard_map/reduce_scatter | solution.py:322
  639.8 652.5 %reduce-scatter.72.cloned.1.call-start = ((), (), s32[]{:S(2)}) async-start(), calls=%async_computation.57 | async-start | bytes 4718592 | tf_op jit(solution)/shard_map/reduce_scatter | solution.py:322
  644.8 702.2 %reduce-scatter.70.cloned.1.call-start = ((), (), s32[]{:S(2)}) async-start(), calls=%async_computation.56 | async-start | bytes 4718592 | tf_op jit(solution)/shard_map/reduce_scatter | solution.py:322
  649.7 752.2 %reduce-scatter.80.cloned.1.call-start = ((), (), s32[]{:S(2)}) async-start(), calls=%async_computation.61 | async-start | bytes 4718592 | tf_op jit(solution)/shard_map/reduce_scatter | solution.py:324
  654.8 801.9 %reduce-scatter.78.cloned.1.call-start = ((), (), s32[]{:S(2)}) async-start(), calls=%async_computation.60 | async-start | bytes 4718592 | tf_op jit(solution)/shard_map/reduce_scatter | solution.py:324
  660.0 851.6 %reduce-scatter.76.cloned.1.call-start = ((), (), s32[]{:S(2)}) async-start(), calls=%async_computation.59 | async-start | bytes 4718592 | tf_op jit(solution)/shard_map/reduce_scatter | solution.py:324
  665.0 885.7 %reduce-scatter.62.cloned.1.call-start = ((), (), s32[]{:S(2)}) async-start(), calls=%async_computation.52 | async-start | bytes 1179648 | tf_op jit(solution)/shard_map/reduce_scatter | solution.py:318
  668.8 921.1 %reduce-scatter.58.cloned.1.call-start = ((), (), s32[]{:S(2)}) async-start(), calls=%async_computation.50 | async-start | bytes 1179648 | tf_op jit(solution)/shard_map/reduce_scatter | solution.py:318
  671.6 957.6 %reduce-scatter.60.cloned.1.call-start = ((), (), s32[]{:S(2)}) async-start(), calls=%async_computation.51 | async-start | bytes 1179648 | tf_op jit(solution)/shard_map/reduce_scatter | solution.py:318
  711.6 956.6 %reduce-scatter.54.cloned.1.call-start = ((), (), s32[]{:S(2)}) async-start(), calls=%async_computation.48 | async-start | bytes 1179648 | tf_op jit(solution)/shard_map/reduce_scatter | solution.py:317
  791.2 916.2 %reduce-scatter.52.cloned.1.call-start = ((), (), s32[]{:S(2)}) async-start(), calls=%async_computation.47 | async-start | bytes 1179648 | tf_op jit(solution)/shard_map/reduce_scatter | solution.py:317
  870.7 875.9 %reduce-scatter.56.cloned.1.call-start = ((), (), s32[]{:S(2)}) async-start(), calls=%async_computation.49 | async-start | bytes 1179648 | tf_op jit(solution)/shard_map/reduce_scatter | solution.py:317
  950.3 832.8 %reduce-scatter.42.cloned.1.call-start = ((), (), s32[]{:S(2)}) async-start(), calls=%async_computation.42 | async-start | bytes 294912 | tf_op jit(solution)/shard_map/reduce_scatter | solution.py:312
  961.2 858.9 %reduce-scatter.44.cloned.1.call-start = ((), (), s32[]{:S(2)}) async-start(), calls=%async_computation.43 | async-start | bytes 294912 | tf_op jit(solution)/shard_map/reduce_scatter | solution.py:312
  966.8 889.9 %reduce-scatter.40.cloned.1.call-start = ((), (), s32[]{:S(2)}) async-start(), calls=%async_computation.41 | async-start | bytes 294912 | tf_op jit(solution)/shard_map/reduce_scatter | solution.py:312
  972.6 991.8 %all-reduce.33.cloned.1.call-start = ((), (), s32[]{:S(2)}) async-start(), calls=%async_computation.62 | async-start | bytes 4718592 | tf_op jit(solution)/shard_map/psum | solution.py:332
  976.4 536.9 %copy-start.116 = (f32[512]{0:T(512)S(1)}, f32[512]{0:T(512)}, u32[]{:S(2)}) copy-start(f32[512]{0:T(512)} %get-tuple-element.147) | copy-start | bytes 6148
  976.4 536.9 %copy-start.117 = (f32[512]{0:T(512)S(1)}, f32[512]{0:T(512)}, u32[]{:S(2)}) copy-start(f32[512]{0:T(512)} %get-tuple-element.149) | copy-start | bytes 6148
  976.4 536.9 %copy-start.118 = (f32[2048]{0:T(1024)S(1)}, f32[2048]{0:T(1024)}, u32[]{:S(2)}) copy-start(f32[2048]{0:T(1024)} %get-tuple-element.219) | copy-start | bytes 24580
  976.5 536.9 %copy-start.119 = (f32[2048]{0:T(1024)S(1)}, f32[2048]{0:T(1024)}, u32[]{:S(2)}) copy-start(f32[2048]{0:T(1024)} %get-tuple-element.221) | copy-start | bytes 24580
  976.5 536.9 %copy-start.120 = (f32[2048]{0:T(1024)S(1)}, f32[2048]{0:T(1024)}, u32[]{:S(2)}) copy-start(f32[2048]{0:T(1024)} %get-tuple-element.223) | copy-start | bytes 24580
  976.5 536.9 %copy-start.121 = (f32[512]{0:T(512)S(1)}, f32[512]{0:T(512)}, u32[]{:S(2)}) copy-start(f32[512]{0:T(512)} %get-tuple-element.52) | copy-start | bytes 6148
  976.5 536.9 %copy-start.122 = (f32[512]{0:T(512)S(1)}, f32[512]{0:T(512)}, u32[]{:S(2)}) copy-start(f32[512]{0:T(512)} %get-tuple-element.151) | copy-start | bytes 6148
  976.5 536.9 %copy-start.123 = (f32[512]{0:T(512)S(1)}, f32[512]{0:T(512)}, u32[]{:S(2)}) copy-start(f32[512]{0:T(512)} %get-tuple-element.161) | copy-start | bytes 6148
  976.5 536.9 %copy-start.124 = (f32[512]{0:T(512)S(1)}, f32[512]{0:T(512)}, u32[]{:S(2)}) copy-start(f32[512]{0:T(512)} %get-tuple-element.164) | copy-start | bytes 6148
  1184.0 564.1 %copy-start.52 = (bf16[100,512]{0,1:T(8,128)(2,1)S(1)}, bf16[100,512]{0,1:T(8,128)(2,1)}, u32[]{:S(2)}) copy-start(bf16[100,512]{0,1:T(8,128)(2,1)} %copy-done.51) | copy-start | bytes 307204
  1184.0 564.2 %copy-start.65 = (bf16[512,512]{0,1:T(8,128)(2,1)S(1)}, bf16[512,512]{0,1:T(8,128)(2,1)}, u32[]{:S(2)}) copy-start(bf16[512,512]{0,1:T(8,128)(2,1)} %copy-done.64) | copy-start | bytes 1572868
  1184.0 564.2 %copy-start.134 = (f32[100]{0:T(128)S(1)}, f32[100]{0:T(128)}, u32[]{:S(2)}) copy-start(f32[100]{0:T(128)} %get-tuple-element.176) | copy-start | bytes 1204
  (130 other events, 6299.3 us)
Sparse Core Ops, SparseCore 0:
  58.2 46.2 all-gather.23
  106.1 44.6 all-gather.21
  152.3 44.8 all-gather.19
  198.7 44.8 all-gather.17
  245.0 44.6 all-gather.11
  291.1 44.6 all-gather.9
  337.7 26.5 all-gather.13
  366.1 27.8 all-gather.15
  472.8 76.7 reduce-scatter.37
  551.8 77.2 reduce-scatter.29
  631.4 77.2 reduce-scatter.33
  711.0 77.2 reduce-scatter.31
  790.6 77.2 reduce-scatter.27
  870.1 77.2 reduce-scatter.35
  950.5 36.5 reduce-scatter.65
  990.1 35.9 reduce-scatter.63
  1029.1 35.9 reduce-scatter.67
  1068.2 35.9 reduce-scatter.47
  1107.4 35.9 reduce-scatter.45
  1146.5 35.9 reduce-scatter.49
  1185.9 51.2 reduce-scatter.73
  1240.9 51.3 reduce-scatter.71
  1295.6 51.3 reduce-scatter.69
  1350.6 51.3 reduce-scatter.79
  1405.3 51.3 reduce-scatter.77
  1460.2 51.3 reduce-scatter.75
  1514.6 36.0 reduce-scatter.61
  1553.8 36.0 reduce-scatter.57
  1593.1 36.0 reduce-scatter.59
  1632.2 35.9 reduce-scatter.53
  1671.4 35.9 reduce-scatter.51
  1710.6 35.9 reduce-scatter.55
  1749.5 33.6 reduce-scatter.41
  1786.4 33.5 reduce-scatter.43
  1823.1 33.5 reduce-scatter.39
  1862.0 102.3 all-reduce.32
where the time goes:
time: 1990 us; the launch traced here: 1980 us
  waiting for transfers between devices  1340 us (67%)
  matrix products  336 us (17%)
  blocking collectives  117 us (6%)
  other arithmetic  112 us (6%)
  local copies, waits for them, and re-layouts  57.2 us (3%)
    reduce_scatter x3, waiting for transfers between devices, body(): lax.psum_scatter(grad_keys, 'table', scatter_dimension=0, tiled=True)  218 us
    reduce_scatter x3, waiting for transfers between devices, body(): lax.psum_scatter(local_grads[10], 'dp', scatter_dimension=0, tiled=True)  159 us
    reduce_scatter x3, waiting for transfers between devices, body(): lax.psum_scatter(local_grads[12], 'dp', scatter_dimension=0, tiled=True)  159 us
    reduce_scatter x3, waiting for transfers between devices, body(): lax.psum_scatter(local_grads[5], 'dp', scatter_dimension=0, tiled=True)  113 us
    reduce_scatter x3, waiting for transfers between devices, body(): lax.psum_scatter(local_grads[4], 'dp', scatter_dimension=0, tiled=True)  113 us
    reduce_scatter x3, waiting for transfers between devices, body(): lax.psum_scatter(local_grads[0], 'dp', scatter_dimension=1, tiled=True)  105 us
    reduce_scatter x3, waiting for transfers between devices, body(): lax.psum_scatter(local_grads[6], 'dp', scatter_dimension=0, tiled=True)  87.1 us
    reduce_scatter x3, waiting for transfers between devices, body(): lax.psum_scatter(local_grads[7], 'dp', scatter_dimension=0, tiled=True)  84 us
  transfers between devices with their start and end apart: 36, of which 33 were waited for; matrix products, arithmetic and copies ran while one was open for 19% of the time, Pallas kernels for 0%

commit v1 on v0

v1 whole, which is shorter than its diff:
```python
import functools

import jax
import jax.numpy as jnp
from jax import lax
from jax.experimental import pallas as pl
from jax.experimental.pallas import tpu as pltpu
from jax.sharding import PartitionSpec as P

HEADS = 4
HEAD_DIM = 128
LANES = 128
EPSILON = 1e-5
SCALE = HEAD_DIM**-0.5
LOG2E = 1.4426950408889634
ROW_BLOCK = 256
KEY_BLOCK = 512
INV_SQRT_TWO = 0.7071067811865476
INV_SQRT_TWO_PI = 0.3989422804014327
BF16 = jnp.bfloat16
F32 = jnp.float32
MESH = pl.DeviceIdType.MESH


def dot_nn(a, b):
    return lax.dot_general(a, b, (((1,), (0,)), ((), ())), preferred_element_type=F32)


def dot_nt(a, b):
    return lax.dot_general(a, b, (((1,), (1,)), ((), ())), preferred_element_type=F32)


def dot_tn(a, b):
    return lax.dot_general(a, b, (((0,), (0,)), ((), ())), preferred_element_type=F32)


def norm_parts(v):
    mean = jnp.mean(v, axis=-1, keepdims=True)
    centred = v - mean
    inv = lax.rsqrt(jnp.mean(centred * centred, axis=-1, keepdims=True) + EPSILON)
    return centred * inv, inv


def norm_back(grad, unit, inv, gain):
    q = grad * gain
    return inv * (
        q
        - jnp.mean(q, axis=-1, keepdims=True)
        - unit * jnp.mean(q * unit, axis=-1, keepdims=True)
    )


def row_sum(v):
    return jnp.sum(v, axis=0, keepdims=True)


def const_spec(shape):
    return pl.BlockSpec(shape, lambda *g: (0,) * len(shape))


def micro_spec(shape):
    return pl.BlockSpec((1,) + shape, lambda m, *g: (m,) + (0,) * len(shape))


def head_spec(shape):
    return pl.BlockSpec((1, 1) + shape, lambda m, h: (m, h) + (0,) * len(shape))


def head_cols_spec(rows):
    return pl.BlockSpec((1, rows, HEAD_DIM), lambda m, h: (m, 0, h))


def vmem(mib, **extra):
    return pltpu.CompilerParams(vmem_limit_bytes=mib * 2**20, **extra)


def toggled(index, hop):
    return index + hop * (1 - 2 * ((index // hop) % 2))


def toggled_by(index, hops):
    for hop in hops:
        index = toggled(index, hop)
    return index


def subsets(hops):
    out = [()]
    for hop in hops:
        out = out + [s + (hop,) for s in out]
    return out


def hops_of(size):
    return [1 << i for i in range(size.bit_length() - 1)]


class Place:
    def __init__(self, dp_size, table_size):
        self.size = {"dp": dp_size, "table": table_size}
        self.hops = {axis: hops_of(n) for axis, n in self.size.items()}
        self.me = {"dp": lax.axis_index("dp"), "table": lax.axis_index("table")}

    def partner(self, axis, hop):
        there = dict(self.me)
        there[axis] = toggled(there[axis], hop)
        return (there["dp"], there["table"])

    def signal_all(self, barrier):
        for axis in ("dp", "table"):
            for hop in self.hops[axis]:
                pl.semaphore_signal(
                    barrier, inc=1, device_id=self.partner(axis, hop), device_id_type=MESH
                )

    def wait_all(self, barrier):
        pl.semaphore_wait(barrier, len(self.hops["dp"]) + len(self.hops["table"]))


def remote(place, axis, hop, src, dst, sems, index):
    return pltpu.make_async_remote_copy(
        src_ref=src, dst_ref=dst, send_sem=sems[0].at[index], recv_sem=sems[1].at[index],
        device_id=place.partner(axis, hop), device_id_type=MESH,
    )


class Gather:
    def __init__(self, place, axis, hops, full, sems, base, own=None):
        self.place, self.axis, self.hops = place, axis, hops
        self.full, self.sems, self.base, self.own = full, sems, base, own
        self.steps = len(hops)

    def whole(self, step):
        part = self.full.at[pl.ds(0, 1 << step)]
        return remote(self.place, self.axis, self.hops[step], part, part, self.sems, self.base + step)

    def start(self, step):
        for s in subsets(self.hops[:step]):
            block = self.full.at[toggled_by(self.place.me[self.axis], s)]
            src = block if s or self.own is None else self.own
            remote(
                self.place, self.axis, self.hops[step], src, block, self.sems, self.base + step
            ).start()

    def arrive(self, step):
        self.whole(step).wait_recv()

    def sent(self):
        for step in range(self.steps):
            self.whole(step).wait_send()


def add_into(into, other):
    lead = into.shape[:-2]
    rows, cols = into.shape[-2:]
    if lead:
        for i in range(lead[0]):
            add_into(into.at[i], other.at[i])
        return
    piece = min(rows, max(16, 65536 // cols))
    piece = rows if rows % piece else piece

    def body(i, carry):
        at = pl.ds(pl.multiple_of(i * piece, piece), piece)
        into[at, :] = (into[at, :].astype(F32) + other[at, :].astype(F32)).astype(into.dtype)
        return carry

    if rows == piece:
        into[...] = (into[...].astype(F32) + other[...].astype(F32)).astype(into.dtype)
    else:
        lax.fori_loop(0, rows // piece, body, 0)


class Reduce:
    def __init__(self, place, axis, hops, blocks, bufs, sems, base, near=None):
        self.place, self.axis, self.hops = place, axis, hops
        self.held, self.near = blocks, near
        self.bufs, self.sems, self.base = bufs, sems, base
        self.steps = len(hops)

    def mine(self, step, s):
        if step == 0:
            return self.held(s)
        order = [set(t) for t in subsets(self.hops[step:])]
        return self.bufs[step - 1].at[order.index(set(s))]

    def copy(self, step, src, dst):
        return remote(self.place, self.axis, self.hops[step], src, dst, self.sems, self.base + step)

    def start(self, step):
        for i, s in enumerate(subsets(self.hops[step + 1 :])):
            self.copy(step, self.mine(step, s + (self.hops[step],)), self.bufs[step].at[i]).start()

    def arrive(self, step):
        self.copy(step, self.bufs[step], self.bufs[step]).wait_recv()
        for i, s in enumerate(subsets(self.hops[step + 1 :])):
            near = step == 0 and self.near is not None
            add_into(self.bufs[step].at[i], self.near.at[i] if near else self.mine(step, s))

    def total(self):
        return self.bufs[-1].at[0]

    def sent(self):
        for step in range(self.steps):
            self.copy(step, self.bufs[step], self.bufs[step]).wait_send()


class Shard:
    def __init__(self, place, dp_hops, grad, scratch, sems, base, near=None):
        n, m = len(dp_hops), len(place.hops["table"])
        dp_bufs, table_bufs, full = scratch[:n], scratch[n : n + m], scratch[n + m]
        self.place, self.grad, self.near = place, grad, near

        def blocks(s):
            return grad.at[toggled_by(place.me["dp"], s)]

        self.dp = Reduce(place, "dp", dp_hops, blocks, dp_bufs, sems, base, near)
        table_hops = place.hops["table"]
        base += self.dp.steps

        def parts(s):
            return self.dp.total().at[toggled_by(place.me["table"], s)]

        self.table = Reduce(place, "table", table_hops, parts, table_bufs, sems, base)
        base += self.table.steps
        self.full = full
        self.back = Gather(place, "table", table_hops[::-1], full, sems, base)
        self.flows = [(f, i) for f in (self.dp, self.table, self.back) for i in range(f.steps)]
        self.steps = len(self.flows)

    def near_copies(self, sem):
        halves = subsets(self.dp.hops[1:])
        return [
            pltpu.make_async_copy(self.dp.held(s), self.near.at[i], sem) for i, s in enumerate(halves)
        ]

    def near_wait(self, sem):
        pltpu.make_async_copy(self.near, self.near, sem).wait()

    def start(self, step):
        flow, i = self.flows[step]
        if flow is self.back and i == 0:
            self.full[self.place.me["table"]] = self.table.total()[...]
        flow.start(i)

    def arrive(self, step):
        flow, i = self.flows[step]
        flow.arrive(i)

    def sent(self):
        for flow in (self.dp, self.table, self.back):
            flow.sent()


class Total:
    def __init__(self, place, hops, sums, got, sems, base):
        self.place, self.hops, self.sums, self.got = place, hops, sums, got
        self.sems, self.base, self.steps = sems, base, len(hops)

    def copy(self, step):
        axis, hop = self.hops[step]
        return remote(
            self.place, axis, hop, self.sums.at[step], self.got.at[step], self.sems, self.base + step
        )

    def start(self, step):
        self.copy(step).start()

    def arrive(self, step):
        self.copy(step).wait_recv()
        self.sums[step + 1] = self.sums[step] + self.got[step]

    def sent(self):
        for step in range(self.steps):
            self.copy(step).wait_send()


def shard_scratch(dp_size, table_size, block, dtype):
    out = [pltpu.VMEM((dp_size >> (i + 1),) + block, dtype) for i in range(len(hops_of(dp_size)))]
    out += [
        pltpu.VMEM((table_size >> (i + 1),) + block[1:], dtype) for i in range(len(hops_of(table_size)))
    ]
    out.append(pltpu.VMEM(block, dtype))
    return out


def attend_core(
    support, get_x, own_x, wet_ref, vec_ref, wq, wk, wv,
    q_ref, k_ref, v_ref, n_ref, u_ref, inv_ref, emb_ref, mixed_ref, p_ref, linv_ref,
):
    length, rows = n_ref.shape[1], q_ref.shape[1]
    own = lax.axis_index("table") * rows
    bias, gain, shift = vec_ref[0:1, :], vec_ref[1:2, :], vec_ref[2:3, :]
    chunk = 256

    @pl.when(pl.program_id(1) == 0)
    def _():
        def project(i, carry):
            at = pl.ds(pl.multiple_of(i * chunk, chunk), chunk)
            embedded = dot_nt(get_x(i, chunk), wet_ref[...]) + bias
            unit, inv = norm_parts(embedded)
            normed = (unit * gain + shift).astype(BF16)
            n_ref[0, at, :] = normed
            u_ref[0, at, :] = unit.astype(BF16)
            inv_ref[0, at, :] = jnp.broadcast_to(inv, (chunk, LANES))
            k_ref[0, at, :] = dot_nn(normed, wk()).astype(BF16)
            v_ref[0, at, :] = dot_nn(normed, wv()).astype(BF16)
            return carry

        lax.fori_loop(0, length // chunk, project, 0, unroll=2)
        here = pl.ds(pl.multiple_of(own, rows), rows)
        emb_ref[0] = dot_nt(own_x(), wet_ref[...]) + bias
        q_ref[0] = dot_nn(n_ref[0, here, :], wq()).astype(BF16)

    block = ROW_BLOCK
    sure = length - rows
    columns = sure + lax.broadcasted_iota(jnp.int32, (1, rows), 1)
    allowed = columns < support
    cols = pl.ds(pl.multiple_of(pl.program_id(1) * HEAD_DIM, HEAD_DIM), HEAD_DIM)

    for i in range(rows // block):
        at = slice(i * block, (i + 1) * block)
        qh = q_ref[0, at, cols]
        first = dot_nt(qh, k_ref[0, :sure, cols])
        last = dot_nt(qh, k_ref[0, sure:, cols])
        last = jnp.where(allowed, last, -1e30)
        top = jnp.maximum(
            jnp.max(first, axis=-1, keepdims=True), jnp.max(last, axis=-1, keepdims=True)
        )
        pf = jnp.exp2((first - top) * (SCALE * LOG2E))
        pt = jnp.exp2((last - top) * (SCALE * LOG2E))
        total = jnp.sum(pf, axis=-1, keepdims=True) + jnp.sum(pt, axis=-1, keepdims=True)
        pf, pt = pf.astype(BF16), pt.astype(BF16)
        p_ref[0, 0, at, :sure] = pf
        p_ref[0, 0, at, sure:] = pt
        linv = 1.0 / total
        linv_ref[0, 0, at, :] = jnp.broadcast_to(linv, (block, LANES))
        out = dot_nn(pf, v_ref[0, :sure, cols]) + dot_nn(pt, v_ref[0, sure:, cols])
        mixed_ref[0, at, cols] = out * linv


def attend_kernel(support_ref, x_ref, wet_ref, vec_ref, wq_ref, wk_ref, wv_ref, *outs):
    rows = outs[0].shape[1]
    own = lax.axis_index("table") * rows

    def get_x(i, chunk):
        return x_ref[0, pl.ds(pl.multiple_of(i * chunk, chunk), chunk), :]

    attend_core(
        support_ref[pl.program_id(0)],
        get_x,
        lambda: x_ref[0, pl.ds(pl.multiple_of(own, rows), rows), :],
        wet_ref, vec_ref, lambda: wq_ref[...], lambda: wk_ref[...], lambda: wv_ref[...], *outs,
    )


def attend_gather_kernel(
    dp_size, table_size, support_ref, feat_ref, mask_ref, ew_ref, packed_ref, wq_in, wk_in, wv_in, wo_in, wu_in, wd_in,
    q_ref, k_ref, v_ref, n_ref, u_ref, inv_ref, emb_ref, mixed_ref, p_ref, linv_ref,
    x_out, wet_out, wq_out, wk_out, wv_out, vec_ref, bu_ref, wo_out, wu_out, wd_out,
    x_buf, wet_buf, packed_buf, wq_buf, wk_buf, wv_buf, own_sem, send_sem, recv_sem,
):
    micro_id, head = pl.program_id(0), pl.program_id(1)
    micro, rows, feat = feat_ref.shape
    shard = wq_in.shape[0]
    width = wq_in.shape[1]
    place = Place(dp_size, table_size)
    dp, table = place.me["dp"], place.me["table"]
    sems = (send_sem, recv_sem)
    hops = place.hops["dp"]
    forth, back = hops[1:] + hops[:1], hops[:0:-1] + hops[:1]
    base = 0

    def gather(axis, order, full, own=None):
        nonlocal base
        flow = Gather(place, axis, order, full, sems, base, own)
        base += flow.steps
        return flow

    table_order = place.hops["table"][::-1]
    feats = [gather("table", table_order, x_buf.at[m]) for m in range(micro)]
    early = [
        gather("dp", forth, wk_buf),
        gather("dp", back, wv_buf),
        gather("dp", forth, wet_buf),
        gather("dp", back, packed_buf),
        gather("dp", back, wq_buf),
    ]
    late = [
        gather("dp", forth, wo_out, wo_in),
        gather("dp", forth, wu_out, wu_in),
        gather("dp", back, wd_out, wd_in),
    ]
    own_copies = [
        pltpu.make_async_copy(src, dst.at[dp], own_sem.at[i])
        for i, (src, dst) in enumerate(((wo_in, wo_out), (wu_in, wu_out), (wd_in, wd_out)))
    ]
    out_copies = [
        pltpu.make_async_copy(src, dst, own_sem.at[3 + i])
        for i, (src, dst) in enumerate(
            ((wet_buf, wet_out), (wq_buf, wq_out), (wk_buf, wk_out), (wv_buf, wv_out))
        )
    ]

    def at_step(m, h):
        return pl.when((micro_id == m) & (head == h))

    @at_step(0, 0)
    def _():
        barrier = pltpu.get_barrier_semaphore()
        place.signal_all(barrier)
        for m in range(micro):
            mask = mask_ref[m].astype(F32)
            x_buf[m, table] = jnp.zeros((rows, LANES), BF16)
            x_buf[m, table, :, :feat] = (feat_ref[m].astype(F32) * mask).astype(BF16)
        tall = jnp.concatenate(
            [ew_ref[...].astype(F32), jnp.zeros((LANES - feat, shard), F32)], axis=0
        )
        wet_buf[dp] = tall.T.astype(BF16)
        packed_buf[dp] = packed_ref[...]
        wq_buf[dp] = wq_in[...]
        wk_buf[dp] = wk_in[...]
        wv_buf[dp] = wv_in[...]
        place.wait_all(barrier)
        feats[0].start(0)
        for flow in early:
            flow.start(0)
        for copy in own_copies:
            copy.start()
        for step in range(1, len(hops)):
            if step < feats[0].steps:
                feats[0].arrive(step - 1)
                feats[0].start(step)
            for flow in early:
                flow.arrive(step - 1)
                flow.start(step)
        for flow in early:
            flow.arrive(len(hops) - 1)
        for flow in late:
            flow.start(0)
        feats[0].arrive(feats[0].steps - 1)
        if micro > 1:
            feats[1].start(0)
        for copy in out_copies:
            copy.start()
        lane = lax.broadcasted_iota(jnp.int32, (8, LANES), 1)
        for d in range(0, dp_size, 2):
            pair = jnp.where(lane < shard, packed_buf[d], pltpu.roll(packed_buf[d + 1], shard, 1))
            vec_ref[:, d * shard : (d + 2) * shard] = pair
        for d in range(dp_size):
            bu_ref[:, 2 * d * LANES : (2 * d + 1) * LANES] = packed_buf[d, 6:7, :]
            bu_ref[:, (2 * d + 1) * LANES : (2 * d + 2) * LANES] = packed_buf[d, 7:8, :]

    @at_step(0, 1)
    def _():
        for flow in late:
            flow.arrive(0)
            flow.start(1)
        feats[1].arrive(0)
        feats[1].start(1)

    @at_step(1, 0)
    def _():
        feats[1].arrive(1)
        feats[2].start(0)

    @at_step(1, 1)
    def _():
        for flow in late:
            flow.arrive(1)
            flow.start(2)
        feats[2].arrive(0)
        feats[2].start(1)

    @at_step(2, 0)
    def _():
        feats[2].arrive(1)
        for flow in late:
            flow.arrive(2)

    def get_x(i, chunk):
        per = rows // chunk
        x = x_buf[micro_id, i // per, pl.ds(pl.multiple_of((i % per) * chunk, chunk), chunk), :]
        x_out[0, pl.ds(pl.multiple_of(i * chunk, chunk), chunk), :] = x
        return x

    def full(buf):
        return lambda: buf[...].reshape(width, width)

    attend_core(
        support_ref[micro_id], get_x, lambda: x_buf[micro_id, table], WetView(wet_buf), vec_ref,
        full(wq_buf), full(wk_buf), full(wv_buf),
        q_ref, k_ref, v_ref, n_ref, u_ref, inv_ref, emb_ref, mixed_ref, p_ref, linv_ref,
    )

    @at_step(micro - 1, HEADS - 1)
    def _():
        for flow in feats + early + late:
            flow.sent()
        for copy in own_copies + out_copies:
            copy.wait()


class WetView:
    def __init__(self, buf):
        self.buf = buf

    def __getitem__(self, _):
        return self.buf[...].reshape(-1, self.buf.shape[-1])


def attend_shapes(rows, length, width):
    out = [
        ((rows, width), BF16),
        ((length, width), BF16),
        ((length, width), BF16),
        ((length, width), BF16),
        ((length, width), BF16),
        ((length, LANES), F32),
        ((rows, width), F32),
        ((rows, width), F32),
    ]
    return out, [((rows, length), BF16), ((rows, LANES), F32)]


def attend_forward_gather(dp_size, table_size, support, feat, mask, ew, packed, wq, wk, wv, wo, wu, wd):
    micro, rows, _ = feat.shape
    length = rows * table_size
    width = wq.shape[1]
    out, heads = attend_shapes(rows, length, width)
    whole = pl.BlockSpec(memory_space=pltpu.VMEM)
    far = pl.BlockSpec(memory_space=pl.ANY)

    def gathered(a):
        return jax.ShapeDtypeStruct((dp_size,) + a.shape, a.dtype)

    wet = jax.ShapeDtypeStruct((dp_size, wq.shape[0], LANES), BF16)
    steps = len(hops_of(dp_size))
    table_steps = len(hops_of(table_size))
    count = micro * table_steps + 8 * steps
    return pl.pallas_call(
        functools.partial(attend_gather_kernel, dp_size, table_size),
        grid=(micro, HEADS),
        in_specs=[pl.BlockSpec(memory_space=pltpu.SMEM)] + [whole] * 7 + [far] * 3,
        out_specs=[micro_spec(s) for s, _ in out]
        + [head_spec(s) for s, _ in heads]
        + [micro_spec((length, LANES))]
        + [far] * 4
        + [const_spec((8, width)), const_spec((1, wu.shape[1]))]
        + [far] * 3,
        out_shape=[jax.ShapeDtypeStruct((micro,) + s, d) for s, d in out]
        + [jax.ShapeDtypeStruct((micro, HEADS) + s, d) for s, d in heads]
        + [jax.ShapeDtypeStruct((micro, length, LANES), BF16)]
        + [wet, gathered(wq), gathered(wk), gathered(wv)]
        + [jax.ShapeDtypeStruct((8, width), F32), jax.ShapeDtypeStruct((1, wu.shape[1]), F32)]
        + [gathered(wo), gathered(wu), gathered(wd)],
        scratch_shapes=[
            pltpu.VMEM((micro, table_size, rows, LANES), BF16),
            pltpu.VMEM(wet.shape, BF16),
            pltpu.VMEM((dp_size,) + packed.shape, F32),
            pltpu.VMEM((dp_size,) + wq.shape, BF16),
            pltpu.VMEM((dp_size,) + wk.shape, BF16),
            pltpu.VMEM((dp_size,) + wv.shape, BF16),
            pltpu.SemaphoreType.DMA((7,)),
            pltpu.SemaphoreType.DMA((count,)),
            pltpu.SemaphoreType.DMA((count,)),
        ],
        compiler_params=vmem(54, collective_id=0, has_side_effects=True),
        name="attend_forward_gather",
    )(support, feat, mask, ew, packed, wq, wk, wv, wo, wu, wd)


def attend_forward(support, x_all, wet, vec, wq, wk, wv, rows):
    micro, length, lanes = x_all.shape
    width = wq.shape[0]
    out, heads = attend_shapes(rows, length, width)
    return pl.pallas_call(
        attend_kernel,
        grid=(micro, HEADS),
        in_specs=[
            pl.BlockSpec(memory_space=pltpu.SMEM),
            micro_spec((length, lanes)),
            const_spec(wet.shape),
            const_spec(vec.shape),
            const_spec(wq.shape),
            const_spec(wk.shape),
            const_spec(wv.shape),
        ],
        out_specs=[micro_spec(s) for s, _ in out] + [head_spec(s) for s, _ in heads],
        out_shape=[jax.ShapeDtypeStruct((micro,) + s, d) for s, d in out]
        + [jax.ShapeDtypeStruct((micro, HEADS) + s, d) for s, d in heads],
        compiler_params=vmem(50),
        name="attend_forward",
    )(support, x_all, wet, vec, wq, wk, wv)


def mlp_kernel(
    mixed_ref, emb_ref, cot_ref, wo_ref, wu_ref, wd_ref, vec_ref, bu_ref,
    act_ref, ghid_ref, gmix_ref, dwo_ref, dwu_ref, dwd_ref, dvec_ref,
    acc_o, acc_u, acc_d, gn2_ref, out_ref,
):
    step, last = pl.program_id(0), pl.num_programs(0) - 1
    hidden_units = wu_ref.shape[1]
    chunk = 512

    @pl.when(step == 0)
    def _():
        acc_o[...] = jnp.zeros_like(acc_o)
        acc_u[...] = jnp.zeros_like(acc_u)
        acc_d[...] = jnp.zeros_like(acc_d)
        dvec_ref[...] = jnp.zeros_like(dvec_ref)

    gain, shift, dbias = vec_ref[3:4, :], vec_ref[4:5, :], vec_ref[5:6, :]
    mixed = mixed_ref[0].astype(BF16)
    g_out = cot_ref[0]
    hidden = emb_ref[0] + dot_nn(mixed, wo_ref[...])
    unit, inv = norm_parts(hidden)
    normed = (unit * gain + shift).astype(BF16)
    out_ref[...] = hidden + dbias
    normed_t = normed.T
    g_out_t = g_out.T
    for f in range(hidden_units // chunk):
        cols = slice(f * chunk, (f + 1) * chunk)
        pre = dot_nn(normed, wu_ref[:, cols]) + bu_ref[:, cols]
        cdf = 0.5 * (1.0 + lax.erf(pre * INV_SQRT_TWO))
        pdf = jnp.exp(-0.5 * pre * pre) * INV_SQRT_TWO_PI
        act = (pre * cdf).astype(BF16)
        out_ref[...] += dot_nn(act, wd_ref[cols, :])
        g_act = dot_nt(g_out, wd_ref[cols, :])
        g_pre_f = g_act * (cdf + pre * pdf)
        g_pre = g_pre_f.astype(BF16)
        acc_u[:, cols] += dot_nn(normed_t, g_pre)
        acc_d[:, cols] += dot_nn(g_out_t, act)
        dvec_ref[8 + f : 9 + f, :] += row_sum(g_pre_f)
        g_part = dot_nt(g_pre, wu_ref[:, cols])
        if f == 0:
            gn2_ref[...] = g_part
        else:
            gn2_ref[...] += g_part
    act_ref[0] = out_ref[...].astype(BF16)
    g_norm = gn2_ref[...]
    g_out_f = g_out.astype(F32)
    dvec_ref[3:4, :] += row_sum(g_norm * unit)
    dvec_ref[4:5, :] += row_sum(g_norm)
    dvec_ref[5:6, :] += row_sum(g_out_f)
    g_hidden = g_out_f + norm_back(g_norm, unit, inv, gain)
    ghid_ref[0] = g_hidden
    branch = g_hidden.astype(BF16)
    acc_o[...] += dot_tn(mixed, branch)
    gmix_ref[0] = dot_nt(branch, wo_ref[...]).astype(BF16)

    @pl.when(step == last)
    def _():
        dwo_ref[...] = acc_o[...].astype(BF16)
        dwu_ref[...] = acc_u[...].astype(BF16)
        for f in range(hidden_units // chunk):
            cols = slice(f * chunk, (f + 1) * chunk)
            dwd_ref[cols, :] = acc_d[:, cols].T.astype(BF16)


def mlp_both(mixed, emb, cot, wo, wu, wd, vec, bu):
    micro, rows, width = mixed.shape
    hidden_units = wu.shape[1]
    per_micro = [((rows, width), BF16), ((rows, width), F32), ((rows, width), BF16)]
    summed = [
        ((width, width), BF16),
        ((width, hidden_units), BF16),
        ((hidden_units, width), BF16),
        ((16, width), F32),
    ]
    return pl.pallas_call(
        mlp_kernel,
        grid=(micro,),
        in_specs=[micro_spec((rows, width))] * 3
        + [const_spec(a.shape) for a in (wo, wu, wd, vec, bu)],
        out_specs=[micro_spec(s) for s, _ in per_micro] + [const_spec(s) for s, _ in summed],
        out_shape=[jax.ShapeDtypeStruct((micro,) + s, d) for s, d in per_micro]
        + [jax.ShapeDtypeStruct(s, d) for s, d in summed],
        scratch_shapes=[
            pltpu.VMEM((width, width), F32),
            pltpu.VMEM((width, hidden_units), F32),
            pltpu.VMEM((width, hidden_units), F32),
            pltpu.VMEM((rows, width), F32),
            pltpu.VMEM((rows, width), F32),
        ],
        compiler_params=vmem(50),
        name="mlp_both",
    )(mixed, emb, cot, wo, wu, wd, vec, bu)


def attend_back_core(
    hooks, p_ref, linv_ref, k_ref, v_ref, q_ref, gmix_ref, mixed_ref, n_ref, u_ref, inv_ref, x_ref, ghid_ref,
    mask_ref, wet_ref, vec_ref, wq_ref, wk_ref, wv_ref,
    dvec_ref, dkv_ref, dq_ref, ig_acc, wkv_t, acc_e, acc_q, acc_kv,
):
    step, head = pl.program_id(0), pl.program_id(1)
    length, rows, width = n_ref.shape[1], dq_ref.shape[0], dq_ref.shape[1]
    own = lax.axis_index("table") * rows
    here = pl.ds(pl.multiple_of(own, rows), rows)

    @pl.when((step == 0) & (head == 0))
    def _():
        acc_e[...] = jnp.zeros_like(acc_e)
        acc_q[...] = jnp.zeros_like(acc_q)
        acc_kv[...] = jnp.zeros_like(acc_kv)
        dvec_ref[...] = jnp.zeros_like(dvec_ref)
        wkv_t[:width, :] = wk_ref[...].T
        wkv_t[width:, :] = wv_ref[...].T

    keys = KEY_BLOCK
    linv = linv_ref[0, 0][:, :1]
    g_low = (gmix_ref[0].astype(F32) * linv).astype(BF16)
    delta = jnp.sum(mixed_ref[0] * g_low.astype(F32), axis=-1, keepdims=True)
    g_low_t = g_low.T
    q_t = q_ref[0].T
    k_rows = pl.ds(pl.multiple_of(head * HEAD_DIM, HEAD_DIM), HEAD_DIM)
    v_rows = pl.ds(pl.multiple_of(width + head * HEAD_DIM, HEAD_DIM), HEAD_DIM)
    dq = None
    for j in range(length // keys):
        at = slice(j * keys, (j + 1) * keys)
        p = p_ref[0, 0, :, at]
        dp = dot_nt(g_low, v_ref[0, at, :])
        ds = (p.astype(F32) * (dp - delta)).astype(BF16)
        dkv_ref[v_rows, at] = dot_nn(g_low_t, p).astype(BF16)
        dkv_ref[k_rows, at] = (dot_nn(q_t, ds) * SCALE).astype(BF16)
        dq_part = dot_nn(ds, k_ref[0, at, :])
        dq = dq_part if dq is None else dq + dq_part
    dq_ref[:, k_rows] = (dq * SCALE).astype(BF16)

    @pl.when(head == HEADS - 1)
    def _():
        gain = vec_ref[1:2, :]
        mask = mask_ref[0].astype(F32)
        part = 256
        for i in range(2 * width // part):
            at = slice(i * part, (i + 1) * part)
            acc_kv[at, :] += dot_nn(dkv_ref[at, :], n_ref[0])
        dq = dq_ref[...]
        acc_q[...] += dot_tn(n_ref[0, here, :], dq)
        hooks.projections_done()

        def embed_back(g_norm, unit, inv, extra, x):
            dvec_ref[1:2, :] += row_sum(g_norm * unit)
            dvec_ref[2:3, :] += row_sum(g_norm)
            g_emb = norm_back(g_norm, unit, inv, gain)
            if extra is not None:
                g_emb = g_emb + extra
            dvec_ref[0:1, :] += row_sum(g_emb)
            g_emb = g_emb.astype(BF16)
            acc_e[...] += dot_tn(x, g_emb)
            return dot_nn(g_emb, wet_ref[...]) * mask

        def others(i, carry):
            at = pl.ds(pl.multiple_of(i * part, part), part)
            g_norm = dot_tn(dkv_ref[:, at], wkv_t[...])
            ig_acc[at, :] = embed_back(
                g_norm, u_ref[0, at, :].astype(F32), inv_ref[0, at, :][:, :1], None, x_ref[0, at, :]
            )
            return carry

        count = length // part
        groups = 4
        for g in range(groups):
            lax.fori_loop(g * count // groups, (g + 1) * count // groups, others, 0, unroll=2)
            hooks.group_done(g)
        ig_acc[here, :] += embed_back(
            dot_nt(dq, wq_ref[...]),
            u_ref[0, here, :].astype(F32),
            inv_ref[0, here, :][:, :1],
            ghid_ref[0],
            x_ref[0, here, :],
        )
        hooks.rows_done()


class Alone:
    def __init__(self, ig_ref, ig_acc):
        self.ig_ref, self.ig_acc = ig_ref, ig_acc

    def projections_done(self):
        pass

    def group_done(self, g):
        pass

    def rows_done(self):
        self.ig_ref[0] = self.ig_acc[...].astype(BF16)


def attend_back_kernel(*refs):
    ins, rest = refs[:18], refs[18:]
    ig_ref, dwe_ref, dwq_ref, dwk_ref, dwv_ref, dvec_ref = rest[:6]
    scratch = rest[6:]
    ig_acc, acc_e, acc_q, acc_kv = scratch[2], scratch[4], scratch[5], scratch[6]
    width = acc_q.shape[0]
    attend_back_core(Alone(ig_ref, ig_acc), *ins, dvec_ref, *scratch)

    @pl.when((pl.program_id(0) == pl.num_programs(0) - 1) & (pl.program_id(1) == HEADS - 1))
    def _():
        dwe_ref[...] = acc_e[...].T.astype(BF16)
        dwq_ref[...] = acc_q[...].astype(BF16)
        dwk_ref[...] = acc_kv[:width, :].T.astype(BF16)
        dwv_ref[...] = acc_kv[width:, :].T.astype(BF16)


class Sums:
    def __init__(self, mlp, tail, small, igs, ig_bufs, ig_out, near_sem, write_tail, write_embed, write_small):
        self.mlp, self.tail, self.small, self.igs = mlp, tail, small, igs
        self.ig_bufs, self.ig_out, self.near_sem = ig_bufs, ig_out, near_sem
        self.write_tail, self.write_embed, self.write_small = write_tail, write_embed, write_small
        self.micro, self.head = pl.program_id(0), pl.program_id(1)
        self.count = len(igs)

    def at(self, m, h):
        return pl.when((self.micro == m) & (self.head == h))

    def mlp_step(self, i):
        for flow in self.mlp:
            if i:
                flow.arrive(i - 1)
            if i < flow.steps:
                flow.start(i)

    def ig_step(self, m, i):
        flow = self.igs[m]
        if i:
            flow.arrive(i - 1)
        if i < flow.steps:
            flow.start(i)
        else:
            self.ig_out[m] = flow.total()[...].astype(F32)

    def ticks(self, place):
        @self.at(0, 0)
        def _():
            barrier = pltpu.get_barrier_semaphore()
            place.signal_all(barrier)
            for i, flow in enumerate(self.mlp):
                for copy in flow.near_copies(self.near_sem.at[i]):
                    copy.start()
            place.wait_all(barrier)
            self.mlp_step(0)

        @self.at(0, 1)
        def _():
            for i, flow in enumerate(self.mlp):
                flow.near_wait(self.near_sem.at[i])
            self.mlp_step(1)

        @self.at(1, 0)
        def _():
            self.mlp_step(2)

        @self.at(1, 2)
        def _():
            self.ig_step(0, 1)
            self.mlp_step(3)

        @self.at(2, 0)
        def _():
            self.mlp_step(5)

        @self.at(2, 2)
        def _():
            self.ig_step(1, 1)

        @self.at(2, 3)
        def _():
            self.mlp_step(6)

    def last(self):
        return pl.when(self.micro == self.count - 1)

    def projections_done(self):
        @pl.when(self.micro == 1)
        def _():
            self.ig_step(0, 2)
            self.mlp_step(4)

        @self.last()
        def _():
            self.ig_step(1, 2)
            self.write_tail()
            for flow in self.tail[1:]:
                flow.start(0)

    def group_done(self, g):
        step = {0: 1, 1: 2, 3: 3}.get(g)
        if step is None:
            return

        @self.last()
        def _():
            for flow in self.tail[1:]:
                flow.arrive(step - 1)
                flow.start(step)

    def rows_done(self):
        for m in range(self.count):

            @pl.when(self.micro == m)
            def _():
                self.ig_bufs[m][...] = self.ig_value()
                self.ig_step(m, 0)

        @self.last()
        def _():
            self.write_embed()
            self.write_small()
            first, others = self.tail[0], self.tail[1:]
            done = 3
            lagging = [first, self.small]
            m = self.count - 1
            for i in range(first.steps + 1):
                for flow in lagging:
                    if 0 < i <= flow.steps:
                        flow.arrive(i - 1)
                    if i < flow.steps:
                        flow.start(i)
                if 0 < i <= self.igs[m].steps:
                    self.ig_step(m, i)
                if done < others[0].steps:
                    for flow in others:
                        flow.arrive(done)
                        if done + 1 < flow.steps:
                            flow.start(done + 1)
                    done += 1
                if i == 0:
                    self.mlp_step(7)
            for flow in self.mlp + self.tail + [self.small] + self.igs:
                flow.sent()


def attend_back_reduce_kernel(dp_size, table_size, *refs):
    refs = list(refs)

    def take(n):
        out = refs[:n]
        del refs[:n]
        return out

    ins = take(18)
    grads = take(3)
    (small_in,) = take(1)
    ig_out, small_out = take(2)
    totals = take(7)
    (dvec_ref,) = take(1)
    core = take(7)
    ig_acc, acc_e, acc_q, acc_kv = core[2], core[4], core[5], core[6]
    width = acc_q.shape[0]
    place = Place(dp_size, table_size)
    steps = len(place.hops["dp"]) + len(place.hops["table"]) + 1
    nears = take(3)
    mlp_scratch = [take(steps) for _ in range(3)]
    tail_grads = take(4)
    tail_scratch = [take(steps) for _ in range(4)]
    sums, got = take(2)
    micro = ig_out.shape[0]
    ig_bufs = take(micro)
    ig_scratch = [take(len(place.hops["table"])) for _ in range(micro)]
    near_sem, send_sem, recv_sem = refs
    sems = (send_sem, recv_sem)
    hops = place.hops["dp"]
    forth, back = hops, hops[:1] + hops[:0:-1]
    base = 0

    def shard(order, grad, scratch, near=None):
        nonlocal base
        flow = Shard(place, order, grad, scratch, sems, base, near)
        base += flow.steps
        return flow

    mlp = [shard(o, g, s, n) for o, g, s, n in zip((forth, forth, back), grads, mlp_scratch, nears)]
    tail = [shard(o, g, s) for o, g, s in zip((forth, back, forth, back), tail_grads, tail_scratch)]
    both = [("dp", hop) for hop in hops] + [("table", hop) for hop in place.hops["table"]]
    small = Total(place, both, sums, got, sems, base)
    base += small.steps
    igs = []
    for m in range(micro):
        buf = ig_bufs[m]
        igs.append(
            Reduce(
                place, "table", place.hops["table"],
                lambda s, buf=buf: buf.at[toggled_by(place.me["table"], s)],
                ig_scratch[m], sems, base,
            )
        )
        base += igs[-1].steps

    def write_tail():
        tail_grads[1][...] = acc_q[...].astype(BF16).reshape(tail_grads[1].shape)
        tail_grads[2][...] = acc_kv[:width, :].T.astype(BF16).reshape(tail_grads[2].shape)
        tail_grads[3][...] = acc_kv[width:, :].T.astype(BF16).reshape(tail_grads[3].shape)

    def write_embed():
        tail_grads[0][...] = acc_e[...].T.astype(BF16).reshape(tail_grads[0].shape)

    def write_small():
        sums[0] = small_in[...] + jnp.concatenate([dvec_ref[...], jnp.zeros_like(dvec_ref)], axis=0)

    hooks = Sums(
        mlp, tail, small, igs, ig_bufs, ig_out, near_sem, write_tail, write_embed, write_small
    )
    hooks.ig_value = lambda: ig_acc[...].astype(BF16).reshape(ig_bufs[0].shape)
    hooks.ticks(place)
    attend_back_core(hooks, *ins, dvec_ref, *core)

    @hooks.at(micro - 1, HEADS - 1)
    def _():
        for flow, out in zip(tail + mlp, totals):
            out[...] = flow.full[...]
        small_out[...] = sums[small.steps]


def back_scratch(length, rows, width):
    return [
        pltpu.VMEM((2 * width, length), BF16),
        pltpu.VMEM((rows, width), BF16),
        pltpu.VMEM((length, LANES), F32),
        pltpu.VMEM((2 * width, width), BF16),
        pltpu.VMEM((LANES, width), F32),
        pltpu.VMEM((width, width), F32),
        pltpu.VMEM((2 * width, width), F32),
    ]


def back_specs(by_head, cols, varied, fixed):
    return (
        [head_spec(a.shape[2:]) for a in by_head]
        + [head_cols_spec(a.shape[1]) for a in cols]
        + [micro_spec(a.shape[1:]) for a in varied]
        + [const_spec(a.shape) for a in fixed]
    )


def attend_backward(p, linv, k, v, q, gmix, mixed, n, u, inv, x, ghid, mask, wet, vec, wq, wk, wv):
    micro, rows, width = q.shape
    length = k.shape[1]
    varied = (n, u, inv, x, ghid, mask)
    fixed = (wet, vec, wq, wk, wv)
    summed = [(wet.shape, BF16)] + [((width, width), BF16)] * 3 + [((8, width), F32)]
    return pl.pallas_call(
        attend_back_kernel,
        grid=(micro, HEADS),
        in_specs=back_specs((p, linv), (k, v, q, gmix, mixed), varied, fixed),
        out_specs=[micro_spec((length, LANES))] + [const_spec(s) for s, _ in summed],
        out_shape=[jax.ShapeDtypeStruct((micro, length, LANES), BF16)]
        + [jax.ShapeDtypeStruct(s, d) for s, d in summed],
        scratch_shapes=back_scratch(length, rows, width),
        compiler_params=vmem(50),
        name="attend_backward",
    )(p, linv, k, v, q, gmix, mixed, *varied, *fixed)


def attend_backward_reduce(
    dp_size, table_size, grads, small, p, linv, k, v, q, gmix, mixed, n, u, inv, x, ghid, mask, wet, vec, wq, wk, wv
):
    micro, rows, width = q.shape
    length = k.shape[1]
    varied = (n, u, inv, x, ghid, mask)
    fixed = (wet, vec, wq, wk, wv)
    far = pl.BlockSpec(memory_space=pl.ANY)
    tail = [(dp_size, table_size, width // dp_size // table_size, c) for c in (LANES, width, width, width)]
    blocks = [t[1:] for t in tail] + [g.shape[1:] for g in grads]
    hops = len(hops_of(dp_size)) + len(hops_of(table_size))
    table_hops = hops_of(table_size)
    scratch = [pltpu.VMEM((8, width), F32)] + back_scratch(length, rows, width)
    scratch += [pltpu.VMEM((dp_size // 2,) + g.shape[1:], BF16) for g in grads]
    for g in grads:
        scratch += shard_scratch(dp_size, table_size, g.shape[1:], BF16)
    scratch += [pltpu.VMEM(t, BF16) for t in tail]
    for t in tail:
        scratch += shard_scratch(dp_size, table_size, t[1:], BF16)
    scratch += [pltpu.VMEM((hops + 1,) + small.shape, F32), pltpu.VMEM((hops,) + small.shape, F32)]
    scratch += [pltpu.VMEM((table_size, rows, LANES), BF16)] * micro
    for _ in range(micro):
        scratch += [pltpu.VMEM((table_size >> (i + 1), rows, LANES), BF16) for i in range(len(table_hops))]
    count = 7 * (hops + len(table_hops)) + hops + micro * len(table_hops)
    scratch += [pltpu.SemaphoreType.DMA((3,))] + [pltpu.SemaphoreType.DMA((count,))] * 2
    return pl.pallas_call(
        functools.partial(attend_back_reduce_kernel, dp_size, table_size),
        grid=(micro, HEADS),
        in_specs=back_specs((p, linv), (k, v, q, gmix, mixed), varied, fixed)
        + [far] * 3
        + [const_spec(small.shape)],
        out_specs=[const_spec((micro, rows, LANES)), const_spec(small.shape)]
        + [const_spec(b) for b in blocks],
        out_shape=[
            jax.ShapeDtypeStruct((micro, rows, LANES), F32),
            jax.ShapeDtypeStruct(small.shape, F32),
        ]
        + [jax.ShapeDtypeStruct(b, BF16) for b in blocks],
        scratch_shapes=scratch,
        compiler_params=vmem(60, collective_id=1, has_side_effects=True),
        name="attend_backward_reduce",
    )(p, linv, k, v, q, gmix, mixed, *varied, *fixed, *grads, small)


def finish_kernel(feat, shard, ig_in, small_in, *refs):
    ins, outs = refs[:7], refs[7:]
    ig_out, dwe, others, vecs, bu = outs[0], outs[1], outs[2:8], outs[8:14], outs[14]
    ig_out[...] = ig_in[:, :, :feat]
    dwe[...] = ins[0][...].astype(F32).T[:feat, :]
    for src, dst in zip(ins[1:], others):
        dst[...] = src[...].astype(F32)
    small = small_in[...]
    width = small.shape[1]
    dp = lax.axis_index("dp")
    turned = pltpu.roll(small, lax.rem(width - dp * shard, width), 1)
    for i, out in enumerate(vecs):
        out[...] = turned[i : i + 1, :shard]
    per_row = width // bu.shape[1]
    rows = small[8 : 8 + 4, :]
    row = dp // per_row
    pick = lax.broadcasted_iota(jnp.int32, rows.shape, 0) == row
    line = jnp.sum(jnp.where(pick, rows, 0.0), axis=0, keepdims=True)
    at = (dp % per_row) * bu.shape[1]
    bu[...] = pltpu.roll(jnp.broadcast_to(line, (8, width)), lax.rem(width - at, width), 1)[:1, : bu.shape[1]]


def finish(feat, ff_shard, ig, small, totals):
    micro, rows, _ = ig.shape
    shard = totals[0].shape[0]
    out_shape = (
        [jax.ShapeDtypeStruct((micro, rows, feat), F32), jax.ShapeDtypeStruct((feat, shard), F32)]
        + [jax.ShapeDtypeStruct(t.shape, F32) for t in totals[1:]]
        + [jax.ShapeDtypeStruct((1, shard), F32)] * 6
        + [jax.ShapeDtypeStruct((1, ff_shard), F32)]
    )
    return pl.pallas_call(
        functools.partial(finish_kernel, feat, shard),
        out_shape=out_shape,
        compiler_params=vmem(50),
        name="finish",
    )(ig, small, *totals)


def body(
    dp_size, table_size, features, feature_mask, support_count, embed_weight, embed_bias, gain_first, shift_first,
    query_weight, key_weight, value_weight, out_weight, gain_second, shift_second, up_weight, up_bias,
    down_weight, down_bias, cotangent,
):
    micro, _, rows, feat = features.shape
    shard, width = query_weight.shape
    hidden_units = up_weight.shape[1]
    ff_shard = up_bias.shape[0]
    features, cotangent, support = features[:, 0], cotangent[:, 0], support_count[:, 0]
    mask = jnp.pad(feature_mask[:, 0].astype(F32), ((0, 0), (0, LANES - feat)))[:, None, :]
    smalls = jnp.stack([embed_bias, gain_first, shift_first, gain_second, shift_second, down_bias])
    if 2 * shard == LANES and micro == 3:
        packed = jnp.concatenate(
            [jnp.pad(smalls, ((0, 0), (0, LANES - shard))), up_bias.reshape(2, LANES)]
        ).astype(F32)
        got = attend_forward_gather(
            dp_size, table_size, support, features, feature_mask, embed_weight, packed,
            query_weight, key_weight, value_weight, out_weight, up_weight, down_weight,
        )
        q, k, v, n, u, inv, emb, mixed, p, linv, x = got[:11]
        wet, wq, wk, wv = (g.reshape(-1, g.shape[-1]) for g in got[11:15])
        vec, bu = got[15:17]
        wo, wu, wd = (g.reshape(-1, g.shape[-1]) for g in got[17:])
        activations, ghid, gmix, dwo, dwu, dwd, small = mlp_both(mixed, emb, cotangent, wo, wu, wd, vec, bu)
        grads = [g.reshape(dp_size, table_size, -1, g.shape[1]) for g in (dwo, dwu, dwd)]
        ig, small, *totals = attend_backward_reduce(
            dp_size, table_size, grads, small, p, linv, k, v, q, gmix, mixed, n, u, inv, x, ghid, mask,
            wet, vec, wq, wk, wv,
        )
        totals = [t.reshape(-1, t.shape[-1]) for t in totals]
        out = finish(feat, ff_shard, ig, small, totals)
        ig, dwe, dwq, dwk, dwv, dwo, dwu, dwd = out[:8]
        smalls = [o.reshape(-1) for o in out[8:14]]
        dbu = out[14].reshape(-1)
    else:
        x = jnp.pad(features, ((0, 0), (0, 0), (0, LANES - feat))) * mask.astype(BF16)
        wet = jnp.pad(embed_weight, ((0, LANES - feat), (0, 0))).T
        shards = [wet, query_weight, key_weight, value_weight, out_weight, up_weight, down_weight]
        wet, wq, wk, wv, wo, wu, wd = (lax.all_gather(s, "dp", axis=0, tiled=True) for s in shards)
        vec = jnp.pad(lax.all_gather(smalls, "dp", axis=1, tiled=True).astype(F32), ((0, 2), (0, 0)))
        bu = lax.all_gather(up_bias, "dp", axis=0, tiled=True).astype(F32)[None]
        x = lax.all_gather(x, "table", axis=1, tiled=True)
        q, k, v, n, u, inv, emb, mixed, p, linv = attend_forward(support, x, wet, vec, wq, wk, wv, rows)
        activations, ghid, gmix, dwo, dwu, dwd, small = mlp_both(mixed, emb, cotangent, wo, wu, wd, vec, bu)
        ig, dwe, dwq, dwk, dwv, dvec = attend_backward(
            p, linv, k, v, q, gmix, mixed, n, u, inv, x, ghid, mask, wet, vec, wq, wk, wv
        )
        big = [dwe, dwq, dwk, dwv, dwo, dwu, dwd]
        own = [lax.psum_scatter(g.astype(F32), "dp", scatter_dimension=0, tiled=True) for g in big]
        dwe, dwq, dwk, dwv, dwo, dwu, dwd = (lax.psum(g, "table") for g in own)
        dwe = dwe[:, :feat].T
        dvec = jnp.concatenate([dvec[:3], small[3:6]])
        smalls = lax.psum(lax.psum_scatter(dvec, "dp", scatter_dimension=1, tiled=True), "table")
        dbu = small[8:].reshape(-1)[:hidden_units]
        dbu = lax.psum(lax.psum_scatter(dbu, "dp", scatter_dimension=0, tiled=True), "table")
        ig = lax.psum_scatter(ig.astype(F32), "table", scatter_dimension=1, tiled=True)[:, :, :feat]
    return (
        activations[:, None], ig[:, None], dwe, smalls[0], smalls[1], smalls[2],
        dwq, dwk, dwv, dwo, smalls[3], smalls[4], dwu, dbu, dwd, smalls[5],
    )


def solution(mesh):
    rows, cols, vecs = P("dp", None), P(None, "dp"), P("dp")
    table = P(None, "dp", "table", None)
    return jax.shard_map(
        functools.partial(body, mesh.shape["dp"], mesh.shape["table"]),
        mesh=mesh,
        in_specs=(
            table, P(None, "dp", None), cols, cols, vecs, vecs, vecs, rows, rows, rows, rows,
            vecs, vecs, rows, vecs, rows, vecs, table,
        ),
        out_specs=(
            table, table, cols, vecs, vecs, vecs, rows, rows, rows, rows, vecs, vecs, rows, vecs, rows, vecs,
        ),
        check_vma=False,
    )
```

time: 1990 us -> 257 us (0.13)
  waiting for transfers between devices: 1340 us -> 0 us
  matrix products: 336 us -> 0 us
  Pallas kernels: 0 us -> 235 us
  blocking collectives: 117 us -> 0 us
  other arithmetic: 112 us -> 1.26 us
  local copies, waits for them, and re-layouts: 57.2 us -> 19.4 us
    reduce_scatter x27 -> x0, waiting for transfers between devices: 1080 us -> none  [the longest x3 218 us: body(): lax.psum_scatter(grad_keys, 'table', scatter_dimension=0, tiled=True)]
    dot_general x81 -> x0, matrix products: 336 us -> none  [the longest x21 62.6 us: inner(): lax.dot_general(left_side, right_side, (((0,), (0,)), ((), ())), preferre...]
    pallas_call x0 -> x4, Pallas kernels: none -> 235 us  [the longest x1 125 us: attend_backward_reduce(): pl.pallas_call(functools.partial(attend_back_reduce_kernel, dp_size, tabl...]
    all_gather x8 -> x0, waiting for transfers between devices: 180 us -> none  [the longest x3 77.1 us: body(): lax.all_gather(value_here, 'table', axis=0, tiled=True)]
    psum x1 -> x0, waiting for transfers between devices: 81.8 us -> none  [body(): lax.psum(owned[4].astype(jnp.bfloat16), 'table').astype(jnp.float32)]
    convert_element_type x33 -> x2, other arithmetic: 71.3 us -> 1.26 us  [the longest x1 1.25 us: body(): packed = jnp.concatenate([jnp.pad(smalls, ((0, 0), (0, LANES - shard))),...]
    all_gather x6 -> x0, blocking collectives: 56.1 us -> none  [the longest x1 10.7 us: fetch_weights(): lax.all_gather(shards[7], 'dp', axis=0, tiled=True)]
    unnamed x2 -> x0, blocking collectives: 39.9 us -> none
  transfers between devices with their start and end apart: 36 -> 0, of which waited for: 33 -> 0; matrix products, arithmetic and copies ran while one was open for 19% -> 0% of each run, Pallas kernels for 0% -> 0%
where the time goes in v1:
time: 257 us; the launch traced here: 256 us
  Pallas kernels  235 us (91%)
  local copies, waits for them, and re-layouts  19.4 us (8%)
    pallas_call x1, Pallas kernels, attend_backward_reduce(): pl.pallas_call(functools.partial(attend_back_reduce_kernel, dp_size, tabl...  125 us
    pallas_call x1, Pallas kernels, attend_forward_gather(): pl.pallas_call(functools.partial(attend_gather_kernel, dp_size, table_siz...  74.1 us
    pallas_call x1, Pallas kernels, mlp_both(): pl.pallas_call(mlp_kernel, grid=(micro,), in_specs=[micro_spec((rows, wid...  33.9 us
    unnamed x36, local copies, waits for them, and re-layouts  18.1 us

profile of v1, /device:TPU:0, one launch (start us, length us, event | category | flops | bytes accessed | tf_op | source)
XLA Modules:
  0.0 256.1 jit_solution(314756673880362664)
XLA Ops:
  0.6 1.9 copy.34
  2.6 1.4 copy.35.ew_ref
  4.0 0.8 stack.27
  4.7 1.3 fusion.2.packed_ref
  6.0 74.1 %attend_forward_gather.1 = (bf16[3,512,512]{2,1,0:T(8,128)(2,1)}, bf16[3,2048,512]{2,1,0:T(8,128)(2,1)}, bf16[3,2048,512]{2,1,0:T(8,128)(2,1)}, bf16[3,2048,512]...) custom-call(s32[3]{0:T(128)} %bitcast.60, ...), custom_call_target="tpu_custom_call" | custom-call | tf_op jit(solution)/shard_map/attend_forward_gather/pallas_call | solution.py:541
  80.1 0.0 copy-start.3
  80.1 1.0 copy-done.3
  81.2 0.0 copy-start.6
  81.2 0.7 copy-done.6
  81.9 0.0 copy-start.14
  81.9 0.7 copy-done.14
  82.6 0.0 copy-start.15
  82.6 33.9 %mlp_both.1 = (bf16[3,512,512]{2,1,0:T(8,128)(2,1)}, f32[3,512,512]{2,1,0:T(8,128)}, bf16[3,512,512]{2,1,0:T(8,128)(2,1)S(1)}, bf16[512,512]{1,0:T(8,128)(2,1)S(...) custom-call(f32[3,512,512]{2,1,0:T(8,128)} %get-tuple-element.67.mixed_ref.refs_6_, ...), custom_call_target="tpu_custom_call" | custom-call | tf_op jit(solution)/shard_map/mlp_both/pallas_call | solution.py:671
  116.5 0.0 copy-start
  116.5 1.2 copy-done
  117.7 0.0 copy-start.2
  117.7 0.8 copy-done.2
  118.5 0.0 copy-start.11
  118.5 0.6 copy-done.11
  119.1 0.0 copy-done.15
  119.1 0.6 broadcast_in_dim.10.refs_12_
  119.7 125.5 %attend_backward_reduce.1 = (f32[3,512,128]{2,1,0:T(8,128)}, f32[16,512]{1,0:T(8,128)}, bf16[4,16,128]{2,1,0:T(8,128)(2,1)}, bf16[4,16,512]{2,1,0:T(8,128)(2,1)}...) custom-call(bf16[3,4,512,2048]{3,2,1,0:T(8,128)(2,1)} %get-tuple-ele, ...), custom_call_target="tpu_custom_call" | custom-call | tf_op jit(solution)/shard_map/attend_backward_reduce/pallas_call | solution.py:1080
  245.1 0.0 copy-start.1
  245.1 1.1 copy-done.1
  246.3 0.0 copy-start.4
  246.3 0.9 copy-done.4
  247.2 0.0 copy-start.5
  247.2 0.9 copy-done.5
  248.2 0.0 copy-start.7
  248.2 0.8 copy-done.7
  249.0 0.0 copy-start.8
  249.0 0.8 copy-done.8
  249.8 0.0 copy-start.9
  249.8 0.8 copy-done.9
  250.7 0.0 copy-start.10
  250.7 0.8 copy-done.10
  251.5 0.0 copy-start.12
  251.5 0.8 copy-done.12
  252.3 0.0 copy-start.13
  252.3 0.7 copy-done.13
  253.0 1.2 finish.1
  254.2 1.2 copy.38
  255.4 0.7 copy.39
  (2 shorter events, 0.0 us)
Async XLA Ops:
  80.1 1.0 copy-start.3
  81.2 0.7 copy-start.6
  81.9 0.7 copy-start.14
  82.6 36.5 %copy-start.15 = (s32[3,1,100]{2,1,0:T(1,128)S(1)}, s32[3,1,100]{2,1,0:T(1,128)}, u32[]{:S(2)}) copy-start(s32[3,1,100]{2,1,0:T(1,128)} %mask_ref.1) | copy-start | bytes 3604
  116.5 1.2 copy-start
  117.7 0.8 copy-start.2
  118.5 0.6 copy-start.11
  245.1 1.1 copy-start.1
  246.3 0.9 copy-start.4
  247.2 0.9 copy-start.5
  248.2 0.8 copy-start.7
  249.0 0.8 copy-start.8
  249.8 0.8 copy-start.9
  250.7 0.8 copy-start.10
  251.5 0.8 copy-start.12
  252.3 0.7 copy-start.13

commit v2 on v1

v2 whole, which is shorter than its diff:
```python
import functools

import jax
import jax.numpy as jnp
from jax import lax
from jax.experimental import pallas as pl
from jax.experimental.pallas import tpu as pltpu
from jax.sharding import PartitionSpec as P

HEADS = 4
HEAD_DIM = 128
LANES = 128
EPSILON = 1e-5
SCALE = HEAD_DIM**-0.5
LOG2E = 1.4426950408889634
ROW_BLOCK = 256
KEY_BLOCK = 512
INV_SQRT_TWO = 0.7071067811865476
INV_SQRT_TWO_PI = 0.3989422804014327
BF16 = jnp.bfloat16
F32 = jnp.float32
MESH = pl.DeviceIdType.MESH


def dot_nn(a, b):
    return lax.dot_general(a, b, (((1,), (0,)), ((), ())), preferred_element_type=F32)


def dot_nt(a, b):
    return lax.dot_general(a, b, (((1,), (1,)), ((), ())), preferred_element_type=F32)


def dot_tn(a, b):
    return lax.dot_general(a, b, (((0,), (0,)), ((), ())), preferred_element_type=F32)


def norm_parts(v):
    mean = jnp.mean(v, axis=-1, keepdims=True)
    centred = v - mean
    inv = lax.rsqrt(jnp.mean(centred * centred, axis=-1, keepdims=True) + EPSILON)
    return centred * inv, inv


def norm_back(grad, unit, inv, gain):
    q = grad * gain
    return inv * (
        q
        - jnp.mean(q, axis=-1, keepdims=True)
        - unit * jnp.mean(q * unit, axis=-1, keepdims=True)
    )


def row_sum(v):
    return jnp.sum(v, axis=0, keepdims=True)


def const_spec(shape):
    return pl.BlockSpec(shape, lambda *g: (0,) * len(shape))


def micro_spec(shape):
    return pl.BlockSpec((1,) + shape, lambda m, *g: (m,) + (0,) * len(shape))


def head_spec(shape):
    return pl.BlockSpec((1, 1) + shape, lambda m, h: (m, h) + (0,) * len(shape))


def head_cols_spec(rows):
    return pl.BlockSpec((1, rows, HEAD_DIM), lambda m, h: (m, 0, h))


def vmem(mib, **extra):
    return pltpu.CompilerParams(vmem_limit_bytes=mib * 2**20, **extra)


def toggled(index, hop):
    return index + hop * (1 - 2 * ((index // hop) % 2))


def toggled_by(index, hops):
    for hop in hops:
        index = toggled(index, hop)
    return index


def subsets(hops):
    out = [()]
    for hop in hops:
        out = out + [s + (hop,) for s in out]
    return out


def hops_of(size):
    return [1 << i for i in range(size.bit_length() - 1)]


class Place:
    def __init__(self, dp_size, table_size):
        self.size = {"dp": dp_size, "table": table_size}
        self.hops = {axis: hops_of(n) for axis, n in self.size.items()}
        self.me = {"dp": lax.axis_index("dp"), "table": lax.axis_index("table")}

    def partner(self, axis, hop):
        there = dict(self.me)
        there[axis] = toggled(there[axis], hop)
        return (there["dp"], there["table"])

    def at(self, axis, shift):
        n = self.size[axis]
        return lax.rem(self.me[axis] + (shift + n), n)

    def ahead(self, axis, shift):
        there = dict(self.me)
        there[axis] = self.at(axis, shift)
        return (there["dp"], there["table"])

    def greet(self, all_dp):
        barrier = pltpu.get_barrier_semaphore()
        peers = [self.ahead("table", s) for s in range(1, self.size["table"])]
        if all_dp:
            peers += [self.ahead("dp", s) for s in range(1, self.size["dp"])]
        else:
            peers += [self.partner("dp", hop) for hop in self.hops["dp"]]
        for peer in peers:
            pl.semaphore_signal(barrier, inc=1, device_id=peer, device_id_type=MESH)
        return lambda: pl.semaphore_wait(barrier, len(peers))


class Swap:
    def __init__(self, place, axis, sems, base, send, put):
        self.place, self.axis, self.sems, self.base = place, axis, sems, base
        self.send, self.put = send, put
        self.shifts = range(1, place.size[axis])

    def copy(self, shift, src, dst):
        index = self.base + shift - 1
        return pltpu.make_async_remote_copy(
            src_ref=src, dst_ref=dst, send_sem=self.sems[0].at[index], recv_sem=self.sems[1].at[index],
            device_id=self.place.ahead(self.axis, shift), device_id_type=MESH,
        )

    def start_one(self, shift):
        to = self.place.at(self.axis, shift)
        self.copy(shift, self.send(to), self.put(self.place.me[self.axis], shift)).start()

    def start(self):
        for shift in self.shifts:
            self.start_one(shift)

    def arrive_one(self, shift):
        here = self.put(self.place.at(self.axis, -shift), shift)
        self.copy(shift, here, here).wait_recv()
        return here

    def arrive(self):
        return [self.arrive_one(shift) for shift in self.shifts]

    def sent(self):
        for shift in self.shifts:
            out = self.send(self.place.at(self.axis, shift))
            self.copy(shift, out, out).wait_send()


def remote(place, axis, hop, src, dst, sems, index):
    return pltpu.make_async_remote_copy(
        src_ref=src, dst_ref=dst, send_sem=sems[0].at[index], recv_sem=sems[1].at[index],
        device_id=place.partner(axis, hop), device_id_type=MESH,
    )


class Gather:
    def __init__(self, place, axis, hops, full, sems, base, own=None):
        self.place, self.axis, self.hops = place, axis, hops
        self.full, self.sems, self.base, self.own = full, sems, base, own
        self.steps = len(hops)

    def whole(self, step):
        part = self.full.at[pl.ds(0, 1 << step)]
        return remote(self.place, self.axis, self.hops[step], part, part, self.sems, self.base + step)

    def start(self, step):
        for s in subsets(self.hops[:step]):
            block = self.full.at[toggled_by(self.place.me[self.axis], s)]
            src = block if s or self.own is None else self.own
            remote(
                self.place, self.axis, self.hops[step], src, block, self.sems, self.base + step
            ).start()

    def arrive(self, step):
        self.whole(step).wait_recv()

    def sent(self):
        for step in range(self.steps):
            self.whole(step).wait_send()


def add_into(into, other):
    lead = into.shape[:-2]
    rows, cols = into.shape[-2:]
    if lead:
        for i in range(lead[0]):
            add_into(into.at[i], other.at[i])
        return
    piece = min(rows, max(16, 65536 // cols))
    piece = rows if rows % piece else piece

    def body(i, carry):
        at = pl.ds(pl.multiple_of(i * piece, piece), piece)
        into[at, :] = (into[at, :].astype(F32) + other[at, :].astype(F32)).astype(into.dtype)
        return carry

    if rows == piece:
        into[...] = (into[...].astype(F32) + other[...].astype(F32)).astype(into.dtype)
    else:
        lax.fori_loop(0, rows // piece, body, 0)


class Reduce:
    def __init__(self, place, axis, hops, blocks, bufs, sems, base, near=None):
        self.place, self.axis, self.hops = place, axis, hops
        self.held, self.near = blocks, near
        self.bufs, self.sems, self.base = bufs, sems, base
        self.steps = len(hops)

    def mine(self, step, s):
        if step == 0:
            return self.held(s)
        order = [set(t) for t in subsets(self.hops[step:])]
        return self.bufs[step - 1].at[order.index(set(s))]

    def copy(self, step, src, dst):
        return remote(self.place, self.axis, self.hops[step], src, dst, self.sems, self.base + step)

    def start(self, step):
        for i, s in enumerate(subsets(self.hops[step + 1 :])):
            self.copy(step, self.mine(step, s + (self.hops[step],)), self.bufs[step].at[i]).start()

    def arrive(self, step):
        self.copy(step, self.bufs[step], self.bufs[step]).wait_recv()
        for i, s in enumerate(subsets(self.hops[step + 1 :])):
            near = step == 0 and self.near is not None
            add_into(self.bufs[step].at[i], self.near.at[i] if near else self.mine(step, s))

    def total(self):
        return self.bufs[-1].at[0]

    def sent(self):
        for step in range(self.steps):
            self.copy(step, self.bufs[step], self.bufs[step]).wait_send()


class Shard:
    def __init__(self, place, dp_hops, grad, scratch, sems, base, near=None):
        n, m = len(dp_hops), len(place.hops["table"])
        dp_bufs, table_bufs, full = scratch[:n], scratch[n : n + m], scratch[n + m]
        self.place, self.grad, self.near = place, grad, near

        def blocks(s):
            return grad.at[toggled_by(place.me["dp"], s)]

        self.dp = Reduce(place, "dp", dp_hops, blocks, dp_bufs, sems, base, near)
        table_hops = place.hops["table"]
        base += self.dp.steps

        def parts(s):
            return self.dp.total().at[toggled_by(place.me["table"], s)]

        self.table = Reduce(place, "table", table_hops, parts, table_bufs, sems, base)
        base += self.table.steps
        self.full = full
        self.back = Gather(place, "table", table_hops[::-1], full, sems, base)
        self.flows = [(f, i) for f in (self.dp, self.table, self.back) for i in range(f.steps)]
        self.steps = len(self.flows)

    def near_copies(self, sem):
        halves = subsets(self.dp.hops[1:])
        return [
            pltpu.make_async_copy(self.dp.held(s), self.near.at[i], sem) for i, s in enumerate(halves)
        ]

    def near_wait(self, sem):
        pltpu.make_async_copy(self.near, self.near, sem).wait()

    def start(self, step):
        flow, i = self.flows[step]
        if flow is self.back and i == 0:
            self.full[self.place.me["table"]] = self.table.total()[...]
        flow.start(i)

    def arrive(self, step):
        flow, i = self.flows[step]
        flow.arrive(i)

    def sent(self):
        for flow in (self.dp, self.table, self.back):
            flow.sent()


class QuickShard:
    def __init__(self, place, dp_hops, grad, scratch, sems, base):
        n = len(dp_hops)
        got, full = scratch[n], scratch[n + 1]
        self.place, self.full = place, full

        def blocks(s):
            return grad.at[toggled_by(place.me["dp"], s)]

        self.dp = Reduce(place, "dp", dp_hops, blocks, scratch[:n], sems, base)
        base += n
        self.out = Swap(
            place, "table", sems, base, lambda t: self.dp.total().at[t], lambda t, s: got.at[s - 1]
        )
        base += place.size["table"] - 1
        self.back = Swap(
            place, "table", sems, base, lambda t: full.at[place.me["table"]], lambda t, s: full.at[t]
        )
        self.steps = n + 2

    def start(self, step):
        n = self.dp.steps
        if step < n:
            self.dp.start(step)
        elif step == n:
            self.out.start()
        else:
            self.back.start()

    def arrive(self, step):
        n = self.dp.steps
        if step < n:
            self.dp.arrive(step)
        elif step == n:
            me = self.place.me["table"]
            total = self.dp.total()[me].astype(F32)
            for got in self.out.arrive():
                total = total + got[...].astype(F32)
            self.full[me] = total.astype(self.full.dtype)
        else:
            self.back.arrive()

    def sent(self):
        self.dp.sent()
        self.out.sent()
        self.back.sent()


def quick_scratch(dp_size, table_size, block, dtype):
    out = [pltpu.VMEM((dp_size >> (i + 1),) + block, dtype) for i in range(len(hops_of(dp_size)))]
    return out + [pltpu.VMEM((table_size - 1,) + block[1:], dtype), pltpu.VMEM(block, dtype)]


def quick_sems(dp_size, table_size):
    return len(hops_of(dp_size)) + 2 * (table_size - 1)


class Small:
    def __init__(self, place, block, got_dp, part, got_table, sems, base):
        self.place, self.block, self.part = place, block, part
        self.first = Swap(place, "dp", sems, base, block, lambda t, s: got_dp.at[s - 1])
        base += place.size["dp"] - 1
        self.second = Swap(
            place, "table", sems, base, lambda t: part, lambda t, s: got_table.at[s - 1]
        )
        self.steps = 2

    def start(self, step):
        (self.first, self.second)[step].start()

    def arrive(self, step):
        if step == 0:
            total = self.block(self.place.me["dp"])[...].astype(F32)
            for got in self.first.arrive():
                total = total + got[...].astype(F32)
            self.part[...] = total.astype(self.part.dtype)
        else:
            total = self.part[...].astype(F32)
            for got in self.second.arrive():
                total = total + got[...].astype(F32)
            self.total = total

    def sent(self):
        self.first.sent()
        self.second.sent()


def small_scratch(dp_size, table_size, block, dtype):
    return [
        pltpu.VMEM((dp_size - 1,) + block, dtype),
        pltpu.VMEM(block, dtype),
        pltpu.VMEM((table_size - 1,) + block, dtype),
    ]


def shard_scratch(dp_size, table_size, block, dtype):
    out = [pltpu.VMEM((dp_size >> (i + 1),) + block, dtype) for i in range(len(hops_of(dp_size)))]
    out += [
        pltpu.VMEM((table_size >> (i + 1),) + block[1:], dtype) for i in range(len(hops_of(table_size)))
    ]
    out.append(pltpu.VMEM(block, dtype))
    return out


def attend_core(
    support, order, get_x, wet_ref, vec_ref, wk, wv, wq,
    q_ref, k_ref, v_ref, n_ref, u_ref, inv_ref, emb_ref, mixed_ref, p_ref, linv_ref,
):
    length, rows = n_ref.shape[1], q_ref.shape[1]
    own = lax.axis_index("table")
    bias, gain, shift = vec_ref[0:1, :], vec_ref[1:2, :], vec_ref[2:3, :]
    chunk = 256

    @pl.when(pl.program_id(1) == 0)
    def _():
        for ready, block in order:
            ready()

            def project(i, carry):
                at = pl.ds(pl.multiple_of(block * rows + i * chunk, chunk), chunk)
                part = pl.ds(pl.multiple_of(i * chunk, chunk), chunk)
                embedded = dot_nt(get_x(block, part), wet_ref[...]) + bias
                unit, inv = norm_parts(embedded)
                normed = (unit * gain + shift).astype(BF16)
                n_ref[0, at, :] = normed
                u_ref[0, at, :] = unit.astype(BF16)
                inv_ref[0, at, :] = jnp.broadcast_to(inv, (chunk, LANES))
                k_ref[0, at, :] = dot_nn(normed, wk()).astype(BF16)
                v_ref[0, at, :] = dot_nn(normed, wv()).astype(BF16)
                return carry

            lax.fori_loop(0, rows // chunk, project, 0, unroll=True)
        here = pl.ds(pl.multiple_of(own * rows, rows), rows)
        emb_ref[0] = dot_nt(get_x(own, slice(None)), wet_ref[...]) + bias
        q_ref[0] = dot_nn(n_ref[0, here, :], wq()).astype(BF16)

    block = ROW_BLOCK
    sure = length - rows
    columns = sure + lax.broadcasted_iota(jnp.int32, (1, rows), 1)
    allowed = columns < support
    cols = pl.ds(pl.multiple_of(pl.program_id(1) * HEAD_DIM, HEAD_DIM), HEAD_DIM)

    for i in range(rows // block):
        at = slice(i * block, (i + 1) * block)
        qh = q_ref[0, at, cols]
        first = dot_nt(qh, k_ref[0, :sure, cols])
        last = dot_nt(qh, k_ref[0, sure:, cols])
        last = jnp.where(allowed, last, -1e30)
        top = jnp.maximum(
            jnp.max(first, axis=-1, keepdims=True), jnp.max(last, axis=-1, keepdims=True)
        )
        pf = jnp.exp2((first - top) * (SCALE * LOG2E))
        pt = jnp.exp2((last - top) * (SCALE * LOG2E))
        total = jnp.sum(pf, axis=-1, keepdims=True) + jnp.sum(pt, axis=-1, keepdims=True)
        pf, pt = pf.astype(BF16), pt.astype(BF16)
        p_ref[0, 0, at, :sure] = pf
        p_ref[0, 0, at, sure:] = pt
        linv = 1.0 / total
        linv_ref[0, 0, at, :] = jnp.broadcast_to(linv, (block, LANES))
        out = dot_nn(pf, v_ref[0, :sure, cols]) + dot_nn(pt, v_ref[0, sure:, cols])
        mixed_ref[0, at, cols] = out * linv


def attend_kernel(support_ref, x_ref, wet_ref, vec_ref, wq_ref, wk_ref, wv_ref, *outs):
    rows = outs[0].shape[1]

    def get_x(block, part):
        x = x_ref[0, pl.ds(pl.multiple_of(block * rows, rows), rows), :]
        return x if part == slice(None) else x_ref[0, pl.ds(block * rows + part.start, part.size), :]

    attend_core(
        support_ref[pl.program_id(0)],
        [(lambda: None, block) for block in range(x_ref.shape[1] // rows)],
        get_x, wet_ref, vec_ref, lambda: wk_ref[...], lambda: wv_ref[...], lambda: wq_ref[...], *outs,
    )


def attend_gather_kernel(
    dp_size, table_size, support_ref, feat_ref, mask_ref, ew_ref,
    v0_ref, v1_ref, v2_ref, v3_ref, v4_ref, v5_ref, ub_ref, wq_in, wk_in, wv_in, wo_in, wu_in, wd_in,
    q_ref, k_ref, v_ref, n_ref, u_ref, inv_ref, emb_ref, mixed_ref, p_ref, linv_ref,
    x_out, wet_out, wq_out, wk_out, wv_out, vec_ref, bu_ref, wo_out, wu_out, wd_out,
    x_buf, wet_buf, packed_buf, wq_buf, wk_buf, wv_buf, own_sem, send_sem, recv_sem,
):
    micro_id, head = pl.program_id(0), pl.program_id(1)
    micro, feat, rows = feat_ref.shape
    shard = wq_in.shape[0]
    width = wq_in.shape[1]
    place = Place(dp_size, table_size)
    dp, table = place.me["dp"], place.me["table"]
    sems = (send_sem, recv_sem)
    hops = place.hops["dp"]
    forth, back = hops[1:] + hops[:1], hops[:0:-1] + hops[:1]
    last = len(hops) - 1
    base = 0

    def gather(order, full, own=None):
        nonlocal base
        flow = Gather(place, "dp", order, full, sems, base, own)
        base += flow.steps
        return flow

    early = [
        gather(forth, wk_buf),
        gather(back, wv_buf),
        gather(forth, wet_buf),
        gather(back, packed_buf),
    ]
    query = gather(forth, wq_buf)
    late = [gather(forth, wo_out, wo_in), gather(forth, wu_out, wu_in), gather(back, wd_out, wd_in)]
    feats = []
    for m in range(micro):
        own_x = x_buf.at[m, table]
        feats.append(
            Swap(
                place, "table", sems, base,
                lambda t, own_x=own_x: own_x,
                lambda t, s, m=m: x_buf.at[m, t],
            )
        )
        base += table_size - 1
    own_copies = [
        pltpu.make_async_copy(src, dst.at[dp], own_sem.at[i])
        for i, (src, dst) in enumerate(((wo_in, wo_out), (wu_in, wu_out), (wd_in, wd_out)))
    ]
    out_copies = [
        pltpu.make_async_copy(src, dst, own_sem.at[3 + i])
        for i, (src, dst) in enumerate(
            ((wet_buf, wet_out), (wq_buf, wq_out), (wk_buf, wk_out), (wv_buf, wv_out))
        )
    ]

    def at_step(m, h):
        return pl.when((micro_id == m) & (head == h))

    @at_step(0, 0)
    def _():
        wait_all = place.greet(False)
        wet_buf[dp] = jnp.zeros((shard, LANES), BF16)
        wet_buf[dp, :, :feat] = ew_ref[...]
        packed_buf[dp] = jnp.zeros((8, LANES), F32)
        for i, ref in enumerate((v0_ref, v1_ref, v2_ref, v3_ref, v4_ref, v5_ref)):
            packed_buf[dp, i : i + 1, :shard] = ref[...].astype(F32)
        packed_buf[dp, 6:8, :] = ub_ref[...].astype(F32)
        wk_buf[dp] = wk_in[...]
        wv_buf[dp] = wv_in[...]
        wq_buf[dp] = wq_in[...]

        def fill(m):
            tall = jnp.concatenate(
                [feat_ref[m].astype(F32), jnp.zeros((LANES - feat, rows), F32)], axis=0
            ).T
            x_buf[m, table] = jnp.zeros((rows, LANES), BF16)
            x_buf[m, table, :, :feat] = (tall[:, :feat] * mask_ref[m].astype(F32)).astype(BF16)

        fill(0)
        wait_all()
        for flow in early:
            flow.start(0)
        feats[0].start()
        for copy in own_copies:
            copy.start()
        for m in range(1, micro):
            fill(m)
        for step in range(last):
            for flow in early:
                flow.arrive(step)
                flow.start(step + 1)
            if step == 0:
                query.start(0)
            else:
                query.arrive(step - 1)
                query.start(step)
        for flow in early:
            flow.arrive(last)
        for flow in late:
            flow.start(0)
        lane = lax.broadcasted_iota(jnp.int32, (8, LANES), 1)
        for d in range(0, dp_size, 2):
            pair = jnp.where(lane < shard, packed_buf[d], pltpu.roll(packed_buf[d + 1], shard, 1))
            vec_ref[:, d * shard : (d + 2) * shard] = pair
        for d in range(dp_size):
            bu_ref[:, 2 * d * LANES : (2 * d + 1) * LANES] = packed_buf[d, 6:7, :]
            bu_ref[:, (2 * d + 1) * LANES : (2 * d + 2) * LANES] = packed_buf[d, 7:8, :]

    @at_step(0, 1)
    def _():
        for flow in late:
            flow.arrive(0)
            flow.start(1)
        for copy in out_copies:
            copy.start()
        feats[1].start()

    @at_step(1, 1)
    def _():
        for flow in late:
            flow.arrive(1)
            flow.start(2)
        feats[2].start()

    @at_step(2, 0)
    def _():
        for flow in late:
            flow.arrive(2)

    def get_x(block, part):
        return x_buf[micro_id, block, part, :]

    shifts = sorted(range(1, table_size), key=lambda s: (min(s, table_size - s), s))

    def ready(i, shift):
        def wait():
            if i == 1:

                @pl.when(micro_id == 0)
                def _():
                    query.arrive(last - 1)
                    query.start(last)

            if shift:
                for m in range(micro):

                    @pl.when(micro_id == m)
                    def _():
                        feats[m].arrive_one(shift)

            if i == table_size - 1:
                x_out[0] = x_buf[micro_id].reshape(x_out.shape[1:])

                @pl.when(micro_id == 0)
                def _():
                    query.arrive(last)

        return wait

    order = [(ready(i, shift), place.at("table", -shift)) for i, shift in enumerate([0] + shifts)]

    def full(buf):
        return lambda: buf[...].reshape(width, width)

    attend_core(
        support_ref[micro_id], order, get_x, WetView(wet_buf), vec_ref, full(wk_buf), full(wv_buf), full(wq_buf),
        q_ref, k_ref, v_ref, n_ref, u_ref, inv_ref, emb_ref, mixed_ref, p_ref, linv_ref,
    )

    @at_step(micro - 1, HEADS - 1)
    def _():
        for flow in feats + early + [query] + late:
            flow.sent()
        for copy in own_copies + out_copies:
            copy.wait()


class WetView:
    def __init__(self, buf):
        self.buf = buf

    def __getitem__(self, _):
        return self.buf[...].reshape(-1, self.buf.shape[-1])


def attend_shapes(rows, length, width):
    out = [
        ((rows, width), BF16),
        ((length, width), BF16),
        ((length, width), BF16),
        ((length, width), BF16),
        ((length, width), BF16),
        ((length, LANES), F32),
        ((rows, width), F32),
        ((rows, width), F32),
    ]
    return out, [((rows, length), BF16), ((rows, LANES), F32)]


def attend_forward_gather(dp_size, table_size, support, feat, mask, ew, vecs, ub, wq, wk, wv, wo, wu, wd):
    micro, _, rows = feat.shape
    length = rows * table_size
    width = wq.shape[1]
    out, heads = attend_shapes(rows, length, width)
    whole = pl.BlockSpec(memory_space=pltpu.VMEM)
    far = pl.BlockSpec(memory_space=pl.ANY)

    def gathered(a):
        return jax.ShapeDtypeStruct((dp_size,) + a.shape, a.dtype)

    wet = jax.ShapeDtypeStruct((dp_size, wq.shape[0], LANES), BF16)
    count = micro * (table_size - 1) + 8 * len(hops_of(dp_size))
    return pl.pallas_call(
        functools.partial(attend_gather_kernel, dp_size, table_size),
        grid=(micro, HEADS),
        in_specs=[pl.BlockSpec(memory_space=pltpu.SMEM)] + [whole] * 13 + [far] * 3,
        out_specs=[micro_spec(s) for s, _ in out]
        + [head_spec(s) for s, _ in heads]
        + [micro_spec((length, LANES))]
        + [far] * 4
        + [const_spec((8, width)), const_spec((1, wu.shape[1]))]
        + [far] * 3,
        out_shape=[jax.ShapeDtypeStruct((micro,) + s, d) for s, d in out]
        + [jax.ShapeDtypeStruct((micro, HEADS) + s, d) for s, d in heads]
        + [jax.ShapeDtypeStruct((micro, length, LANES), BF16)]
        + [wet, gathered(wq), gathered(wk), gathered(wv)]
        + [jax.ShapeDtypeStruct((8, width), F32), jax.ShapeDtypeStruct((1, wu.shape[1]), F32)]
        + [gathered(wo), gathered(wu), gathered(wd)],
        scratch_shapes=[
            pltpu.VMEM((micro, table_size, rows, LANES), BF16),
            pltpu.VMEM(wet.shape, BF16),
            pltpu.VMEM((dp_size, 8, LANES), F32),
            pltpu.VMEM((dp_size,) + wq.shape, BF16),
            pltpu.VMEM((dp_size,) + wk.shape, BF16),
            pltpu.VMEM((dp_size,) + wv.shape, BF16),
            pltpu.SemaphoreType.DMA((7,)),
            pltpu.SemaphoreType.DMA((count,)),
            pltpu.SemaphoreType.DMA((count,)),
        ],
        compiler_params=vmem(60, collective_id=0, has_side_effects=True),
        name="attend_forward_gather",
    )(support, feat, mask, ew, *vecs, ub, wq, wk, wv, wo, wu, wd)


def attend_forward(support, x_all, wet, vec, wq, wk, wv, rows):
    micro, length, lanes = x_all.shape
    width = wq.shape[0]
    out, heads = attend_shapes(rows, length, width)
    return pl.pallas_call(
        attend_kernel,
        grid=(micro, HEADS),
        in_specs=[
            pl.BlockSpec(memory_space=pltpu.SMEM),
            micro_spec((length, lanes)),
            const_spec(wet.shape),
            const_spec(vec.shape),
            const_spec(wq.shape),
            const_spec(wk.shape),
            const_spec(wv.shape),
        ],
        out_specs=[micro_spec(s) for s, _ in out] + [head_spec(s) for s, _ in heads],
        out_shape=[jax.ShapeDtypeStruct((micro,) + s, d) for s, d in out]
        + [jax.ShapeDtypeStruct((micro, HEADS) + s, d) for s, d in heads],
        compiler_params=vmem(50),
        name="attend_forward",
    )(support, x_all, wet, vec, wq, wk, wv)


def mlp_kernel(
    mixed_ref, emb_ref, cot_ref, wo_ref, wu_ref, wd_ref, vec_ref, bu_ref,
    act_ref, ghid_ref, gmix_ref, dwo_ref, dwu_ref, dwd_ref, dvec_ref,
    acc_o, acc_u, acc_d, gn2_ref, out_ref,
):
    step, last = pl.program_id(0), pl.num_programs(0) - 1
    hidden_units = wu_ref.shape[1]
    chunk = 512

    @pl.when(step == 0)
    def _():
        acc_o[...] = jnp.zeros_like(acc_o)
        acc_u[...] = jnp.zeros_like(acc_u)
        acc_d[...] = jnp.zeros_like(acc_d)
        dvec_ref[...] = jnp.zeros_like(dvec_ref)

    gain, shift, dbias = vec_ref[3:4, :], vec_ref[4:5, :], vec_ref[5:6, :]
    mixed = mixed_ref[0].astype(BF16)
    g_out = cot_ref[0]
    hidden = emb_ref[0] + dot_nn(mixed, wo_ref[...])
    unit, inv = norm_parts(hidden)
    normed = (unit * gain + shift).astype(BF16)
    out_ref[...] = hidden + dbias
    normed_t = normed.T
    g_out_t = g_out.T
    for f in range(hidden_units // chunk):
        cols = slice(f * chunk, (f + 1) * chunk)
        pre = dot_nn(normed, wu_ref[:, cols]) + bu_ref[:, cols]
        cdf = 0.5 * (1.0 + lax.erf(pre * INV_SQRT_TWO))
        pdf = jnp.exp(-0.5 * pre * pre) * INV_SQRT_TWO_PI
        act = (pre * cdf).astype(BF16)
        out_ref[...] += dot_nn(act, wd_ref[cols, :])
        g_act = dot_nt(g_out, wd_ref[cols, :])
        g_pre_f = g_act * (cdf + pre * pdf)
        g_pre = g_pre_f.astype(BF16)
        acc_u[:, cols] += dot_nn(normed_t, g_pre)
        acc_d[:, cols] += dot_nn(g_out_t, act)
        dvec_ref[8 + f : 9 + f, :] += row_sum(g_pre_f)
        g_part = dot_nt(g_pre, wu_ref[:, cols])
        if f == 0:
            gn2_ref[...] = g_part
        else:
            gn2_ref[...] += g_part
    act_ref[0] = out_ref[...].astype(BF16)
    g_norm = gn2_ref[...]
    g_out_f = g_out.astype(F32)
    dvec_ref[3:4, :] += row_sum(g_norm * unit)
    dvec_ref[4:5, :] += row_sum(g_norm)
    dvec_ref[5:6, :] += row_sum(g_out_f)
    g_hidden = g_out_f + norm_back(g_norm, unit, inv, gain)
    ghid_ref[0] = g_hidden
    branch = g_hidden.astype(BF16)
    acc_o[...] += dot_tn(mixed, branch)
    gmix_ref[0] = dot_nt(branch, wo_ref[...]).astype(BF16)

    @pl.when(step == last)
    def _():
        dwo_ref[...] = acc_o[...].astype(BF16)
        dwu_ref[...] = acc_u[...].astype(BF16)
        for f in range(hidden_units // chunk):
            cols = slice(f * chunk, (f + 1) * chunk)
            dwd_ref[cols, :] = acc_d[:, cols].T.astype(BF16)


def mlp_both(mixed, emb, cot, wo, wu, wd, vec, bu):
    micro, rows, width = mixed.shape
    hidden_units = wu.shape[1]
    per_micro = [((rows, width), BF16), ((rows, width), F32), ((rows, width), BF16)]
    summed = [
        ((width, width), BF16),
        ((width, hidden_units), BF16),
        ((hidden_units, width), BF16),
        ((16, width), F32),
    ]
    return pl.pallas_call(
        mlp_kernel,
        grid=(micro,),
        in_specs=[micro_spec((rows, width))] * 3
        + [const_spec(a.shape) for a in (wo, wu, wd, vec, bu)],
        out_specs=[micro_spec(s) for s, _ in per_micro] + [const_spec(s) for s, _ in summed],
        out_shape=[jax.ShapeDtypeStruct((micro,) + s, d) for s, d in per_micro]
        + [jax.ShapeDtypeStruct(s, d) for s, d in summed],
        scratch_shapes=[
            pltpu.VMEM((width, width), F32),
            pltpu.VMEM((width, hidden_units), F32),
            pltpu.VMEM((width, hidden_units), F32),
            pltpu.VMEM((rows, width), F32),
            pltpu.VMEM((rows, width), F32),
        ],
        compiler_params=vmem(60),
        name="mlp_both",
    )(mixed, emb, cot, wo, wu, wd, vec, bu)


def attend_back_core(
    hooks, order, p_ref, linv_ref, k_ref, v_ref, q_ref, gmix_ref, mixed_ref, n_ref, u_ref, inv_ref, x_ref, ghid_ref,
    wet_ref, vec_ref, wq_ref, wk_ref, wv_ref,
    dvec_ref, dkv_ref, dq_ref, wkv_t, acc_e, acc_q, acc_kv,
):
    step, head = pl.program_id(0), pl.program_id(1)
    length, rows, width = n_ref.shape[1], dq_ref.shape[0], dq_ref.shape[1]
    own = lax.axis_index("table")
    here = pl.ds(pl.multiple_of(own * rows, rows), rows)

    @pl.when((step == 0) & (head == 0))
    def _():
        acc_e[...] = jnp.zeros_like(acc_e)
        acc_q[...] = jnp.zeros_like(acc_q)
        acc_kv[...] = jnp.zeros_like(acc_kv)
        dvec_ref[...] = jnp.zeros_like(dvec_ref)
        for h in range(HEADS):
            cols = slice(h * HEAD_DIM, (h + 1) * HEAD_DIM)
            wkv_t[2 * h * HEAD_DIM : (2 * h + 1) * HEAD_DIM, :] = wk_ref[:, cols].T
            wkv_t[(2 * h + 1) * HEAD_DIM : (2 * h + 2) * HEAD_DIM, :] = wv_ref[:, cols].T

    keys = KEY_BLOCK
    linv = linv_ref[0, 0][:, :1]
    g_low = (gmix_ref[0].astype(F32) * linv).astype(BF16)
    delta = jnp.sum(mixed_ref[0] * g_low.astype(F32), axis=-1, keepdims=True)
    g_low_t = g_low.T
    q_t = q_ref[0].T
    cols = pl.ds(pl.multiple_of(head * HEAD_DIM, HEAD_DIM), HEAD_DIM)
    k_rows = pl.ds(pl.multiple_of(2 * head * HEAD_DIM, HEAD_DIM), HEAD_DIM)
    v_rows = pl.ds(pl.multiple_of((2 * head + 1) * HEAD_DIM, HEAD_DIM), HEAD_DIM)
    dq = None
    for j in range(length // keys):
        at = slice(j * keys, (j + 1) * keys)
        p = p_ref[0, 0, :, at]
        dp = dot_nt(g_low, v_ref[0, at, :])
        ds = (p.astype(F32) * (dp - delta)).astype(BF16)
        dkv_ref[v_rows, at] = dot_nn(g_low_t, p).astype(BF16)
        dkv_ref[k_rows, at] = (dot_nn(q_t, ds) * SCALE).astype(BF16)
        dq_part = dot_nn(ds, k_ref[0, at, :])
        dq = dq_part if dq is None else dq + dq_part
    dq_ref[:, cols] = (dq * SCALE).astype(BF16)

    @pl.when(lax.rem(head, 2) == 1)
    def _():
        part = 2 * HEAD_DIM
        for i in range(2):
            at = pl.ds(pl.multiple_of((head - 1 + i) * part, part), part)
            acc_kv[at, :] += dot_nn(dkv_ref[at, :], n_ref[0])
        pair = pl.ds(pl.multiple_of((head - 1) * HEAD_DIM, part), part)
        acc_q[:, pair] += dot_tn(n_ref[0, here, :], dq_ref[:, pair])

    hooks.pair_done()

    @pl.when(head == HEADS - 1)
    def _():
        gain = vec_ref[1:2, :]
        part = 256
        hooks.tick(HEADS)
        for g, (block, mine) in enumerate(order):

            def others(i, carry):
                at = pl.ds(pl.multiple_of(block * rows + i * part, part), part)
                inner = pl.ds(pl.multiple_of(i * part, part), part)
                unit, inv = u_ref[0, at, :].astype(F32), inv_ref[0, at, :][:, :1]
                g_norm = dot_tn(dkv_ref[:, at], wkv_t[...])
                if mine:
                    g_norm = g_norm + dot_nt(dq_ref[inner, :], wq_ref[...])
                dvec_ref[1:2, :] += row_sum(g_norm * unit)
                dvec_ref[2:3, :] += row_sum(g_norm)
                g_emb = norm_back(g_norm, unit, inv, gain)
                if mine:
                    g_emb = g_emb + ghid_ref[0, inner, :]
                dvec_ref[0:1, :] += row_sum(g_emb)
                g_emb = g_emb.astype(BF16)
                acc_e[...] += dot_tn(x_ref[0, at, :], g_emb)
                hooks.put(block, mine, inner, dot_nn(g_emb, wet_ref[...]))
                return carry

            lax.fori_loop(0, rows // part, others, 0, unroll=True)
            hooks.block_done(g, block, mine)
            hooks.tick(HEADS + 1 + g)


class Alone:
    def __init__(self, ig_ref, rows):
        self.ig_ref, self.rows = ig_ref, rows

    def tick(self, k):
        pass

    def pair_done(self):
        pass

    def put(self, block, mine, inner, value):
        self.ig_ref[0, pl.ds(block * self.rows + inner.start, inner.size), :] = value.astype(BF16)

    def block_done(self, g, block, mine):
        pass


def attend_back_kernel(*refs):
    ins, rest = refs[:17], refs[17:]
    ig_ref, dwe_ref, dwq_ref, dwk_ref, dwv_ref, dvec_ref = rest[:6]
    scratch = rest[6:]
    acc_e, acc_q, acc_kv = scratch[3:6]
    rows = scratch[1].shape[0]
    table = lax.axis_index("table")
    size = ig_ref.shape[1] // rows
    order = [(lax.rem(table + i, size), i == size) for i in range(1, size + 1)]
    attend_back_core(Alone(ig_ref, rows), order, *ins, dvec_ref, *scratch)

    @pl.when((pl.program_id(0) == pl.num_programs(0) - 1) & (pl.program_id(1) == HEADS - 1))
    def _():
        dwe_ref[...] = acc_e[...].T.astype(BF16)
        dwq_ref[...] = acc_q[...].astype(BF16)
        for h in range(HEADS):
            cols = slice(h * HEAD_DIM, (h + 1) * HEAD_DIM)
            dwk_ref[:, cols] = acc_kv[2 * h * HEAD_DIM : (2 * h + 1) * HEAD_DIM, :].T.astype(BF16)
            dwv_ref[:, cols] = acc_kv[(2 * h + 1) * HEAD_DIM : (2 * h + 2) * HEAD_DIM, :].T.astype(BF16)


class Sums:
    def __init__(self, place, mlp, tail, smalls, igs):
        self.place, self.mlp, self.tail, self.smalls, self.igs = place, mlp, tail, smalls, igs
        self.micro, self.head = pl.program_id(0), pl.program_id(1)
        self.count = len(igs)
        self.todo = {}

    def tick(self, k):
        for m in range(self.count):
            actions = self.todo.get((m, k), [])
            if not actions:
                continue

            @pl.when((self.micro == m) & (self.head == k) if k < HEADS else self.micro == m)
            def _():
                for action in actions:
                    action()

    def start_of_step(self):
        for k in range(HEADS):
            self.tick(k)

    def at(self, m, k, action):
        self.todo.setdefault((m, k), []).append(action)

    def step(self, flows, i):
        def action():
            for flow in flows:
                if i:
                    flow.arrive(i - 1)
                if i < flow.steps:
                    flow.start(i)

        return action

    def pair_done(self):
        for g in range(HEADS // 2):

            @pl.when((self.micro == self.count - 1) & (self.head == 2 * g + 1))
            def _():
                self.write_pair(g)
                self.step(self.tail[g], 0)()

    def put(self, block, mine, inner, value):
        if mine:
            self.ig_own[inner, :] = value
            return
        for m in range(self.count):

            @pl.when(self.micro == m)
            def _():
                self.ig_bufs[m][block, inner, :] = value.astype(BF16)

    def block_done(self, g, block, mine):
        for m in range(self.count):

            @pl.when(self.micro == m)
            def _():
                if mine:
                    self.ig_out[m] = self.ig_own[...]
                else:
                    self.igs[m].start_one(g + 1)

    def ig_finish(self, m):
        def action():
            total = self.ig_out[m]
            for got in self.igs[m].arrive():
                total = total + got[...].astype(F32)
            self.ig_out[m] = total

        return action


def attend_back_reduce_kernel(dp_size, table_size, *refs):
    refs = list(refs)

    def take(n):
        out = refs[:n]
        del refs[:n]
        return out

    ins = take(17)
    grads = take(3)
    (small_in,) = take(1)
    ig_out, small_out, embed_out = take(3)
    totals = take(7)
    (dvec_ref,) = take(1)
    core = take(6)
    acc_e, acc_q, acc_kv = core[3:6]
    place = Place(dp_size, table_size)
    hops = place.hops["dp"]
    steps = len(hops) + len(place.hops["table"]) + 1
    nears = take(3)
    mlp_scratch = [take(steps) for _ in range(3)]
    tail_grads = take(4)
    tail_scratch = [take(len(hops) + 2) for _ in range(4)]
    embed_grad, small_grad = take(2)
    embed_scratch, small_scratch_ = take(3), take(3)
    micro = ig_out.shape[0]
    ig_bufs = take(micro)
    ig_got = take(micro)
    (ig_own,) = take(1)
    near_sem, send_sem, recv_sem = refs
    sems = (send_sem, recv_sem)
    forth, back = hops, hops[:1] + hops[:0:-1]
    base = 0

    def count_up(n):
        nonlocal base
        base += n
        return base - n

    mlp = []
    for order, grad, scratch, near in zip((forth, forth, back), grads, mlp_scratch, nears):
        mlp.append(Shard(place, order, grad, scratch, sems, base, near))
        count_up(mlp[-1].steps)
    tail = []
    for g in range(2):
        pair = []
        for i, order in enumerate((forth, back)):
            at = count_up(quick_sems(dp_size, table_size))
            pair.append(
                QuickShard(place, order, tail_grads[2 * g + i], tail_scratch[2 * g + i], sems, at)
            )
        tail.append(pair)
    others = dp_size + table_size - 2
    embed = Small(place, lambda d: embed_grad.at[d], *embed_scratch, sems, count_up(others))
    small = Small(place, lambda d: small_grad, *small_scratch_, sems, count_up(others))
    igs = []
    for m in range(micro):
        igs.append(
            Swap(
                place, "table", sems, count_up(table_size - 1),
                lambda t, m=m: ig_bufs[m].at[t],
                lambda t, s, m=m: ig_got[m].at[s - 1],
            )
        )
    hooks = Sums(place, mlp, tail, (embed, small), igs)
    hooks.ig_bufs, hooks.ig_own, hooks.ig_out = ig_bufs, ig_own, ig_out

    def write_pair(g):
        one, two = tail_grads[2 * g], tail_grads[2 * g + 1]
        shape = one.shape[:-1]

        def put(ref, at, value):
            ref[:, :, :, at * HEAD_DIM : at * HEAD_DIM + value.shape[1]] = value.astype(BF16).reshape(
                shape + (value.shape[1],)
            )

        def rows_of(h, side):
            at = (2 * h + side) * HEAD_DIM
            return acc_kv[at : at + HEAD_DIM, :].T

        put(one, 0, acc_q[:, 2 * g * HEAD_DIM : (2 * g + 2) * HEAD_DIM])
        put(one, 2, rows_of(2 * g, 0))
        put(two, 0, rows_of(2 * g + 1, 0))
        put(two, 1, rows_of(2 * g, 1))
        put(two, 2, rows_of(2 * g + 1, 1))

    hooks.write_pair = write_pair

    def enter():
        wait_all = place.greet(True)
        for i, flow in enumerate(mlp):
            for copy in flow.near_copies(near_sem.at[i]):
                copy.start()
        wait_all()

    def nears_there():
        for i, flow in enumerate(mlp):
            flow.near_wait(near_sem.at[i])

    last = micro - 1
    hooks.at(0, 0, enter)
    hooks.at(0, 0, hooks.step(mlp, 0))
    hooks.at(0, 2, nears_there)
    hooks.at(0, 2, hooks.step(mlp, 1))
    hooks.at(0, 8, hooks.step(mlp, 2))
    hooks.at(1, 2, hooks.step(mlp, 3))
    hooks.at(1, 4, hooks.ig_finish(0))
    hooks.at(1, 4, hooks.step(mlp, 4))
    hooks.at(2, 1, hooks.step(mlp, 5))
    hooks.at(2, 2, hooks.step(tail[0], 1))
    hooks.at(2, 3, hooks.step(tail[0], 2))
    hooks.at(2, 3, hooks.step(mlp, 6))
    hooks.at(2, 4, hooks.ig_finish(1))
    hooks.at(2, 4, hooks.step(tail[0], 3))
    hooks.at(2, 5, hooks.step(tail[1], 1))
    hooks.at(2, 6, hooks.step(tail[0], 4))
    hooks.at(2, 7, hooks.step(tail[1], 2))

    def finish():
        embed_grad[...] = acc_e[...].T.astype(BF16).reshape(embed_grad.shape)
        small_grad[...] = small_in[...] + jnp.concatenate(
            [dvec_ref[...], jnp.zeros_like(dvec_ref)], axis=0
        )
        ends = [embed, small]
        hooks.step(ends, 0)()
        hooks.step(tail[1], 3)()
        hooks.step(mlp, 7)()
        hooks.step(ends, 1)()
        hooks.step(tail[0], 5)()
        hooks.step(tail[1], 4)()
        hooks.ig_finish(last)()
        hooks.step(ends, 2)()
        hooks.step(tail[1], 5)()
        for flow in mlp + tail[0] + tail[1] + ends + igs:
            flow.sent()
        embed_out[...] = embed.total
        small_out[...] = small.total
        for flow, out in zip(mlp + tail[0] + tail[1], totals):
            out[...] = flow.full[...]

    hooks.at(last, 8, finish)
    hooks.start_of_step()
    order = [(place.at("table", i), i == table_size) for i in range(1, table_size + 1)]
    attend_back_core(hooks, order, *ins, dvec_ref, *core)


def back_scratch(length, rows, width):
    return [
        pltpu.VMEM((2 * width, length), BF16),
        pltpu.VMEM((rows, width), BF16),
        pltpu.VMEM((2 * width, width), BF16),
        pltpu.VMEM((LANES, width), F32),
        pltpu.VMEM((width, width), F32),
        pltpu.VMEM((2 * width, width), F32),
    ]


def back_specs(by_head, cols, varied, fixed):
    return (
        [head_spec(a.shape[2:]) for a in by_head]
        + [head_cols_spec(a.shape[1]) for a in cols]
        + [micro_spec(a.shape[1:]) for a in varied]
        + [const_spec(a.shape) for a in fixed]
    )


def attend_backward(p, linv, k, v, q, gmix, mixed, n, u, inv, x, ghid, wet, vec, wq, wk, wv):
    micro, rows, width = q.shape
    length = k.shape[1]
    varied = (n, u, inv, x, ghid)
    fixed = (wet, vec, wq, wk, wv)
    summed = [(wet.shape, BF16)] + [((width, width), BF16)] * 3 + [((8, width), F32)]
    return pl.pallas_call(
        attend_back_kernel,
        grid=(micro, HEADS),
        in_specs=back_specs((p, linv), (k, v, q, gmix, mixed), varied, fixed),
        out_specs=[micro_spec((length, LANES))] + [const_spec(s) for s, _ in summed],
        out_shape=[jax.ShapeDtypeStruct((micro, length, LANES), BF16)]
        + [jax.ShapeDtypeStruct(s, d) for s, d in summed],
        scratch_shapes=back_scratch(length, rows, width),
        compiler_params=vmem(50),
        name="attend_backward",
    )(p, linv, k, v, q, gmix, mixed, *varied, *fixed)


def attend_backward_reduce(
    dp_size, table_size, grads, small, p, linv, k, v, q, gmix, mixed, n, u, inv, x, ghid, wet, vec, wq, wk, wv
):
    micro, rows, width = q.shape
    length = k.shape[1]
    varied = (n, u, inv, x, ghid)
    fixed = (wet, vec, wq, wk, wv)
    far = pl.BlockSpec(memory_space=pl.ANY)
    shard = width // dp_size
    tail = (dp_size, table_size, shard // table_size, 3 * HEAD_DIM)
    blocks = [g.shape[1:] for g in grads] + [tail[1:]] * 4
    hops = len(hops_of(dp_size)) + len(hops_of(table_size))
    scratch = [pltpu.VMEM((8, width), F32)] + back_scratch(length, rows, width)
    scratch += [pltpu.VMEM((dp_size // 2,) + g.shape[1:], BF16) for g in grads]
    for g in grads:
        scratch += shard_scratch(dp_size, table_size, g.shape[1:], BF16)
    scratch += [pltpu.VMEM(tail, BF16)] * 4
    for _ in range(4):
        scratch += quick_scratch(dp_size, table_size, tail[1:], BF16)
    scratch += [pltpu.VMEM((dp_size, shard, LANES), BF16), pltpu.VMEM(small.shape, F32)]
    scratch += small_scratch(dp_size, table_size, (shard, LANES), BF16)
    scratch += small_scratch(dp_size, table_size, small.shape, F32)
    scratch += [pltpu.VMEM((table_size, rows, LANES), BF16)] * micro
    scratch += [pltpu.VMEM((table_size - 1, rows, LANES), BF16)] * micro
    scratch += [pltpu.VMEM((rows, LANES), F32)]
    count = 3 * (hops + len(hops_of(table_size))) + 4 * quick_sems(dp_size, table_size)
    count += 2 * (dp_size + table_size - 2) + micro * (table_size - 1)
    scratch += [pltpu.SemaphoreType.DMA((3,))] + [pltpu.SemaphoreType.DMA((count,))] * 2
    outs = [((micro, rows, LANES), F32), (small.shape, F32), ((shard, LANES), F32)]
    outs += [(b, BF16) for b in blocks]
    return pl.pallas_call(
        functools.partial(attend_back_reduce_kernel, dp_size, table_size),
        grid=(micro, HEADS),
        in_specs=back_specs((p, linv), (k, v, q, gmix, mixed), varied, fixed)
        + [far] * 3
        + [const_spec(small.shape)],
        out_specs=[const_spec(shape) for shape, _ in outs],
        out_shape=[jax.ShapeDtypeStruct(shape, dtype) for shape, dtype in outs],
        scratch_shapes=scratch,
        compiler_params=vmem(60, collective_id=1, has_side_effects=True),
        name="attend_backward_reduce",
    )(p, linv, k, v, q, gmix, mixed, *varied, *fixed, *grads, small)


def finish_kernel(feat, shard, mask_ref, ig_in, small_in, embed_in, *refs):
    ins, outs = refs[:7], refs[7:]
    ig_out, dwe, dwq, dwk, dwv, dwo, dwu, dwd = outs[:8]
    vecs, bu = outs[8:14], outs[14]
    for m in range(ig_in.shape[0]):
        ig_out[m] = ig_in[m].T[:feat, :] * mask_ref[m].astype(F32)
    dwe[...] = embed_in[:, :feat]
    for src, dst in zip(ins[:3], (dwo, dwu, dwd)):
        dst[...] = src[...].astype(F32)
    for g in range(HEADS // 2):
        one, two = ins[3 + 2 * g], ins[4 + 2 * g]
        at = 2 * g * HEAD_DIM
        dwq[:, at : at + 2 * HEAD_DIM] = one[:, : 2 * HEAD_DIM].astype(F32)
        dwk[:, at : at + HEAD_DIM] = one[:, 2 * HEAD_DIM :].astype(F32)
        dwk[:, at + HEAD_DIM : at + 2 * HEAD_DIM] = two[:, :HEAD_DIM].astype(F32)
        dwv[:, at : at + 2 * HEAD_DIM] = two[:, HEAD_DIM:].astype(F32)
    small = small_in[...]
    width = small.shape[1]
    dp = lax.axis_index("dp")
    turned = pltpu.roll(small, lax.rem(width - dp * shard, width), 1)
    for i, out in enumerate(vecs):
        out[...] = turned[i : i + 1, :shard]
    per_row = width // bu.shape[1]
    rows = small[8 : 8 + 4, :]
    row = dp // per_row
    pick = lax.broadcasted_iota(jnp.int32, rows.shape, 0) == row
    line = jnp.sum(jnp.where(pick, rows, 0.0), axis=0, keepdims=True)
    at = (dp % per_row) * bu.shape[1]
    bu[...] = pltpu.roll(jnp.broadcast_to(line, (8, width)), lax.rem(width - at, width), 1)[:1, : bu.shape[1]]


def finish(feat, ff_shard, mask, ig, small, embed, totals):
    micro, rows, _ = ig.shape
    shard = embed.shape[0]
    width = small.shape[1]
    out_shape = (
        [jax.ShapeDtypeStruct((micro, feat, rows), F32), jax.ShapeDtypeStruct((shard, feat), F32)]
        + [jax.ShapeDtypeStruct((shard, width), F32)] * 3
        + [jax.ShapeDtypeStruct(t.shape, F32) for t in totals[:3]]
        + [jax.ShapeDtypeStruct((1, shard), F32)] * 6
        + [jax.ShapeDtypeStruct((1, ff_shard), F32)]
    )
    return pl.pallas_call(
        functools.partial(finish_kernel, feat, shard),
        out_shape=out_shape,
        compiler_params=vmem(60),
        name="finish",
    )(mask, ig, small, embed, *totals)


def body(
    dp_size, table_size, features, feature_mask, support_count, embed_weight, embed_bias, gain_first, shift_first,
    query_weight, key_weight, value_weight, out_weight, gain_second, shift_second, up_weight, up_bias,
    down_weight, down_bias, cotangent,
):
    micro, _, rows, feat = features.shape
    shard, width = query_weight.shape
    hidden_units = up_weight.shape[1]
    ff_shard = up_bias.shape[0]
    features, cotangent, support = features[:, 0], cotangent[:, 0], support_count[:, 0]
    vectors = (embed_bias, gain_first, shift_first, gain_second, shift_second, down_bias)
    if 2 * shard == LANES and micro == 3 and table_size == 4:
        got = attend_forward_gather(
            dp_size, table_size, support, features.transpose(0, 2, 1), feature_mask, embed_weight.T,
            [a[None] for a in vectors], up_bias.reshape(-1, LANES),
            query_weight, key_weight, value_weight, out_weight, up_weight, down_weight,
        )
        q, k, v, n, u, inv, emb, mixed, p, linv, x = got[:11]
        wet, wq, wk, wv = (g.reshape(-1, g.shape[-1]) for g in got[11:15])
        vec, bu = got[15:17]
        wo, wu, wd = (g.reshape(-1, g.shape[-1]) for g in got[17:])
        activations, ghid, gmix, dwo, dwu, dwd, small = mlp_both(mixed, emb, cotangent, wo, wu, wd, vec, bu)
        grads = [g.reshape(dp_size, table_size, -1, g.shape[1]) for g in (dwo, dwu, dwd)]
        ig, small, embed, *totals = attend_backward_reduce(
            dp_size, table_size, grads, small, p, linv, k, v, q, gmix, mixed, n, u, inv, x, ghid,
            wet, vec, wq, wk, wv,
        )
        totals = [t.reshape(-1, t.shape[-1]) for t in totals]
        out = finish(feat, ff_shard, feature_mask.reshape(micro, feat, 1), ig, small, embed, totals)
        ig, dwe, dwq, dwk, dwv, dwo, dwu, dwd = out[:8]
        ig, dwe = ig.transpose(0, 2, 1), dwe.T
        smalls = [o.reshape(-1) for o in out[8:14]]
        dbu = out[14].reshape(-1)
    else:
        smalls = jnp.stack(vectors)
        mask = jnp.pad(feature_mask[:, 0], ((0, 0), (0, LANES - feat)))[:, None, :]
        x = jnp.pad(features, ((0, 0), (0, 0), (0, LANES - feat))) * mask.astype(BF16)
        wet = jnp.pad(embed_weight, ((0, LANES - feat), (0, 0))).T
        shards = [wet, query_weight, key_weight, value_weight, out_weight, up_weight, down_weight]
        wet, wq, wk, wv, wo, wu, wd = (lax.all_gather(s, "dp", axis=0, tiled=True) for s in shards)
        vec = jnp.pad(lax.all_gather(smalls, "dp", axis=1, tiled=True).astype(F32), ((0, 2), (0, 0)))
        bu = lax.all_gather(up_bias, "dp", axis=0, tiled=True).astype(F32)[None]
        x = lax.all_gather(x, "table", axis=1, tiled=True)
        q, k, v, n, u, inv, emb, mixed, p, linv = attend_forward(support, x, wet, vec, wq, wk, wv, rows)
        activations, ghid, gmix, dwo, dwu, dwd, small = mlp_both(mixed, emb, cotangent, wo, wu, wd, vec, bu)
        ig, dwe, dwq, dwk, dwv, dvec = attend_backward(
            p, linv, k, v, q, gmix, mixed, n, u, inv, x, ghid, wet, vec, wq, wk, wv
        )
        big = [dwe, dwq, dwk, dwv, dwo, dwu, dwd]
        own = [lax.psum_scatter(g.astype(F32), "dp", scatter_dimension=0, tiled=True) for g in big]
        dwe, dwq, dwk, dwv, dwo, dwu, dwd = (lax.psum(g, "table") for g in own)
        dwe = dwe[:, :feat].T
        dvec = jnp.concatenate([dvec[:3], small[3:6]])
        smalls = lax.psum(lax.psum_scatter(dvec, "dp", scatter_dimension=1, tiled=True), "table")
        dbu = small[8:].reshape(-1)[:hidden_units]
        dbu = lax.psum(lax.psum_scatter(dbu, "dp", scatter_dimension=0, tiled=True), "table")
        ig = lax.psum_scatter(ig.astype(F32) * mask, "table", scatter_dimension=1, tiled=True)[:, :, :feat]
    return (
        activations[:, None], ig[:, None], dwe, smalls[0], smalls[1], smalls[2],
        dwq, dwk, dwv, dwo, smalls[3], smalls[4], dwu, dbu, dwd, smalls[5],
    )


def solution(mesh):
    rows, cols, vecs = P("dp", None), P(None, "dp"), P("dp")
    table = P(None, "dp", "table", None)
    return jax.shard_map(
        functools.partial(body, mesh.shape["dp"], mesh.shape["table"]),
        mesh=mesh,
        in_specs=(
            table, P(None, "dp", None), cols, cols, vecs, vecs, vecs, rows, rows, rows, rows,
            vecs, vecs, rows, vecs, rows, vecs, table,
        ),
        out_specs=(
            table, table, cols, vecs, vecs, vecs, rows, rows, rows, rows, vecs, vecs, rows, vecs, rows, vecs,
        ),
        check_vma=False,
    )
```

time: 257 us -> 212 us (0.82)
  Pallas kernels: 235 us -> 208 us
  local copies, waits for them, and re-layouts: 19.4 us -> 3.36 us
    pallas_call x1, Pallas kernels: 125 us -> 101 us  [attend_backward_reduce(): pl.pallas_call(functools.partial(attend_back_reduce_kernel, dp_size, tabl...]
    unnamed x36 -> x3, local copies, waits for them, and re-layouts: 18.1 us -> 2.54 us
    pallas_call x1, Pallas kernels: 74.1 us -> 70 us  [attend_forward_gather(): pl.pallas_call(functools.partial(attend_gather_kernel, dp_size, table_siz...]
where the time goes in v2:
time: 212 us
  Pallas kernels  208 us (98%)
  local copies, waits for them, and re-layouts  3.36 us (2%)
    pallas_call x1, Pallas kernels, attend_backward_reduce(): pl.pallas_call(functools.partial(attend_back_reduce_kernel, dp_size, tabl...  101 us
    pallas_call x1, Pallas kernels, attend_forward_gather(): pl.pallas_call(functools.partial(attend_gather_kernel, dp_size, table_siz...  70 us
    pallas_call x1, Pallas kernels, mlp_both(): pl.pallas_call(mlp_kernel, grid=(micro,), in_specs=[micro_spec((rows, wid...  34.4 us

profile of v2, /device:TPU:0, one launch (start us, length us, event | category | flops | bytes accessed | tf_op | source)
XLA Modules:
  0.0 212.2 jit_solution(17518916629441298434)
XLA Ops:
  0.7 70.0 %attend_forward_gather.1 = (bf16[3,512,512]{2,1,0:T(8,128)(2,1)}, bf16[3,2048,512]{2,1,0:T(8,128)(2,1)}, bf16[3,2048,512]{2,1,0:T(8,128)(2,1)}, bf16[3,2048,512]...) custom-call(s32[3]{0:T(128)} %bitcast.67, ...), custom_call_target="tpu_custom_call" | custom-call | tf_op jit(solution)/shard_map/attend_forward_gather/pallas_call | solution.py:689
  70.7 34.4 %mlp_both.1 = (bf16[3,512,512]{2,1,0:T(8,128)(2,1)}, f32[3,512,512]{2,1,0:T(8,128)}, bf16[3,512,512]{2,1,0:T(8,128)(2,1)}, bf16[512,512]{1,0:T(8,128)(2,1)}, bf1...) custom-call(f32[3,512,512]{2,1,0:T(8,128)} %get-tuple-element.68.mixed_ref.refs_6_, ...), custom_call_target="tpu_custom_call" | custom-call | tf_op jit(solution)/shard_map/mlp_both/pallas_call | solution.py:819
  105.0 0.0 copy-start
  105.0 100.7 %attend_backward_reduce.1 = (f32[3,512,128]{2,1,0:T(8,128)}, f32[16,512]{1,0:T(8,128)}, f32[64,128]{1,0:T(8,128)}, bf16[4,16,512]{2,1,0:T(8,128)(2,1)}, bf16[4,1...) custom-call(bf16[3,4,512,2048]{3,2,1,0:T(8,128)(2,1)} %get-tuple-ele, ...), custom_call_target="tpu_custom_call" | custom-call | tf_op jit(solution)/shard_map/attend_backward_reduce/pallas_call | solution.py:1248
  205.8 0.0 copy-done
  205.8 0.8 copy.36.mask_ref
  206.6 3.1 %finish.1 = (f32[3,100,512]{2,1,0:T(8,128)}, f32[64,100]{1,0:T(8,128)}, f32[64,512]{1,0:T(8,128)}, f32[64,512]{1,0:T(8,128)}, f32[64,512]{1,0:T(8,128)}, /*index...) custom-call(s32[3,100,1]{2,1,0:T(8,128)} %copy.36.mask_ref, ...), custom_call_target="tpu_custom_call" | custom-call | tf_op jit(solution)/shard_map/finish/pallas_call | solution.py:1304
  209.7 2.5 %copy.38 = f32[3,1,512,100]{2,1,3,0:T(1,128)} copy(f32[3,1,512,100]{2,3,0,1:T(8,128)} %bitcast.50) | data formatting | bytes 1228800
Async XLA Ops:
  105.0 100.7 %copy-start = (s32[3,1,100]{2,1,0:T(1,128)S(1)}, s32[3,1,100]{2,1,0:T(1,128)}, u32[]{:S(2)}) copy-start(s32[3,1,100]{2,1,0:T(1,128)} %mask_ref.1) | copy-start | bytes 3604

commit v3 on v2

v3 whole, which is shorter than its diff:
```python
import functools

import jax
import jax.numpy as jnp
from jax import lax
from jax.experimental import pallas as pl
from jax.experimental.pallas import tpu as pltpu
from jax.sharding import PartitionSpec as P

HEADS = 4
HEAD_DIM = 128
LANES = 128
EPSILON = 1e-5
SCALE = HEAD_DIM**-0.5
LOG2E = 1.4426950408889634
ROW_BLOCK = 256
KEY_BLOCK = 512
BACK_BLOCK = 256
GROUPS = 4
NORM_BLOCK = 256
HEADS_STEP = 2
PAIRS = HEADS // HEADS_STEP
CHUNKS = 4
TABLE_STEPS = 3
INV_SQRT_TWO = 0.7071067811865476
INV_SQRT_TWO_PI = 0.3989422804014327
BF16 = jnp.bfloat16
F32 = jnp.float32
MESH = pl.DeviceIdType.MESH


def dot_nn(a, b):
    return lax.dot_general(a, b, (((1,), (0,)), ((), ())), preferred_element_type=F32)


def dot_nt(a, b):
    return lax.dot_general(a, b, (((1,), (1,)), ((), ())), preferred_element_type=F32)


def dot_tn(a, b):
    return lax.dot_general(a, b, (((0,), (0,)), ((), ())), preferred_element_type=F32)


def norm_parts(v):
    mean = jnp.mean(v, axis=-1, keepdims=True)
    centred = v - mean
    inv = lax.rsqrt(jnp.mean(centred * centred, axis=-1, keepdims=True) + EPSILON)
    return centred * inv, inv


def norm_back(grad, unit, inv, gain):
    q = grad * gain
    return inv * (
        q
        - jnp.mean(q, axis=-1, keepdims=True)
        - unit * jnp.mean(q * unit, axis=-1, keepdims=True)
    )


def row_sum(v):
    return jnp.sum(v, axis=0, keepdims=True)


def const_spec(shape):
    return pl.BlockSpec(shape, lambda *g: (0,) * len(shape))


def micro_spec(shape):
    return pl.BlockSpec((1,) + shape, lambda m, *g: (m,) + (0,) * len(shape))


def head_spec(shape):
    return pl.BlockSpec((1, 1) + shape, lambda m, h: (m, h) + (0,) * len(shape))


def heads_spec(shape):
    return pl.BlockSpec((1, HEADS_STEP) + shape, lambda m, h: (m, h) + (0,) * len(shape))


def head_cols_spec(rows):
    return pl.BlockSpec((1, rows, HEAD_DIM), lambda m, h: (m, 0, h))


def vmem(mib, **extra):
    return pltpu.CompilerParams(vmem_limit_bytes=mib * 2**20, **extra)


def toggled(index, hop):
    return index + hop * (1 - 2 * ((index // hop) % 2))


def toggled_by(index, hops):
    for hop in hops:
        index = toggled(index, hop)
    return index


def subsets(hops):
    out = [()]
    for hop in hops:
        out = out + [s + (hop,) for s in out]
    return out


def hops_of(size):
    return [1 << i for i in range(size.bit_length() - 1)]


class Place:
    def __init__(self, dp_size, table_size):
        self.size = {"dp": dp_size, "table": table_size}
        self.hops = {axis: hops_of(n) for axis, n in self.size.items()}
        self.me = {"dp": lax.axis_index("dp"), "table": lax.axis_index("table")}

    def partner(self, axis, hop):
        there = dict(self.me)
        there[axis] = toggled(there[axis], hop)
        return (there["dp"], there["table"])

    def at(self, axis, shift):
        n = self.size[axis]
        return lax.rem(self.me[axis] + (shift + n), n)

    def ahead(self, axis, shift):
        there = dict(self.me)
        there[axis] = self.at(axis, shift)
        return (there["dp"], there["table"])

    def greet(self, all_dp):
        barrier = pltpu.get_barrier_semaphore()
        peers = [self.ahead("table", s) for s in range(1, self.size["table"])]
        if all_dp:
            peers += [self.ahead("dp", s) for s in range(1, self.size["dp"])]
        else:
            peers += [self.partner("dp", hop) for hop in self.hops["dp"]]
        for peer in peers:
            pl.semaphore_signal(barrier, inc=1, device_id=peer, device_id_type=MESH)
        return lambda: pl.semaphore_wait(barrier, len(peers))


class Swap:
    def __init__(self, place, axis, sems, base, send, put):
        self.place, self.axis, self.sems, self.base = place, axis, sems, base
        self.send, self.put = send, put
        self.shifts = range(1, place.size[axis])

    def copy(self, shift, src, dst):
        index = self.base + shift - 1
        return pltpu.make_async_remote_copy(
            src_ref=src, dst_ref=dst, send_sem=self.sems[0].at[index], recv_sem=self.sems[1].at[index],
            device_id=self.place.ahead(self.axis, shift), device_id_type=MESH,
        )

    def start_one(self, shift):
        to = self.place.at(self.axis, shift)
        self.copy(shift, self.send(to), self.put(self.place.me[self.axis], shift)).start()

    def start(self):
        for shift in self.shifts:
            self.start_one(shift)

    def arrive_one(self, shift):
        here = self.put(self.place.at(self.axis, -shift), shift)
        self.copy(shift, here, here).wait_recv()
        return here

    def arrive(self):
        return [self.arrive_one(shift) for shift in self.shifts]

    def sent(self):
        for shift in self.shifts:
            out = self.send(self.place.at(self.axis, shift))
            self.copy(shift, out, out).wait_send()


def remote(place, axis, hop, src, dst, sems, index):
    return pltpu.make_async_remote_copy(
        src_ref=src, dst_ref=dst, send_sem=sems[0].at[index], recv_sem=sems[1].at[index],
        device_id=place.partner(axis, hop), device_id_type=MESH,
    )


class Gather:
    def __init__(self, place, axis, hops, full, sems, base, own=None):
        self.place, self.axis, self.hops = place, axis, hops
        self.full, self.sems, self.base, self.own = full, sems, base, own
        self.steps = len(hops)

    def whole(self, step):
        part = self.full.at[pl.ds(0, 1 << step)]
        return remote(self.place, self.axis, self.hops[step], part, part, self.sems, self.base + step)

    def start(self, step):
        for s in subsets(self.hops[:step]):
            block = self.full.at[toggled_by(self.place.me[self.axis], s)]
            src = block if s or self.own is None else self.own
            remote(
                self.place, self.axis, self.hops[step], src, block, self.sems, self.base + step
            ).start()

    def arrive(self, step):
        self.whole(step).wait_recv()

    def sent(self):
        for step in range(self.steps):
            self.whole(step).wait_send()


def add_into(into, other):
    into[...] = (into[...].astype(F32) + other[...].astype(F32)).astype(into.dtype)


class Reduce:
    def __init__(self, place, axis, hops, blocks, bufs, sems, base):
        self.place, self.axis, self.hops = place, axis, hops
        self.held = blocks
        self.bufs, self.sems, self.base = bufs, sems, base
        self.steps = len(hops)

    def mine(self, step, s):
        if step == 0:
            return self.held(s)
        order = [set(t) for t in subsets(self.hops[step:])]
        return self.bufs[step - 1].at[order.index(set(s))]

    def copy(self, step, src, dst):
        return remote(self.place, self.axis, self.hops[step], src, dst, self.sems, self.base + step)

    def start(self, step):
        for i, s in enumerate(subsets(self.hops[step + 1 :])):
            self.copy(step, self.mine(step, s + (self.hops[step],)), self.bufs[step].at[i]).start()

    def arrive(self, step):
        self.copy(step, self.bufs[step], self.bufs[step]).wait_recv()
        for i, s in enumerate(subsets(self.hops[step + 1 :])):
            add_into(self.bufs[step].at[i], self.mine(step, s))

    def total(self):
        return self.bufs[-1].at[0]

    def sent_one(self, step):
        self.copy(step, self.bufs[step], self.bufs[step]).wait_send()


class QuickShard:
    def __init__(self, place, dp_hops, blocks, scratch, sems, base, back_only=False):
        n = len(dp_hops)
        self.place, self.full, self.blocks = place, scratch[-1], blocks
        got = None if back_only else scratch[n]
        self.dp = Reduce(place, "dp", dp_hops, blocks, scratch[:n], sems, base)
        base += n
        self.out = self.back = None
        if not back_only:
            self.out = Swap(
                place, "table", sems, base, lambda t: self.dp_total().at[t], lambda t, s: got.at[s - 1]
            )
            base += place.size["table"] - 1
        self.back = Swap(
            place, "table", sems, base, lambda t: self.full.at[place.me["table"]], lambda t, s: self.full.at[t]
        )
        self.stages = [(self.dp, i) for i in range(n)] + ([] if back_only else [(self.out, 0)]) + [(self.back, 0)]
        self.steps = len(self.stages)
        self.done = 0

    def dp_total(self):
        return self.dp.total() if self.dp.steps else self.blocks(())

    def start(self, step):
        flow, i = self.stages[step]
        self.done = max(self.done, step + 1)
        if flow is self.dp:
            flow.start(i)
            return
        if flow is self.back and self.out is None:
            self.full[self.place.me["table"]] = self.blocks(())[...]
        flow.start()

    def arrive(self, step):
        flow, i = self.stages[step]
        if flow is self.dp:
            flow.arrive(i)
        elif flow is self.out:
            me = self.place.me["table"]
            total = self.dp_total()[me].astype(F32)
            for got in flow.arrive():
                total = total + got[...].astype(F32)
            self.full[me] = total.astype(self.full.dtype)
        else:
            flow.arrive()

    def sent(self):
        for flow, i in self.stages[: self.done]:
            if flow is self.dp:
                flow.sent_one(i)
            else:
                flow.sent()


def quick_scratch(dp_hops, table_size, block, dtype, back_only=False):
    out = [pltpu.VMEM((1 << (dp_hops - 1 - i),) + block, dtype) for i in range(dp_hops)]
    if not back_only:
        out.append(pltpu.VMEM((table_size - 1,) + block[1:], dtype))
    return out + [pltpu.VMEM(block, dtype)]


def quick_sems(dp_hops, table_size, back_only=False):
    return dp_hops + (1 if back_only else 2) * (table_size - 1)


class Small:
    def __init__(self, place, block, got_dp, part, got_table, sems, base):
        self.place, self.block, self.part = place, block, part
        self.first = Swap(place, "dp", sems, base, block, lambda t, s: got_dp.at[s - 1])
        base += place.size["dp"] - 1
        self.second = Swap(
            place, "table", sems, base, lambda t: part, lambda t, s: got_table.at[s - 1]
        )
        self.steps = 2

    def start(self, step):
        (self.first, self.second)[step].start()

    def arrive(self, step):
        if step == 0:
            total = self.block(self.place.me["dp"])[...].astype(F32)
            for got in self.first.arrive():
                total = total + got[...].astype(F32)
            self.part[...] = total.astype(self.part.dtype)
        else:
            total = self.part[...].astype(F32)
            for got in self.second.arrive():
                total = total + got[...].astype(F32)
            self.total = total

    def sent(self):
        self.first.sent()
        self.second.sent()


def small_scratch(dp_size, table_size, block, dtype):
    return [
        pltpu.VMEM((dp_size - 1,) + block, dtype),
        pltpu.VMEM(block, dtype),
        pltpu.VMEM((table_size - 1,) + block, dtype),
    ]


def attend_core(
    support, project_all, wq, q_ref, k_ref, v_ref, n_ref, emb_ref, mixed_ref, mixed_low_ref, p_ref, linv_ref, s_bufs, get_x, wet,
):
    length, rows = n_ref.shape[1], q_ref.shape[1]
    own = lax.axis_index("table")

    @pl.when(pl.program_id(1) == 0)
    def _():
        project_all()
        here = pl.ds(pl.multiple_of(own * rows, rows), rows)
        emb_ref[0] = dot_nt(get_x(own, slice(0, rows)), wet())
        q_ref[0] = dot_nn(n_ref[0, here, :], wq()).astype(BF16)

    block = s_bufs[0].shape[0]
    sure = length - rows
    columns = sure + lax.broadcasted_iota(jnp.int32, (1, rows), 1)
    allowed = columns < support
    heads = p_ref.shape[1]
    units = [(h, i) for h in range(heads) for i in range(rows // block)]
    first_head = pl.program_id(1) * heads

    def cols_of(h):
        return pl.ds(pl.multiple_of((first_head + h) * HEAD_DIM, HEAD_DIM), HEAD_DIM)

    def score(j):
        h, i = units[j]
        q = q_ref[0, i * block : (i + 1) * block, cols_of(h)]
        s_bufs[j % 2][...] = dot_nt(q, k_ref[0, :, cols_of(h)])

    score(0)
    for j, (h, i) in enumerate(units):
        if j + 1 < len(units):
            score(j + 1)
        at = slice(i * block, (i + 1) * block)
        first = s_bufs[j % 2][:, :sure]
        last = jnp.where(allowed, s_bufs[j % 2][:, sure:], -1e30)
        top = jnp.maximum(
            jnp.max(first, axis=-1, keepdims=True), jnp.max(last, axis=-1, keepdims=True)
        )
        pf = jnp.exp2((first - top) * (SCALE * LOG2E))
        pt = jnp.exp2((last - top) * (SCALE * LOG2E))
        total = jnp.sum(pf, axis=-1, keepdims=True) + jnp.sum(pt, axis=-1, keepdims=True)
        pf, pt = pf.astype(BF16), pt.astype(BF16)
        p_ref[0, h, at, :sure] = pf
        p_ref[0, h, at, sure:] = pt
        linv = 1.0 / total
        linv_ref[0, h, at, :] = jnp.broadcast_to(linv, (block, LANES))
        out = dot_nn(pf, v_ref[0, :sure, cols_of(h)]) + dot_nn(pt, v_ref[0, sure:, cols_of(h)])
        out = out * linv
        mixed_ref[0, at, cols_of(h)] = out
        mixed_low_ref[0, at, cols_of(h)] = out.astype(BF16)


def project(blocks, rows, get_x, wet, vec_ref, wk, wv, k_ref, v_ref, n_ref, e_bufs):
    gain, shift = vec_ref[1:2, :], vec_ref[2:3, :]
    chunk = e_bufs[0].shape[0]
    units = [(b, i) for b in blocks for i in range(rows // chunk)]

    def embed(j):
        b, i = units[j]
        e_bufs[j % 2][...] = dot_nt(get_x(b, slice(i * chunk, (i + 1) * chunk)), wet())

    embed(0)
    for j, (b, i) in enumerate(units):
        if j + 1 < len(units):
            embed(j + 1)
        at = pl.ds(pl.multiple_of(b * rows + i * chunk, chunk), chunk)
        unit, _ = norm_parts(e_bufs[j % 2][...])
        normed = (unit * gain + shift).astype(BF16)
        n_ref[0, at, :] = normed
        k_ref[0, at, :] = dot_nn(normed, wk()).astype(BF16)
        v_ref[0, at, :] = dot_nn(normed, wv()).astype(BF16)


def attend_kernel(support_ref, x_ref, wet_ref, vec_ref, wq_ref, wk_ref, wv_ref, *rest):
    outs, bufs = rest[:9], rest[9:]
    q_ref, k_ref, v_ref, n_ref = outs[:4]
    rows = q_ref.shape[1]

    def get_x(block, part):
        at = pl.ds(pl.multiple_of(block * rows + part.start, NORM_BLOCK), part.stop - part.start)
        return x_ref[0, at, :]

    def project_all():
        project(
            range(x_ref.shape[1] // rows), rows, get_x, lambda: wet_ref[...], vec_ref,
            lambda: wk_ref[...], lambda: wv_ref[...], k_ref, v_ref, n_ref, bufs[:2],
        )

    attend_core(
        support_ref[pl.program_id(0)], project_all, lambda: wq_ref[...], *outs, bufs[2:], get_x, lambda: wet_ref[...]
    )


def attend_scratch(length, width):
    return [pltpu.VMEM((NORM_BLOCK, width), F32)] * 2 + [pltpu.VMEM((ROW_BLOCK, length), F32)] * 2


def attend_gather_kernel(
    dp_size, table_size, support_ref, feat_ref, mask_ref, ew_ref,
    v0_ref, v1_ref, v2_ref, v3_ref, v4_ref, v5_ref, ub_ref, wq_in, wk_in, wv_in, wo_in, wu_in, wd_in,
    q_ref, k_ref, v_ref, n_ref, emb_ref, mixed_ref, mixed_low_ref, p_ref, linv_ref,
    x_out, wet_out, wq_out, wk_out, wv_out, vec_ref, bu_ref, wo_out, wu_out, wd_out,
    x_buf, wet_buf, packed_buf, wq_buf, wk_buf, wv_buf, e_one, e_two, s_one, s_two, own_sem, send_sem, recv_sem,
):
    micro_id, head = pl.program_id(0), pl.program_id(1)
    micro, feat, rows = feat_ref.shape
    shard = wq_in.shape[0]
    width = wq_in.shape[1]
    place = Place(dp_size, table_size)
    dp, table = place.me["dp"], place.me["table"]
    sems = (send_sem, recv_sem)
    hops = place.hops["dp"]
    forth, back = hops[1:] + hops[:1], hops[:0:-1] + hops[:1]
    last = len(hops) - 1
    base = 0

    def gather(order, full, own=None):
        nonlocal base
        flow = Gather(place, "dp", order, full, sems, base, own)
        base += flow.steps
        return flow

    early = [
        gather(forth, wk_buf),
        gather(back, wv_buf),
        gather(forth, wet_buf),
        gather(back, packed_buf),
    ]
    query = gather(forth, wq_buf)
    late = [gather(forth, wo_out, wo_in), gather(forth, wu_out, wu_in), gather(back, wd_out, wd_in)]
    feats = []
    for m in range(micro):
        own_x = x_buf.at[m, table]
        feats.append(
            Swap(
                place, "table", sems, base,
                lambda t, own_x=own_x: own_x,
                lambda t, s, m=m: x_buf.at[m, t],
            )
        )
        base += table_size - 1
    own_copies = [
        pltpu.make_async_copy(src, dst.at[dp], own_sem.at[i])
        for i, (src, dst) in enumerate(((wo_in, wo_out), (wu_in, wu_out), (wd_in, wd_out)))
    ]
    out_copies = [
        pltpu.make_async_copy(src, dst, own_sem.at[3 + i])
        for i, (src, dst) in enumerate(
            ((wet_buf, wet_out), (wq_buf, wq_out), (wk_buf, wk_out), (wv_buf, wv_out))
        )
    ]

    def at_step(m, h):
        return pl.when((micro_id == m) & (head == h))

    @at_step(0, 0)
    def _():
        wait_all = place.greet(False)
        packed_buf[dp] = jnp.zeros((8, LANES), F32)
        for i, ref in enumerate((v0_ref, v1_ref, v2_ref, v3_ref, v4_ref, v5_ref)):
            packed_buf[dp, i : i + 1, :shard] = ref[...].astype(F32)
        place_of = lax.broadcasted_iota(jnp.int32, (LANES, LANES), 0) == feat
        bias = jnp.where(place_of, jnp.broadcast_to(packed_buf[dp, 0:1, :], (LANES, LANES)), 0.0)
        wet_buf[dp] = bias.T[:shard, :].astype(BF16)
        wet_buf[dp, :, :feat] = ew_ref[...]
        packed_buf[dp, 6:8, :] = ub_ref[...].astype(F32)
        wk_buf[dp] = wk_in[...]
        wv_buf[dp] = wv_in[...]
        wq_buf[dp] = wq_in[...]

        def fill(m):
            tall = jnp.concatenate(
                [feat_ref[m].astype(F32), jnp.zeros((LANES - feat, rows), F32)], axis=0
            ).T
            lane = lax.broadcasted_iota(jnp.int32, (rows, LANES), 1)
            x_buf[m, table] = jnp.where(lane == feat, 1.0, 0.0).astype(BF16)
            x_buf[m, table, :, :feat] = (tall[:, :feat] * mask_ref[m].astype(F32)).astype(BF16)

        fill(0)
        wait_all()
        for flow in early:
            flow.start(0)
        feats[0].start()
        for copy in own_copies:
            copy.start()
        for m in range(1, micro):
            fill(m)
        for step in range(last):
            for flow in early:
                flow.arrive(step)
                flow.start(step + 1)
            if step == 0:
                query.start(0)
            else:
                query.arrive(step - 1)
                query.start(step)
        for flow in early:
            flow.arrive(last)
        for flow in late:
            flow.start(0)
        lane = lax.broadcasted_iota(jnp.int32, (8, LANES), 1)
        for d in range(0, dp_size, 2):
            pair = jnp.where(lane < shard, packed_buf[d], pltpu.roll(packed_buf[d + 1], shard, 1))
            vec_ref[:, d * shard : (d + 2) * shard] = pair
        for d in range(dp_size):
            bu_ref[:, 2 * d * LANES : (2 * d + 1) * LANES] = packed_buf[d, 6:7, :]
            bu_ref[:, (2 * d + 1) * LANES : (2 * d + 2) * LANES] = packed_buf[d, 7:8, :]

    @at_step(0, 1)
    def _():
        for flow in late:
            flow.arrive(0)
            flow.start(1)
        for copy in out_copies:
            copy.start()

    @at_step(1, 0)
    def _():
        feats[1].arrive()
        feats[2].start()

    @at_step(2, 0)
    def _():
        feats[2].arrive()
        for flow in late:
            flow.arrive(1)
            flow.start(2)

    def get_x(block, part):
        return x_buf[micro_id, block, part, :]

    shifts = sorted(range(1, table_size), key=lambda s: (min(s, table_size - s), s))

    def full(buf):
        return lambda: buf[...].reshape(-1, buf.shape[-1])

    def some(blocks):
        project(
            blocks, rows, get_x, full(wet_buf), vec_ref, full(wk_buf), full(wv_buf), k_ref, v_ref, n_ref, (e_one, e_two)
        )

    def project_all():
        @pl.when(micro_id == 0)
        def _():
            query.arrive(last - 1)
            query.start(last)
            for shift in shifts:
                feats[0].arrive_one(shift)
            feats[1].start()
            query.arrive(last)

        some([place.at("table", shift) for shift in range(table_size)])

        x_out[0] = x_buf[micro_id].reshape(x_out.shape[1:])

    attend_core(
        support_ref[micro_id], project_all, full(wq_buf),
        q_ref, k_ref, v_ref, n_ref, emb_ref, mixed_ref, mixed_low_ref, p_ref, linv_ref, (s_one, s_two), get_x, full(wet_buf),
    )

    @at_step(micro - 1, HEADS // HEADS_STEP - 1)
    def _():
        for flow in late:
            flow.arrive(2)
        for flow in feats + early + [query] + late:
            flow.sent()
        for copy in own_copies + out_copies:
            copy.wait()


def attend_shapes(rows, length, width):
    out = [
        ((rows, width), BF16),
        ((length, width), BF16),
        ((length, width), BF16),
        ((length, width), BF16),
        ((rows, width), F32),
        ((rows, width), F32),
        ((rows, width), BF16),
    ]
    return out, [((rows, length), BF16), ((rows, LANES), F32)]


def attend_forward_gather(dp_size, table_size, support, feat, mask, ew, vecs, ub, wq, wk, wv, wo, wu, wd):
    micro, _, rows = feat.shape
    length = rows * table_size
    width = wq.shape[1]
    out, heads = attend_shapes(rows, length, width)
    whole = pl.BlockSpec(memory_space=pltpu.VMEM)
    far = pl.BlockSpec(memory_space=pl.ANY)

    def gathered(a):
        return jax.ShapeDtypeStruct((dp_size,) + a.shape, a.dtype)

    wet = jax.ShapeDtypeStruct((dp_size, wq.shape[0], LANES), BF16)
    count = micro * (table_size - 1) + 8 * len(hops_of(dp_size))
    return pl.pallas_call(
        functools.partial(attend_gather_kernel, dp_size, table_size),
        grid=(micro, HEADS // HEADS_STEP),
        in_specs=[pl.BlockSpec(memory_space=pltpu.SMEM)] + [whole] * 13 + [far] * 3,
        out_specs=[micro_spec(s) for s, _ in out]
        + [heads_spec(s) for s, _ in heads]
        + [micro_spec((length, LANES))]
        + [far] * 4
        + [const_spec((8, width)), const_spec((1, wu.shape[1]))]
        + [far] * 3,
        out_shape=[jax.ShapeDtypeStruct((micro,) + s, d) for s, d in out]
        + [jax.ShapeDtypeStruct((micro, HEADS) + s, d) for s, d in heads]
        + [jax.ShapeDtypeStruct((micro, length, LANES), BF16)]
        + [wet, gathered(wq), gathered(wk), gathered(wv)]
        + [jax.ShapeDtypeStruct((8, width), F32), jax.ShapeDtypeStruct((1, wu.shape[1]), F32)]
        + [gathered(wo), gathered(wu), gathered(wd)],
        scratch_shapes=[
            pltpu.VMEM((micro, table_size, rows, LANES), BF16),
            pltpu.VMEM(wet.shape, BF16),
            pltpu.VMEM((dp_size, 8, LANES), F32),
            pltpu.VMEM((dp_size,) + wq.shape, BF16),
            pltpu.VMEM((dp_size,) + wk.shape, BF16),
            pltpu.VMEM((dp_size,) + wv.shape, BF16),
            *attend_scratch(length, width),
            pltpu.SemaphoreType.DMA((7,)),
            pltpu.SemaphoreType.DMA((count,)),
            pltpu.SemaphoreType.DMA((count,)),
        ],
        compiler_params=vmem(60, collective_id=0, has_side_effects=True),
        name="attend_forward_gather",
    )(support, feat, mask, ew, *vecs, ub, wq, wk, wv, wo, wu, wd)


def attend_forward(support, x_all, wet, vec, wq, wk, wv, rows):
    micro, length, lanes = x_all.shape
    width = wq.shape[0]
    out, heads = attend_shapes(rows, length, width)
    return pl.pallas_call(
        attend_kernel,
        grid=(micro, HEADS // HEADS_STEP),
        in_specs=[
            pl.BlockSpec(memory_space=pltpu.SMEM),
            micro_spec((length, lanes)),
            const_spec(wet.shape),
            const_spec(vec.shape),
            const_spec(wq.shape),
            const_spec(wk.shape),
            const_spec(wv.shape),
        ],
        out_specs=[micro_spec(s) for s, _ in out] + [heads_spec(s) for s, _ in heads],
        out_shape=[jax.ShapeDtypeStruct((micro,) + s, d) for s, d in out]
        + [jax.ShapeDtypeStruct((micro, HEADS) + s, d) for s, d in heads],
        scratch_shapes=attend_scratch(length, width),
        compiler_params=vmem(58),
        name="attend_forward",
    )(support, x_all, wet, vec, wq, wk, wv)


def mlp_kernel(
    mixed_ref, emb_ref, cot_ref, wo_ref, wu_ref, wd_ref, vec_ref, bu_ref,
    act_ref, ghid_ref, gmix_ref, dwo_ref, dwu_ref, dwd_ref, dvec_ref,
    acc_o, acc_u, acc_d, gn2_ref, out_ref, *bufs,
):
    step, last = pl.program_id(0), pl.num_programs(0) - 1
    hidden_units = wu_ref.shape[1]
    chunk = 512

    @pl.when(step == 0)
    def _():
        acc_o[...] = jnp.zeros_like(acc_o)
        acc_u[...] = jnp.zeros_like(acc_u)
        acc_d[...] = jnp.zeros_like(acc_d)
        dvec_ref[...] = jnp.zeros_like(dvec_ref)

    gain, shift, dbias = vec_ref[3:4, :], vec_ref[4:5, :], vec_ref[5:6, :]
    mixed = mixed_ref[0]
    g_out = cot_ref[0]
    hidden = emb_ref[0] + dot_nn(mixed, wo_ref[...])
    unit, inv = norm_parts(hidden)
    normed = (unit * gain + shift).astype(BF16)
    out_ref[...] = hidden + dbias
    normed_t = normed.T
    g_out_t = g_out.T
    chunks = hidden_units // chunk

    def products(f):
        cols = slice(f * chunk, (f + 1) * chunk)
        bufs[2 * (f % 2)][...] = dot_nn(normed, wu_ref[:, cols])
        bufs[2 * (f % 2) + 1][...] = dot_nt(g_out, wd_ref[cols, :])

    products(0)
    for f in range(chunks):
        if f + 1 < chunks:
            products(f + 1)
        cols = slice(f * chunk, (f + 1) * chunk)
        pre = bufs[2 * (f % 2)][...] + bu_ref[:, cols]
        g_act = bufs[2 * (f % 2) + 1][...]
        cdf = 0.5 * (1.0 + lax.erf(pre * INV_SQRT_TWO))
        pdf = jnp.exp(-0.5 * pre * pre) * INV_SQRT_TWO_PI
        act = (pre * cdf).astype(BF16)
        out_ref[...] += dot_nn(act, wd_ref[cols, :])
        acc_d[:, cols] += dot_nn(g_out_t, act)
        g_pre_f = g_act * (cdf + pre * pdf)
        g_pre = g_pre_f.astype(BF16)
        acc_u[:, cols] += dot_nn(normed_t, g_pre)
        dvec_ref[8 + f : 9 + f, :] += row_sum(g_pre_f)
        g_part = dot_nt(g_pre, wu_ref[:, cols])
        if f == 0:
            gn2_ref[...] = g_part
        else:
            gn2_ref[...] += g_part
    act_ref[0] = out_ref[...].astype(BF16)
    g_norm = gn2_ref[...]
    g_out_f = g_out.astype(F32)
    dvec_ref[3:4, :] += row_sum(g_norm * unit)
    dvec_ref[4:5, :] += row_sum(g_norm)
    dvec_ref[5:6, :] += row_sum(g_out_f)
    g_hidden = g_out_f + norm_back(g_norm, unit, inv, gain)
    ghid_ref[0] = g_hidden
    branch = g_hidden.astype(BF16)
    acc_o[...] += dot_tn(mixed, branch)
    gmix_ref[0] = dot_nt(branch, wo_ref[...]).astype(BF16)

    @pl.when(step == last)
    def _():
        dwo_ref[...] = acc_o[...].astype(BF16)
        dwu_ref[...] = acc_u[...].astype(BF16)
        for f in range(hidden_units // chunk):
            cols = slice(f * chunk, (f + 1) * chunk)
            dwd_ref[cols, :] = acc_d[:, cols].T.astype(BF16)


def mlp_both(mixed, emb, cot, wo, wu, wd, vec, bu):
    micro, rows, width = mixed.shape
    hidden_units = wu.shape[1]
    per_micro = [((rows, width), BF16), ((rows, width), F32), ((rows, width), BF16)]
    summed = [
        ((width, width), BF16),
        ((width, hidden_units), BF16),
        ((hidden_units, width), BF16),
        ((16, width), F32),
    ]
    return pl.pallas_call(
        mlp_kernel,
        grid=(micro,),
        in_specs=[micro_spec((rows, width))] * 3
        + [const_spec(a.shape) for a in (wo, wu, wd, vec, bu)],
        out_specs=[micro_spec(s) for s, _ in per_micro] + [const_spec(s) for s, _ in summed],
        out_shape=[jax.ShapeDtypeStruct((micro,) + s, d) for s, d in per_micro]
        + [jax.ShapeDtypeStruct(s, d) for s, d in summed],
        scratch_shapes=[
            pltpu.VMEM((width, width), F32),
            pltpu.VMEM((width, hidden_units), F32),
            pltpu.VMEM((width, hidden_units), F32),
            pltpu.VMEM((rows, width), F32),
            pltpu.VMEM((rows, width), F32),
        ]
        + [pltpu.VMEM((rows, 512), F32)] * 4,
        compiler_params=vmem(60),
        name="mlp_both",
    )(mixed, emb, cot, wo, wu, wd, vec, bu)


def halves(lane, shift, low, high):
    half = LANES // 2
    return jnp.where(lane < half, pltpu.roll(low, shift, 1), pltpu.roll(high, half - shift, 1))


def mlp_reduce_kernel(dp_size, table_size, *refs):
    refs = list(refs)

    def take(n):
        out = refs[:n]
        del refs[:n]
        return out

    mixed_in, emb_in, cot_in, wo_in, wu_in, wd_in, vec_ref, bu_ref = take(8)
    act_out, ghid_out, gmix_out, dwo_out, small_out = take(5)
    part_outs = [take(2) for _ in range(CHUNKS)]
    mixed_s, emb_s, cot_s, wo_s, wu_s, wd_s = take(6)
    normed_s, normed_t, g_out_t, unit_s, out_s, gn2_s = take(6)
    act_s, gmix_s, ghid_s = normed_s, normed_t, emb_s
    wu_c, wd_c, acc_u, acc_d, acc_o, inv_s = take(6)
    pre_b, gact_b = take(2), take(2)
    grads = [take(2) for _ in range(CHUNKS)]
    hops = len(hops_of(dp_size))
    scratch = [[take(hops + 2) for _ in range(2)] for _ in range(CHUNKS)]
    in_sem, out_sem, send_sem, recv_sem = refs
    micro, rows, width = mixed_s.shape
    hidden_units = wu_s.shape[-1]
    place = Place(dp_size, table_size)
    chunk, last = pl.program_id(0), CHUNKS - 1
    forth, back = place.hops["dp"], place.hops["dp"][:1] + place.hops["dp"][:0:-1]
    flows = []
    base = 0
    for f in range(CHUNKS):
        pair = []
        for grad, order, scr in zip(grads[f], (forth, back), scratch[f]):
            pair.append(
                QuickShard(
                    place, order, lambda s, grad=grad: grad.at[toggled_by(place.me["dp"], s)], scr,
                    (send_sem, recv_sem), base,
                )
            )
            base += quick_sems(hops, table_size)
        flows.append(pair)

    names = []
    for m in range(micro):
        names += [(mixed_in.at[m], mixed_s.at[m])] + [(wo_in, wo_s)] * (m == 0)
        names += [(emb_in.at[m], emb_s.at[m]), (cot_in.at[m], cot_s.at[m])]
        names += [(wu_in, wu_s), (wd_in, wd_s)] * (m == 0)
    copies = [pltpu.make_async_copy(src, dst, in_sem.at[n]) for n, (src, dst) in enumerate(names)]
    gain, shift, dbias = vec_ref[3:4, :], vec_ref[4:5, :], vec_ref[5:6, :]
    half = LANES // 2
    own = hidden_units // dp_size

    def add(ref, first, value):
        ref[...] = value if first else ref[...] + value

    upto = {0: 5, 1: 4, 2: 3, 3: 2}

    def step(f, i):
        for flow in flows[f]:
            if i:
                flow.arrive(i - 1)
            if i < upto[f]:
                flow.start(i)

    def at(c, *steps):
        @pl.when(chunk == c)
        def _():
            for f, i in steps:
                step(f, i)

    @pl.when(chunk == 0)
    def _():
        for copy in copies:
            copy.start()
        wait_all = place.greet(False)
        small_out[...] = jnp.zeros_like(small_out)
        gn2_s[...] = jnp.zeros_like(gn2_s)
        n = 0
        for m in range(micro):
            copies[n].wait()
            copies[n + 1].wait()
            n += 2
            if m == 0:
                copies[n].wait()
                n += 1
            hidden = emb_s[m] + dot_nn(mixed_s[m], wo_s[...])
            unit, inv = norm_parts(hidden)
            unit_s[m] = unit
            inv_s[m] = jnp.broadcast_to(inv, (rows, LANES))
            normed = (unit * gain + shift).astype(BF16)
            normed_s[m] = normed
            normed_t[m] = normed.T
            out_s[m] = hidden + dbias
            copies[n].wait()
            n += 1
            g_out_t[m] = cot_s[m].T
            if m == 0:
                copies[n].wait()
                copies[n + 1].wait()
                n += 2
        wait_all()

    lane = lax.broadcasted_iota(jnp.int32, (width, LANES), 1)
    line = lax.broadcasted_iota(jnp.int32, (8, LANES), 1)
    turn = lax.rem(chunk, 2) * half
    biases = []
    for o in range(0, dp_size, 2):
        tiles = [pl.ds(pl.multiple_of((q * own // LANES + chunk // 2) * LANES, LANES), LANES) for q in (o, o + 1)]
        low, high = (wu_s[:, t].astype(F32) for t in tiles)
        wu_c[:, o * half : o * half + LANES] = halves(lane, turn, low, high).astype(BF16)
        low, high = (jnp.broadcast_to(bu_ref[:, t], (8, LANES)) for t in tiles)
        biases.append(halves(line, turn, low, high)[:1])
    bias = jnp.concatenate(biases, axis=1)
    wd_c[...] = wd_s[:, pl.ds(pl.multiple_of(chunk * half, half), half), :].reshape(width, width)

    def products(m):
        pre_b[m % 2][...] = dot_nn(normed_s[m], wu_c[...])
        gact_b[m % 2][...] = dot_nt(cot_s[m], wd_c[...])

    products(0)
    bias_rows = 0.0
    for m in range(micro):
        if m + 1 < micro:
            products(m + 1)
        pre = pre_b[m % 2][...] + bias
        cdf = 0.5 * (1.0 + lax.erf(pre * INV_SQRT_TWO))
        pdf = jnp.exp(-0.5 * pre * pre) * INV_SQRT_TWO_PI
        act = (pre * cdf).astype(BF16)
        out_s[m] += dot_nn(act, wd_c[...])
        add(acc_d, m == 0, dot_nn(g_out_t[m], act))
        g_pre_f = gact_b[m % 2][...] * (cdf + pre * pdf)
        g_pre = g_pre_f.astype(BF16)
        add(acc_u, m == 0, dot_nn(normed_t[m], g_pre))
        bias_rows = bias_rows + row_sum(g_pre_f)
        gn2_s[m] += dot_nt(g_pre, wu_c[...])
        if m == 0:
            at(2, (0, 2))
            at(3, (0, 3), (1, 2))
        if m == 1:
            at(1, (0, 1))
            at(2, (1, 1))
            at(3, (2, 1))
    row = lax.broadcasted_iota(jnp.int32, (8, width), 0)
    small_out[8:16, :] += jnp.where(row == chunk, jnp.broadcast_to(bias_rows, (8, width)), 0.0)
    up, down = acc_u[...].astype(BF16), acc_d[...].T.astype(BF16)
    for f in range(CHUNKS):

        @pl.when(chunk == f)
        def _():
            grads[f][0][...] = up.reshape(grads[f][0].shape)
            grads[f][1][...] = down.reshape(grads[f][1].shape)
            step(f, 0)

    @pl.when(chunk == last)
    def _():
        step(0, 4)
        step(1, 3)
        step(2, 2)
        outs = []
        for m in range(micro):
            if m == 2:
                step(3, 1)
            act_s[m] = out_s[m].astype(BF16)
            unit, g_norm = unit_s[m], gn2_s[m]
            g_out_f = cot_s[m].astype(F32)
            small_out[3:4, :] += row_sum(g_norm * unit)
            small_out[4:5, :] += row_sum(g_norm)
            small_out[5:6, :] += row_sum(g_out_f)
            g_hidden = g_out_f + norm_back(g_norm, unit, inv_s[m][:, :1], gain)
            ghid_s[m] = g_hidden
            branch = g_hidden.astype(BF16)
            add(acc_o, m == 0, dot_tn(mixed_s[m], branch))
            gmix_s[m] = dot_nt(branch, wo_s[...]).astype(BF16)
            for src, dst in ((act_s, act_out), (ghid_s, ghid_out), (gmix_s, gmix_out)):
                outs.append(pltpu.make_async_copy(src.at[m], dst.at[m], out_sem.at[len(outs)]))
                outs[-1].start()
        dwo_out[...] = acc_o[...].astype(BF16).reshape(dwo_out.shape)
        for f in range(CHUNKS):
            step(f, upto[f])
        for i in range(2):
            part_outs[0][i][...] = flows[0][i].full[...]
            part_outs[1][i][...] = flows[1][i].full[place.me["table"]]
            part_outs[2][i][...] = flows[2][i].dp_total()[...]
            part_outs[3][i][...] = flows[3][i].dp.bufs[1][...]
        for f in range(CHUNKS):
            for flow in flows[f]:
                flow.done = upto[f]
                flow.sent()
        for copy in outs:
            copy.wait()


def mlp_both_reduce(dp_size, table_size, mixed, emb, cot, wo, wu, wd, vec, bu):
    micro, rows, width = mixed.shape
    hidden_units = wu.shape[1]
    own = hidden_units // dp_size
    wd = wd.reshape(dp_size, own, width)
    far = pl.BlockSpec(memory_space=pl.ANY)
    whole = pl.BlockSpec(memory_space=pltpu.VMEM)
    block = (table_size, width // dp_size // table_size, width)
    parts = [block, block[1:], block, (2,) + block]
    hops = len(hops_of(dp_size))

    def per_micro(dtype):
        return pltpu.VMEM((micro, rows, width), dtype)

    def square(dtype):
        return pltpu.VMEM((width, width), dtype)

    scratch = [per_micro(BF16), per_micro(F32), per_micro(BF16)]
    scratch += [square(BF16), pltpu.VMEM(wu.shape, BF16), pltpu.VMEM(wd.shape, BF16)]
    scratch += [per_micro(BF16)] + [pltpu.VMEM((micro, width, rows), BF16)] * 2
    scratch += [per_micro(F32)] * 3
    scratch += [square(BF16)] * 2 + [square(F32)] * 3 + [pltpu.VMEM((micro, rows, LANES), F32)]
    scratch += [pltpu.VMEM((rows, width), F32)] * 4
    scratch += [pltpu.VMEM((dp_size,) + block, BF16)] * (2 * CHUNKS)
    for _ in range(2 * CHUNKS):
        scratch += quick_scratch(hops, table_size, block, BF16)
    count = 2 * CHUNKS * quick_sems(hops, table_size)
    scratch += [pltpu.SemaphoreType.DMA((3 * micro + 3,)), pltpu.SemaphoreType.DMA((3 * micro,))]
    scratch += [pltpu.SemaphoreType.DMA((count,))] * 2
    return pl.pallas_call(
        functools.partial(mlp_reduce_kernel, dp_size, table_size),
        grid=(CHUNKS,),
        in_specs=[far] * 6 + [whole] * 2,
        out_specs=[far] * 3 + [whole] * (2 + 2 * CHUNKS),
        out_shape=[jax.ShapeDtypeStruct((micro, rows, width), d) for d in (BF16, F32, BF16)]
        + [jax.ShapeDtypeStruct((dp_size,) + block, BF16), jax.ShapeDtypeStruct((16, width), F32)]
        + [jax.ShapeDtypeStruct(p, BF16) for p in parts for _ in range(2)],
        scratch_shapes=scratch,
        compiler_params=vmem(60, collective_id=2, has_side_effects=True),
        name="mlp_both_reduce",
    )(mixed, emb, cot, wo, wu, wd, vec, bu)


def attend_back_core(
    hooks, p_ref, linv_ref, k_ref, v_ref, q_ref, gmix_ref, mixed_ref, n_ref, x_ref, ghid_ref,
    wet_ref, vec_ref, wq_ref, wk_ref, wv_ref,
    sums_ref, dkv_ref, dq_ref, wkv_t, wq_t, acc_e, acc_q, acc_kv, d_bufs, e_bufs, g_bufs,
):
    step, pair = pl.program_id(0), pl.program_id(1)
    length, rows, width = n_ref.shape[1], dq_ref.shape[0], dq_ref.shape[1]
    heads = p_ref.shape[1]
    own = lax.axis_index("table")
    here = pl.ds(pl.multiple_of(own * rows, rows), rows)

    @pl.when((step == 0) & (pair == 0))
    def _():
        acc_e[...] = jnp.zeros_like(acc_e)
        acc_q[...] = jnp.zeros_like(acc_q)
        acc_kv[...] = jnp.zeros_like(acc_kv)
        sums_ref[...] = jnp.zeros_like(sums_ref)
        gain = vec_ref[1:2, :]

        def weigh(w):
            w = w.T.astype(F32) * gain
            return (w - jnp.mean(w, axis=-1, keepdims=True)).astype(BF16)

        for h in range(HEADS):
            cols = slice(h * HEAD_DIM, (h + 1) * HEAD_DIM)
            wkv_t[2 * h * HEAD_DIM : (2 * h + 1) * HEAD_DIM, :] = weigh(wk_ref[:, cols])
            wkv_t[(2 * h + 1) * HEAD_DIM : (2 * h + 2) * HEAD_DIM, :] = weigh(wv_ref[:, cols])
            wq_t[cols, :] = weigh(wq_ref[:, cols])

    keys = d_bufs[0].shape[1]
    units = [(h, j) for h in range(heads) for j in range(length // keys)]
    low, low_t, delta, q_t, dq = {}, {}, {}, {}, {}

    def prepare(h):
        cols = slice(h * HEAD_DIM, (h + 1) * HEAD_DIM)
        linv = linv_ref[0, h][:, :1]
        low[h] = (gmix_ref[0, :, cols].astype(F32) * linv).astype(BF16)
        delta[h] = jnp.sum(mixed_ref[0, :, cols] * low[h].astype(F32), axis=-1, keepdims=True)
        low_t[h] = low[h].T
        q_t[h] = q_ref[0, :, cols].T

    def grad_p(u):
        h, j = units[u]
        if j == 0:
            prepare(h)
        at = slice(j * keys, (j + 1) * keys)
        d_bufs[u % 2][...] = dot_nt(low[h], v_ref[0, at, h * HEAD_DIM : (h + 1) * HEAD_DIM])

    grad_p(0)
    for u, (h, j) in enumerate(units):
        if u + 1 < len(units):
            grad_p(u + 1)
        at = slice(j * keys, (j + 1) * keys)
        cols = slice(h * HEAD_DIM, (h + 1) * HEAD_DIM)
        k_rows = pl.ds(pl.multiple_of(2 * (pair * heads + h) * HEAD_DIM, HEAD_DIM), HEAD_DIM)
        v_rows = pl.ds(pl.multiple_of((2 * (pair * heads + h) + 1) * HEAD_DIM, HEAD_DIM), HEAD_DIM)
        p = p_ref[0, h, :, at]
        dkv_ref[v_rows, at] = dot_nn(low_t[h], p).astype(BF16)
        ds = (p.astype(F32) * (d_bufs[u % 2][...] - delta[h])).astype(BF16)
        dkv_ref[k_rows, at] = (dot_nn(q_t[h], ds) * SCALE).astype(BF16)
        dq_part = dot_nn(ds, k_ref[0, at, cols])
        dq[h] = dq_part if j == 0 else dq[h] + dq_part
    for h in range(heads):
        cols = pl.ds(pl.multiple_of((pair * heads + h) * HEAD_DIM, HEAD_DIM), HEAD_DIM)
        dq_ref[:, cols] = (dq[h] * SCALE).astype(BF16)
    for h in range(heads):
        at = pl.ds(pl.multiple_of((pair * heads + h) * 2 * HEAD_DIM, 2 * HEAD_DIM), 2 * HEAD_DIM)
        acc_kv[at, :] += dot_nn(dkv_ref[at, :], n_ref[0])
    both = pl.ds(pl.multiple_of(pair * heads * HEAD_DIM, heads * HEAD_DIM), heads * HEAD_DIM)
    acc_q[both, :] += dot_tn(dq_ref[:, both], n_ref[0, here, :])
    sums_ref[0:1, both] += row_sum(gmix_ref[0].astype(F32))
    sums_ref[1:2, both] += row_sum(dq_ref[:, both].astype(F32))
    hooks.pair_done()

    @pl.when(pair == HEADS // heads - 1)
    def _():
        part = e_bufs[0].shape[0]
        hooks.tick(HEADS // heads, None)

        def rows_back(block, mine):
            def spot(u):
                return pl.ds(pl.multiple_of(block * rows + u * part, part), part), slice(u * part, (u + 1) * part)

            def products(u):
                at, inner = spot(u)
                e_bufs[u % 2][...] = dot_nt(x_ref[0, at, :], wet_ref[...])
                q = dot_tn(dkv_ref[:, at], wkv_t[...])
                if mine:
                    q = q + dot_nn(dq_ref[inner, :], wq_t[...])
                g_bufs[u % 2][...] = q

            products(0)
            for u in range(rows // part):
                if u + 1 < rows // part:
                    products(u + 1)
                at, inner = spot(u)
                unit, inv = norm_parts(e_bufs[u % 2][...])
                q = g_bufs[u % 2][...]
                g_emb = inv * (q - unit * jnp.mean(q * unit, axis=-1, keepdims=True))
                if mine:
                    g_emb = g_emb + ghid_ref[0, inner, :]
                g_emb = g_emb.astype(BF16)
                acc_e[...] += dot_tn(x_ref[0, at, :], g_emb)
                hooks.put(block, mine, inner, dot_nn(g_emb, wet_ref[...]))

        size = length // rows

        def other(g, carry):
            block = lax.rem(own + 1 + g, size)
            rows_back(block, False)
            hooks.block_done(g, block)
            hooks.tick(HEADS // heads + 1, g)
            return carry

        lax.fori_loop(0, size - 1, other, 0)
        rows_back(own, True)
        hooks.own_done()


def norm_one_grads(vec_ref, wq_ref, wk_ref, wv_ref, sums_ref, acc_q, acc_kv):
    gain, shift = vec_ref[1:2, :], vec_ref[2:3, :]
    total = row_sum(wq_ref[...].T.astype(F32) * acc_q[...])
    for h in range(HEADS):
        cols = slice(h * HEAD_DIM, (h + 1) * HEAD_DIM)
        k_rows = slice(2 * h * HEAD_DIM, (2 * h + 1) * HEAD_DIM)
        v_rows = slice((2 * h + 1) * HEAD_DIM, (2 * h + 2) * HEAD_DIM)
        total += row_sum(wk_ref[:, cols].T.astype(F32) * acc_kv[k_rows, :])
        total += row_sum(wv_ref[:, cols].T.astype(F32) * acc_kv[v_rows, :])
    sums = sums_ref[...]
    high = sums.astype(BF16)
    rest = (sums - high.astype(F32)).astype(BF16)
    by_v = dot_nt(high, wv_ref[...]) + dot_nt(rest, wv_ref[...])
    by_q = dot_nt(high, wq_ref[...]) + dot_nt(rest, wq_ref[...])
    d_shift = by_v[0:1, :] + by_q[1:2, :]
    return (total - shift * d_shift) / gain, d_shift


class Alone:
    def __init__(self, ig_ref, rows):
        self.ig_ref, self.rows = ig_ref, rows

    def tick(self, k, g):
        pass

    def pair_done(self):
        pass

    def put(self, block, mine, inner, value):
        at = pl.ds(pl.multiple_of(block * self.rows + inner.start, 128), inner.stop - inner.start)
        self.ig_ref[0, at, :] = value.astype(BF16)

    def block_done(self, g, block):
        pass

    def own_done(self):
        pass


def attend_back_kernel(*refs):
    ins, rest = refs[:15], refs[15:]
    ig_ref, dwe_ref, dwq_ref, dwk_ref, dwv_ref, dvec_ref = rest[:6]
    scratch, bufs = rest[6:14], rest[14:]
    sums_ref, acc_e, acc_q, acc_kv = scratch[0], *scratch[5:8]
    vec_ref, wq_ref, wk_ref, wv_ref = ins[11:15]
    rows = scratch[2].shape[0]
    attend_back_core(Alone(ig_ref, rows), *ins, *scratch, bufs[:2], bufs[2:4], bufs[4:])

    @pl.when((pl.program_id(0) == pl.num_programs(0) - 1) & (pl.program_id(1) == pl.num_programs(1) - 1))
    def _():
        dwe_ref[...] = acc_e[...].T.astype(BF16)
        dwq_ref[...] = acc_q[...].T.astype(BF16)
        d_gain, d_shift = norm_one_grads(vec_ref, wq_ref, wk_ref, wv_ref, sums_ref, acc_q, acc_kv)
        dvec_ref[...] = jnp.zeros_like(dvec_ref)
        dvec_ref[1:2, :] = d_gain
        dvec_ref[2:3, :] = d_shift
        for h in range(HEADS):
            cols = slice(h * HEAD_DIM, (h + 1) * HEAD_DIM)
            dwk_ref[:, cols] = acc_kv[2 * h * HEAD_DIM : (2 * h + 1) * HEAD_DIM, :].T.astype(BF16)
            dwv_ref[:, cols] = acc_kv[(2 * h + 1) * HEAD_DIM : (2 * h + 2) * HEAD_DIM, :].T.astype(BF16)


class Sums:
    def __init__(self, tail, igs):
        self.tail, self.igs = tail, igs
        self.micro, self.head = pl.program_id(0), pl.program_id(1)
        self.count = len(igs)
        self.todo = {}

    def tick(self, k, g=None):
        for m in range(self.count):
            for i in range(1 if g is None else TABLE_STEPS):
                actions = self.todo.get((m, k + i), [])
                if not actions:
                    continue
                now = self.micro == m
                now = now & (self.head == k) if k < PAIRS else now if g is None else now & (g == i)

                @pl.when(now)
                def _():
                    for action in actions:
                        action()

    def start_of_step(self):
        for k in range(PAIRS):
            self.tick(k)

    def at(self, m, k, action):
        self.todo.setdefault((m, k), []).append(action)

    def step(self, flows, i):
        def action():
            for flow in flows:
                if i:
                    flow.arrive(i - 1)
                if i < flow.steps:
                    flow.start(i)

        return action

    def pair_done(self):
        for g in range(PAIRS):

            @pl.when((self.micro == self.count - 1) & (self.head == g))
            def _():
                self.write_pair(g)
                self.step(self.tail[g], 0)()

    def put(self, block, mine, inner, value):
        if mine:
            self.ig_own[inner, :] = value
        else:
            self.ig_bufs[self.micro, block, inner, :] = value.astype(BF16)

    def block_done(self, g, block):
        for m in range(self.count):

            @pl.when(self.micro == m)
            def _():
                self.igs[m].start_one(g + 1)

    def own_done(self):
        self.ig_out[self.micro] = self.ig_own[...]
        self.tick(PAIRS + 1 + TABLE_STEPS)

    def ig_finish(self, m):
        def action():
            total = self.ig_out[m]
            for got in self.igs[m].arrive():
                total = total + got[...].astype(F32)
            self.ig_out[m] = total

        return action


def attend_back_reduce_kernel(dp_size, table_size, *refs):
    refs = list(refs)

    def take(n):
        out = refs[:n]
        del refs[:n]
        return out

    ins = take(15)
    vec_ref, wq_ref, wk_ref, wv_ref = ins[11:15]
    parts = take(7)
    (small_in,) = take(1)
    ig_out, small_out, embed_out = take(3)
    totals = take(11)
    core = take(8)
    sums_ref, acc_e, acc_q, acc_kv = core[0], *core[5:8]
    bufs = take(6)
    place = Place(dp_size, table_size)
    hops = place.hops["dp"]
    part_scratch = [take(n) for n in [len(hops) + 2] + [3] * 2 + [2] * 2 + [1] * 2]
    tail_grads = take(4)
    tail_scratch = [take(len(hops) + 2) for _ in range(4)]
    embed_grad, small_grad = take(2)
    embed_scratch, small_scratch_ = take(3), take(3)
    micro = ig_out.shape[0]
    (ig_bufs,) = take(1)
    ig_got = take(micro)
    (ig_own,) = take(1)
    send_sem, recv_sem = refs
    sems = (send_sem, recv_sem)
    forth, back = hops, hops[:1] + hops[:0:-1]
    base = 0

    def count_up(n):
        nonlocal base
        base += n
        return base - n

    def quick(order, blocks, scratch, back_only=False):
        at = count_up(quick_sems(len(order), table_size, back_only))
        return QuickShard(place, order, blocks, scratch, sems, at, back_only)

    def by_owner(grad):
        return lambda s: grad.at[toggled_by(place.me["dp"], s)]

    out_flow = quick(forth, by_owner(parts[0]), part_scratch[0])
    thirds = [
        quick(order[-1:], lambda s, p=p: p.at[len(s)], scr)
        for order, p, scr in zip((forth, back), parts[1:3], part_scratch[1:3])
    ]
    seconds = [quick([], lambda s, p=p: p, scr) for p, scr in zip(parts[3:5], part_scratch[3:5])]
    firsts = [quick([], lambda s, p=p: p, scr, True) for p, scr in zip(parts[5:], part_scratch[5:])]
    mlp = [out_flow] + thirds + seconds + firsts
    tail = [
        [
            quick(order, by_owner(tail_grads[2 * g + i]), tail_scratch[2 * g + i])
            for i, order in enumerate((forth, back))
        ]
        for g in range(2)
    ]
    others = dp_size + table_size - 2
    embed = Small(place, lambda d: embed_grad.at[d], *embed_scratch, sems, count_up(others))
    small = Small(place, lambda d: small_grad.at[d // 2], *small_scratch_, sems, count_up(others))
    igs = []
    for m in range(micro):
        igs.append(
            Swap(
                place, "table", sems, count_up(table_size - 1),
                lambda t, m=m: ig_bufs.at[m, t],
                lambda t, s, m=m: ig_got[m].at[s - 1],
            )
        )
    hooks = Sums(tail, igs)
    hooks.ig_bufs, hooks.ig_own, hooks.ig_out = ig_bufs, ig_own, ig_out

    def write_pair(g):
        one, two = tail_grads[2 * g], tail_grads[2 * g + 1]
        shape = one.shape[:-1]

        def put(ref, at, value):
            ref[:, :, :, at * HEAD_DIM : at * HEAD_DIM + value.shape[1]] = value.astype(BF16).reshape(
                shape + (value.shape[1],)
            )

        def rows_of(h, side):
            at = (2 * h + side) * HEAD_DIM
            return acc_kv[at : at + HEAD_DIM, :].T

        put(one, 0, acc_q[2 * g * HEAD_DIM : (2 * g + 2) * HEAD_DIM, :].T)
        put(one, 2, rows_of(2 * g, 0))
        put(two, 0, rows_of(2 * g + 1, 0))
        put(two, 1, rows_of(2 * g, 1))
        put(two, 2, rows_of(2 * g + 1, 1))

    hooks.write_pair = write_pair

    last = micro - 1
    hooks.at(0, 0, lambda: place.greet(True)())
    for i, (m, k) in enumerate(((0, 0), (0, 1), (0, 2), (1, 0), (1, 1), (1, 2))):
        hooks.at(m, k, hooks.step([f for f in mlp if i <= f.steps], i))
    hooks.at(1, 2, hooks.ig_finish(0))
    hooks.at(2, 1, hooks.step(tail[0], 1))
    hooks.at(2, 2, hooks.step(tail[0], 2))
    hooks.at(2, 3, hooks.ig_finish(1))
    hooks.at(2, 3, hooks.step(tail[1], 1))
    hooks.at(2, 4, hooks.step(tail[0], 3))
    hooks.at(2, 5, hooks.step(tail[1], 2))

    def finish():
        embed_grad[...] = acc_e[...].T.astype(BF16).reshape(embed_grad.shape)
        hooks.step([embed], 0)()
        d_gain, d_shift = norm_one_grads(vec_ref, wq_ref, wk_ref, wv_ref, sums_ref, acc_q, acc_kv)
        for t in range(dp_size // 2):
            cols = slice(t * LANES, (t + 1) * LANES)
            small_grad[t] = small_in[:, cols]
            small_grad[t, 1:2, :] = d_gain[:, cols]
            small_grad[t, 2:3, :] = d_shift[:, cols]
        ends = [embed, small]
        hooks.step([small], 0)()
        hooks.step(tail[1], 3)()
        hooks.step(tail[0], 4)()
        hooks.step(ends, 1)()
        hooks.step(tail[1], 4)()
        hooks.step(tail[0], 5)()
        hooks.ig_finish(last)()
        hooks.step(ends, 2)()
        hooks.step(tail[1], 5)()
        for flow in mlp + tail[0] + tail[1] + ends + igs:
            flow.sent()
        embed_out[...] = embed.total
        small_out[...] = small.total
        for flow, out in zip(mlp + tail[0] + tail[1], totals):
            out[...] = flow.full[...]

    hooks.at(last, PAIRS + 1 + TABLE_STEPS, finish)
    hooks.start_of_step()
    attend_back_core(hooks, *ins, *core, bufs[:2], bufs[2:4], bufs[4:])


def back_scratch(length, rows, width):
    return [
        pltpu.VMEM((8, width), F32),
        pltpu.VMEM((2 * width, length), BF16),
        pltpu.VMEM((rows, width), BF16),
        pltpu.VMEM((2 * width, width), BF16),
        pltpu.VMEM((width, width), BF16),
        pltpu.VMEM((LANES, width), F32),
        pltpu.VMEM((width, width), F32),
        pltpu.VMEM((2 * width, width), F32),
    ]


def back_buffers(rows, width):
    return [pltpu.VMEM((rows, KEY_BLOCK), F32)] * 2 + [pltpu.VMEM((BACK_BLOCK, width), F32)] * 4


def back_specs(by_head, cols, varied, fixed):
    return (
        [heads_spec(a.shape[2:]) for a in by_head]
        + [pl.BlockSpec((1, a.shape[1], HEADS_STEP * HEAD_DIM), lambda m, h: (m, 0, h)) for a in cols]
        + [micro_spec(a.shape[1:]) for a in varied]
        + [const_spec(a.shape) for a in fixed]
    )


def attend_backward(p, linv, k, v, q, gmix, mixed, n, x, ghid, wet, vec, wq, wk, wv):
    micro, rows, width = q.shape
    length = k.shape[1]
    varied = (n, x, ghid)
    fixed = (wet, vec, wq, wk, wv)
    summed = [(wet.shape, BF16)] + [((width, width), BF16)] * 3 + [((8, width), F32)]
    return pl.pallas_call(
        attend_back_kernel,
        grid=(micro, HEADS // HEADS_STEP),
        in_specs=back_specs((p, linv), (k, v, q, gmix, mixed), varied, fixed),
        out_specs=[micro_spec((length, LANES))] + [const_spec(s) for s, _ in summed],
        out_shape=[jax.ShapeDtypeStruct((micro, length, LANES), BF16)]
        + [jax.ShapeDtypeStruct(s, d) for s, d in summed],
        scratch_shapes=back_scratch(length, rows, width) + back_buffers(rows, width),
        compiler_params=vmem(58),
        name="attend_backward",
    )(p, linv, k, v, q, gmix, mixed, *varied, *fixed)


def attend_backward_reduce(
    dp_size, table_size, parts, small, p, linv, k, v, q, gmix, mixed, n, x, ghid, wet, vec, wq, wk, wv
):
    micro, rows, width = q.shape
    length = k.shape[1]
    varied = (n, x, ghid)
    fixed = (wet, vec, wq, wk, wv)
    whole = pl.BlockSpec(memory_space=pltpu.VMEM)
    shard = width // dp_size
    block = (table_size, shard // table_size, width)
    tail = (dp_size, table_size, shard // table_size, 3 * HEAD_DIM)
    blocks = [block] * 7 + [tail[1:]] * 4
    hops = len(hops_of(dp_size))
    kinds = [(hops, False)] + [(1, False)] * 2 + [(0, False)] * 2 + [(0, True)] * 2
    scratch = back_scratch(length, rows, width) + back_buffers(rows, width)
    for n, back_only in kinds:
        scratch += quick_scratch(n, table_size, block, BF16, back_only)
    scratch += [pltpu.VMEM(tail, BF16)] * 4
    for _ in range(4):
        scratch += quick_scratch(hops, table_size, tail[1:], BF16)
    tile = (small.shape[0], LANES)
    scratch += [pltpu.VMEM((dp_size, shard, LANES), BF16), pltpu.VMEM((dp_size // 2,) + tile, F32)]
    scratch += small_scratch(dp_size, table_size, (shard, LANES), BF16)
    scratch += small_scratch(dp_size, table_size, tile, F32)
    scratch += [pltpu.VMEM((micro, table_size, rows, LANES), BF16)]
    scratch += [pltpu.VMEM((table_size - 1, rows, LANES), BF16)] * micro
    scratch += [pltpu.VMEM((rows, LANES), F32)]
    count = sum(quick_sems(n, table_size, back_only) for n, back_only in kinds + [(hops, False)] * 4)
    count += 2 * (dp_size + table_size - 2) + micro * (table_size - 1)
    scratch += [pltpu.SemaphoreType.DMA((count,))] * 2
    outs = [((micro, rows, LANES), F32), (tile, F32), ((shard, LANES), F32)]
    outs += [(b, BF16) for b in blocks]
    return pl.pallas_call(
        functools.partial(attend_back_reduce_kernel, dp_size, table_size),
        grid=(micro, PAIRS),
        in_specs=back_specs((p, linv), (k, v, q, gmix, mixed), varied, fixed)
        + [whole] * 7
        + [const_spec(small.shape)],
        out_specs=[const_spec(shape) for shape, _ in outs],
        out_shape=[jax.ShapeDtypeStruct(shape, dtype) for shape, dtype in outs],
        scratch_shapes=scratch,
        compiler_params=vmem(60, collective_id=1, has_side_effects=True),
        name="attend_backward_reduce",
    )(p, linv, k, v, q, gmix, mixed, *varied, *fixed, *parts, small)


def finish_kernel(feat, shard, mask_ref, ig_in, small_in, embed_in, *refs):
    chunk_ins, out_in, pair_ins, outs = refs[: 2 * CHUNKS], refs[2 * CHUNKS], refs[2 * CHUNKS + 1 : 2 * CHUNKS + 5], refs[2 * CHUNKS + 5 :]
    ig_out, dwe, dwq, dwk, dwv, dwo, dwu, dwd = outs[:8]
    vecs, bu = outs[8:14], outs[14]
    half = LANES // 2
    for m in range(ig_in.shape[0]):
        ig_out[m] = ig_in[m].T[:feat, :] * mask_ref[m].astype(F32)
    dwe[...] = embed_in[:, :feat]
    dwo[...] = out_in[...].astype(F32)
    lane = lax.broadcasted_iota(jnp.int32, (shard, LANES), 1)
    ups, downs = chunk_ins[::2], chunk_ins[1::2]
    for f in range(CHUNKS):
        dwd[f * half : (f + 1) * half, :] = downs[f][...].astype(F32)
    per_owner = bu.shape[1]
    for o in range(dwu.shape[1] // per_owner):
        for f in range(0, CHUNKS, 2):
            tile = slice(o // 2 * LANES, (o // 2 + 1) * LANES)
            low, high = ups[f][:, tile].astype(F32), ups[f + 1][:, tile].astype(F32)
            at = o * per_owner + f * half
            dwu[:, at : at + LANES] = halves(lane, o % 2 * half, low, high)
    for g in range(HEADS // 2):
        one, two = pair_ins[2 * g], pair_ins[2 * g + 1]
        at = 2 * g * HEAD_DIM
        dwq[:, at : at + 2 * HEAD_DIM] = one[:, : 2 * HEAD_DIM].astype(F32)
        dwk[:, at : at + HEAD_DIM] = one[:, 2 * HEAD_DIM :].astype(F32)
        dwk[:, at + HEAD_DIM : at + 2 * HEAD_DIM] = two[:, :HEAD_DIM].astype(F32)
        dwv[:, at : at + 2 * HEAD_DIM] = two[:, HEAD_DIM:].astype(F32)
    small = small_in[...]
    turned = pltpu.roll(small, lax.rem(lax.axis_index("dp"), 2) * half, 1)
    vecs[0][...] = embed_in[...].T[feat : feat + 1, :]
    for i, out in enumerate(vecs[1:]):
        out[...] = turned[i + 1 : i + 2, :shard]
    rows = turned[8:16, :]
    line = lax.broadcasted_iota(jnp.int32, (8, LANES), 1)
    for f in range(0, CHUNKS, 2):
        low = jnp.broadcast_to(rows[f : f + 1, :], (8, LANES))
        high = jnp.broadcast_to(rows[f + 1 : f + 2, :], (8, LANES))
        bu[:, f * half : f * half + LANES] = halves(line, 0, low, high)[:1]


def finish(feat, ff_shard, mask, ig, small, embed, chunks, rest):
    micro, rows, _ = ig.shape
    shard = embed.shape[0]
    width = rest[0].shape[1]
    out_shape = (
        [jax.ShapeDtypeStruct((micro, feat, rows), F32), jax.ShapeDtypeStruct((shard, feat), F32)]
        + [jax.ShapeDtypeStruct((shard, width), F32)] * 4
        + [jax.ShapeDtypeStruct((shard, CHUNKS * width), F32), jax.ShapeDtypeStruct((ff_shard, width), F32)]
        + [jax.ShapeDtypeStruct((1, shard), F32)] * 6
        + [jax.ShapeDtypeStruct((1, ff_shard), F32)]
    )
    return pl.pallas_call(
        functools.partial(finish_kernel, feat, shard),
        out_shape=out_shape,
        compiler_params=vmem(60),
        name="finish",
    )(mask, ig, small, embed, *chunks, *rest)


def body(
    dp_size, table_size, features, feature_mask, support_count, embed_weight, embed_bias, gain_first, shift_first,
    query_weight, key_weight, value_weight, out_weight, gain_second, shift_second, up_weight, up_bias,
    down_weight, down_bias, cotangent,
):
    micro, _, rows, feat = features.shape
    shard, width = query_weight.shape
    hidden_units = up_weight.shape[1]
    ff_shard = up_bias.shape[0]
    features, cotangent, support = features[:, 0], cotangent[:, 0], support_count[:, 0]
    vectors = (embed_bias, gain_first, shift_first, gain_second, shift_second, down_bias)
    if 2 * shard == LANES and micro == 3 and table_size == 4 and ff_shard == CHUNKS * shard:
        got = attend_forward_gather(
            dp_size, table_size, support, features.transpose(0, 2, 1), feature_mask, embed_weight.T,
            [a[None] for a in vectors], up_bias.reshape(-1, LANES),
            query_weight, key_weight, value_weight, out_weight, up_weight, down_weight,
        )
        q, k, v, n, emb, mixed, mixed_low, p, linv, x = got[:10]
        wet, wq, wk, wv = (g.reshape(-1, g.shape[-1]) for g in got[10:14])
        vec, bu = got[14:16]
        wo, wu, wd = (g.reshape(-1, g.shape[-1]) for g in got[16:])
        activations, ghid, gmix, dwo, small, *parts = mlp_both_reduce(
            dp_size, table_size, mixed_low, emb, cotangent, wo, wu, wd, vec, bu
        )
        ig, small, embed, *totals = attend_backward_reduce(
            dp_size, table_size, [dwo] + parts[6:] + parts[4:6] + parts[2:4], small,
            p, linv, k, v, q, gmix, mixed, n, x, ghid, wet, vec, wq, wk, wv,
        )
        totals = [t.reshape(-1, t.shape[-1]) for t in totals]
        chunks = [t.reshape(-1, t.shape[-1]) for t in parts[:2]] + totals[5:7] + totals[3:5] + totals[1:3]
        mask = feature_mask.reshape(micro, feat, 1)
        out = finish(feat, ff_shard, mask, ig, small, embed, chunks, totals[:1] + totals[7:])
        ig, dwe, dwq, dwk, dwv, dwo, dwu, dwd = out[:8]
        ig, dwe = ig.transpose(0, 2, 1), dwe.T
        smalls = [o.reshape(-1) for o in out[8:14]]
        dbu = out[14].reshape(-1)
    else:
        smalls = jnp.stack(vectors)
        mask = jnp.pad(feature_mask[:, 0], ((0, 0), (0, LANES - feat)))[:, None, :]
        x = jnp.pad(features, ((0, 0), (0, 0), (0, LANES - feat))) * mask.astype(BF16)
        x = x.at[:, :, feat].set(1.0)
        wet = jnp.concatenate([embed_weight, embed_bias[None]])
        wet = jnp.pad(wet, ((0, LANES - feat - 1), (0, 0))).T
        shards = [wet, query_weight, key_weight, value_weight, out_weight, up_weight, down_weight]
        wet, wq, wk, wv, wo, wu, wd = (lax.all_gather(s, "dp", axis=0, tiled=True) for s in shards)
        vec = jnp.pad(lax.all_gather(smalls, "dp", axis=1, tiled=True).astype(F32), ((0, 2), (0, 0)))
        bu = lax.all_gather(up_bias, "dp", axis=0, tiled=True).astype(F32)[None]
        x = lax.all_gather(x, "table", axis=1, tiled=True)
        q, k, v, n, emb, mixed, mixed_low, p, linv = attend_forward(support, x, wet, vec, wq, wk, wv, rows)
        activations, ghid, gmix, dwo, dwu, dwd, small = mlp_both(mixed_low, emb, cotangent, wo, wu, wd, vec, bu)
        ig, dwe, dwq, dwk, dwv, dvec = attend_backward(
            p, linv, k, v, q, gmix, mixed, n, x, ghid, wet, vec, wq, wk, wv
        )
        big = [dwe, dwq, dwk, dwv, dwo, dwu, dwd]
        own = [lax.psum_scatter(g.astype(F32), "dp", scatter_dimension=0, tiled=True) for g in big]
        dwe, dwq, dwk, dwv, dwo, dwu, dwd = (lax.psum(g, "table") for g in own)
        dbe, dwe = dwe[:, feat], dwe[:, :feat].T
        dvec = jnp.concatenate([dvec[:3], small[3:6]])
        smalls = lax.psum(lax.psum_scatter(dvec, "dp", scatter_dimension=1, tiled=True), "table")
        smalls = [dbe] + [smalls[i] for i in range(1, 6)]
        dbu = small[8:].reshape(-1)[:hidden_units]
        dbu = lax.psum(lax.psum_scatter(dbu, "dp", scatter_dimension=0, tiled=True), "table")
        ig = lax.psum_scatter(ig.astype(F32) * mask, "table", scatter_dimension=1, tiled=True)[:, :, :feat]
    return (
        activations[:, None], ig[:, None], dwe, smalls[0], smalls[1], smalls[2],
        dwq, dwk, dwv, dwo, smalls[3], smalls[4], dwu, dbu, dwd, smalls[5],
    )


def solution(mesh):
    rows, cols, vecs = P("dp", None), P(None, "dp"), P("dp")
    table = P(None, "dp", "table", None)
    return jax.shard_map(
        functools.partial(body, mesh.shape["dp"], mesh.shape["table"]),
        mesh=mesh,
        in_specs=(
            table, P(None, "dp", None), cols, cols, vecs, vecs, vecs, rows, rows, rows, rows,
            vecs, vecs, rows, vecs, rows, vecs, table,
        ),
        out_specs=(
            table, table, cols, vecs, vecs, vecs, rows, rows, rows, rows, vecs, vecs, rows, vecs, rows, vecs,
        ),
        check_vma=False,
    )
```

time: 212 us -> 205 us (0.967)
  Pallas kernels: 208 us -> 199 us
    pallas_call x1, Pallas kernels: 34.4 us -> 44.4 us  [mlp_both_reduce(): pl.pallas_call(functools.partial(mlp_reduce_kernel, dp_size, table_size),...]
    pallas_call x1, Pallas kernels: 101 us -> 91 us  [attend_backward_reduce(): pl.pallas_call(functools.partial(attend_back_reduce_kernel, dp_size, tabl...]
    pallas_call x1, Pallas kernels: 70 us -> 60.5 us  [attend_forward_gather(): pl.pallas_call(functools.partial(attend_gather_kernel, dp_size, table_siz...]
where the time goes in v3:
time: 205 us; the launch traced here: 204 us
  Pallas kernels  199 us (97%)
  local copies, waits for them, and re-layouts  4.51 us (2%)
    pallas_call x1, Pallas kernels, attend_backward_reduce(): pl.pallas_call(functools.partial(attend_back_reduce_kernel, dp_size, tabl...  91 us
    pallas_call x1, Pallas kernels, attend_forward_gather(): pl.pallas_call(functools.partial(attend_gather_kernel, dp_size, table_siz...  60.5 us
    pallas_call x1, Pallas kernels, mlp_both_reduce(): pl.pallas_call(functools.partial(mlp_reduce_kernel, dp_size, table_size),...  44.4 us

profile of v3, /device:TPU:0, one launch (start us, length us, event | category | flops | bytes accessed | tf_op | source)
XLA Modules:
  0.0 204.4 jit_solution(13048341373476836318)
XLA Ops:
  0.7 60.5 %attend_forward_gather.1 = (bf16[3,512,512]{2,1,0:T(8,128)(2,1)}, bf16[3,2048,512]{2,1,0:T(8,128)(2,1)}, bf16[3,2048,512]{2,1,0:T(8,128)(2,1)}, bf16[3,2048,512]...) custom-call(s32[3]{0:T(128)} %bitcast.72, ...), custom_call_target="tpu_custom_call" | custom-call | tf_op jit(solution)/shard_map/attend_forward_gather/pallas_call | solution.py:645
  61.2 44.4 %mlp_both_reduce.1 = (bf16[3,512,512]{2,1,0:T(8,128)(2,1)}, f32[3,512,512]{2,1,0:T(8,128)}, bf16[3,512,512]{2,1,0:T(8,128)(2,1)}, bf16[8,4,16,512]{3,2,1,0:T(8,1...) custom-call(bf16[3,512,512]{2,1,0:T(8,128)(2,1)} %get-tuple-element., ...), custom_call_target="tpu_custom_call" | custom-call | tf_op jit(solution)/shard_map/mlp_both_reduce/pallas_call | solution.py:1031
  105.6 0.0 copy-start.1
  105.6 91.0 %attend_backward_reduce.1 = (f32[3,512,128]{2,1,0:T(8,128)}, f32[16,128]{1,0:T(8,128)}, f32[64,128]{1,0:T(8,128)}, bf16[4,16,512]{2,1,0:T(8,128)(2,1)}, bf16[4,1...) custom-call(bf16[3,4,512,2048]{3,2,1,0:T(8,128)(2,1)} %get-tuple-ele, ...), custom_call_target="tpu_custom_call" | custom-call | tf_op jit(solution)/shard_map/attend_backward_reduce/pallas_call | solution.py:1515
  196.6 0.0 copy-start
  196.6 0.0 copy-done.1
  196.6 0.8 copy.36.mask_ref
  197.4 3.3 %finish.1 = (f32[3,100,512]{2,1,0:T(8,128)}, f32[64,100]{1,0:T(8,128)}, f32[64,512]{1,0:T(8,128)}, f32[64,512]{1,0:T(8,128)}, f32[64,512]{1,0:T(8,128)}, /*index...) custom-call(s32[3,100,1]{2,1,0:T(8,128)} %copy.36.mask_ref, ...), custom_call_target="tpu_custom_call" | custom-call | tf_op jit(solution)/shard_map/finish/pallas_call | solution.py:1580
  200.8 2.5 %copy.38 = f32[3,1,512,100]{2,1,3,0:T(1,128)} copy(f32[3,1,512,100]{2,3,0,1:T(8,128)} %bitcast.50) | data formatting | bytes 1228800
  203.3 0.0 copy-done
  203.3 1.1 copy.40
Async XLA Ops:
  105.6 91.0 %copy-start.1 = (s32[3,1,100]{2,1,0:T(1,128)S(1)}, s32[3,1,100]{2,1,0:T(1,128)}, u32[]{:S(2)}) copy-start(s32[3,1,100]{2,1,0:T(1,128)} %mask_ref.1) | copy-start | bytes 3604
  196.6 6.7 %copy-start = (bf16[3,512,512]{2,1,0:T(8,128)(2,1)S(1)}, bf16[3,512,512]{2,1,0:T(8,128)(2,1)}, u32[]{:S(2)}) copy-start(bf16[3,512,512]{2,1,0:T(8,128)(2,1)} %get-tuple-element.84) | copy-start | bytes 4718596

commit v4 on v3

--- a/solution.py
+++ b/solution.py
@@ -85,20 +85,10 @@
     return pltpu.CompilerParams(vmem_limit_bytes=mib * 2**20, **extra)
 
 
-def toggled(index, hop):
-    return index + hop * (1 - 2 * ((index // hop) % 2))
-
-
-def toggled_by(index, hops):
-    for hop in hops:
-        index = toggled(index, hop)
-    return index
-
-
 def subsets(hops):
     out = [()]
-    for hop in hops:
-        out = out + [s + (hop,) for s in out]
+    for hop in reversed(hops):
+        out = out + [(hop,) + s for s in out]
     return out
 
 
@@ -111,15 +101,28 @@
         self.size = {"dp": dp_size, "table": table_size}
         self.hops = {axis: hops_of(n) for axis, n in self.size.items()}
         self.me = {"dp": lax.axis_index("dp"), "table": lax.axis_index("table")}
+        self.across, self.next = {}, {}
+        for axis, n in self.size.items():
+            me = self.me[axis]
+            turn = {hop: hop * (1 - 2 * lax.rem(lax.div(me, hop), 2)) for hop in self.hops[axis]}
+            for s in subsets(self.hops[axis]):
+                self.across[axis, frozenset(s)] = sum([turn[hop] for hop in s], me)
+            for shift in range(n):
+                self.next[axis, shift] = lax.rem(me + shift, n)
+
+    def toggled(self, axis, hops):
+        return self.across[axis, frozenset(hops)]
 
     def partner(self, axis, hop):
         there = dict(self.me)
-        there[axis] = toggled(there[axis], hop)
+        there[axis] = self.toggled(axis, (hop,))
         return (there["dp"], there["table"])
 
     def at(self, axis, shift):
         n = self.size[axis]
-        return lax.rem(self.me[axis] + (shift + n), n)
+        if isinstance(shift, int):
+            return self.next[axis, shift % n]
+        return lax.rem(self.me[axis] + shift, n)
 
     def ahead(self, axis, shift):
         there = dict(self.me)
@@ -192,7 +195,7 @@
 
     def start(self, step):
         for s in subsets(self.hops[:step]):
-            block = self.full.at[toggled_by(self.place.me[self.axis], s)]
+            block = self.full.at[self.place.toggled(self.axis, s)]
             src = block if s or self.own is None else self.own
             remote(
                 self.place, self.axis, self.hops[step], src, block, self.sems, self.base + step
@@ -211,29 +214,36 @@
 
 
 class Reduce:
-    def __init__(self, place, axis, hops, blocks, bufs, sems, base):
+    def __init__(self, place, axis, hops, blocks, bufs, sems, base, array=None):
         self.place, self.axis, self.hops = place, axis, hops
-        self.held = blocks
+        self.blocks, self.array = blocks, array
         self.bufs, self.sems, self.base = bufs, sems, base
         self.steps = len(hops)
 
-    def mine(self, step, s):
-        if step == 0:
-            return self.held(s)
-        order = [set(t) for t in subsets(self.hops[step:])]
-        return self.bufs[step - 1].at[order.index(set(s))]
+    def before(self, step):
+        return self.bufs[step - 1] if step else self.array
 
     def copy(self, step, src, dst):
         return remote(self.place, self.axis, self.hops[step], src, dst, self.sems, self.base + step)
 
     def start(self, step):
-        for i, s in enumerate(subsets(self.hops[step + 1 :])):
-            self.copy(step, self.mine(step, s + (self.hops[step],)), self.bufs[step].at[i]).start()
+        rest = subsets(self.hops[step + 1 :])
+        held = self.before(step)
+        if held is not None:
+            self.copy(step, held.at[pl.ds(len(rest), len(rest))], self.bufs[step]).start()
+            return
+        for i, s in enumerate(rest):
+            self.copy(step, self.blocks(s + (self.hops[step],)), self.bufs[step].at[i]).start()
 
     def arrive(self, step):
         self.copy(step, self.bufs[step], self.bufs[step]).wait_recv()
-        for i, s in enumerate(subsets(self.hops[step + 1 :])):
-            add_into(self.bufs[step].at[i], self.mine(step, s))
+        rest = subsets(self.hops[step + 1 :])
+        held = self.before(step)
+        if held is not None:
+            add_into(self.bufs[step], held.at[pl.ds(0, len(rest))])
+            return
+        for i, s in enumerate(rest):
+            add_into(self.bufs[step].at[i], self.blocks(s))
 
     def total(self):
         return self.bufs[-1].at[0]
@@ -243,11 +253,11 @@
 
 
 class QuickShard:
-    def __init__(self, place, dp_hops, blocks, scratch, sems, base, back_only=False):
+    def __init__(self, place, dp_hops, blocks, scratch, sems, base, back_only=False, array=None):
         n = len(dp_hops)
-        self.place, self.full, self.blocks = place, scratch[-1], blocks
+        self.place, self.full, self.array = place, scratch[-1], array
         got = None if back_only else scratch[n]
-        self.dp = Reduce(place, "dp", dp_hops, blocks, scratch[:n], sems, base)
+        self.dp = Reduce(place, "dp", dp_hops, blocks, scratch[:n], sems, base, array)
         base += n
         self.out = self.back = None
         if not back_only:
@@ -263,7 +273,7 @@
         self.done = 0
 
     def dp_total(self):
-        return self.dp.total() if self.dp.steps else self.blocks(())
+        return self.dp.total() if self.dp.steps else self.array
 
     def start(self, step):
         flow, i = self.stages[step]
@@ -272,7 +282,7 @@
             flow.start(i)
             return
         if flow is self.back and self.out is None:
-            self.full[self.place.me["table"]] = self.blocks(())[...]
+            self.full[self.place.me["table"]] = self.array[...]
         flow.start()
 
     def arrive(self, step):
@@ -308,8 +318,8 @@
 
 
 class Small:
-    def __init__(self, place, block, got_dp, part, got_table, sems, base):
-        self.place, self.block, self.part = place, block, part
+    def __init__(self, place, block, got_dp, part, got_table, sems, base, out):
+        self.place, self.block, self.part, self.out = place, block, part, out
         self.first = Swap(place, "dp", sems, base, block, lambda t, s: got_dp.at[s - 1])
         base += place.size["dp"] - 1
         self.second = Swap(
@@ -330,7 +340,7 @@
             total = self.part[...].astype(F32)
             for got in self.second.arrive():
                 total = total + got[...].astype(F32)
-            self.total = total
+            self.out[...] = total
 
     def sent(self):
         self.first.sent()
@@ -447,7 +457,7 @@
     dp_size, table_size, support_ref, feat_ref, mask_ref, ew_ref,
     v0_ref, v1_ref, v2_ref, v3_ref, v4_ref, v5_ref, ub_ref, wq_in, wk_in, wv_in, wo_in, wu_in, wd_in,
     q_ref, k_ref, v_ref, n_ref, emb_ref, mixed_ref, mixed_low_ref, p_ref, linv_ref,
-    x_out, wet_out, wq_out, wk_out, wv_out, vec_ref, bu_ref, wo_out, wu_out, wd_out,
+    x_out, wet_out, wq_out, wk_out, wv_out, vec_ref, bu_ref, wo_out, wu_out, wd_out, mask_out,
     x_buf, wet_buf, packed_buf, wq_buf, wk_buf, wv_buf, e_one, e_two, s_one, s_two, own_sem, send_sem, recv_sem,
 ):
     micro_id, head = pl.program_id(0), pl.program_id(1)
@@ -517,6 +527,8 @@
         wq_buf[dp] = wq_in[...]
 
         def fill(m):
+            mask_out[m] = jnp.zeros((8, LANES), F32)
+            mask_out[m, :, :feat] = jnp.broadcast_to(mask_ref[m].astype(F32), (8, feat))
             tall = jnp.concatenate(
                 [feat_ref[m].astype(F32), jnp.zeros((LANES - feat, rows), F32)], axis=0
             ).T
@@ -651,13 +663,15 @@
         + [micro_spec((length, LANES))]
         + [far] * 4
         + [const_spec((8, width)), const_spec((1, wu.shape[1]))]
-        + [far] * 3,
+        + [far] * 3
+        + [const_spec((micro, 8, LANES))],
         out_shape=[jax.ShapeDtypeStruct((micro,) + s, d) for s, d in out]
         + [jax.ShapeDtypeStruct((micro, HEADS) + s, d) for s, d in heads]
         + [jax.ShapeDtypeStruct((micro, length, LANES), BF16)]
         + [wet, gathered(wq), gathered(wk), gathered(wv)]
         + [jax.ShapeDtypeStruct((8, width), F32), jax.ShapeDtypeStruct((1, wu.shape[1]), F32)]
-        + [gathered(wo), gathered(wu), gathered(wd)],
+        + [gathered(wo), gathered(wu), gathered(wd)]
+        + [jax.ShapeDtypeStruct((micro, 8, LANES), F32)],
         scratch_shapes=[
             pltpu.VMEM((micro, table_size, rows, LANES), BF16),
             pltpu.VMEM(wet.shape, BF16),
@@ -820,7 +834,7 @@
 
     mixed_in, emb_in, cot_in, wo_in, wu_in, wd_in, vec_ref, bu_ref = take(8)
     act_out, ghid_out, gmix_out, dwo_out, small_out = take(5)
-    part_outs = [take(2) for _ in range(CHUNKS)]
+    part_outs = take(4)
     mixed_s, emb_s, cot_s, wo_s, wu_s, wd_s = take(6)
     normed_s, normed_t, g_out_t, unit_s, out_s, gn2_s = take(6)
     act_s, gmix_s, ghid_s = normed_s, normed_t, emb_s
@@ -842,7 +856,7 @@
         for grad, order, scr in zip(grads[f], (forth, back), scratch[f]):
             pair.append(
                 QuickShard(
-                    place, order, lambda s, grad=grad: grad.at[toggled_by(place.me["dp"], s)], scr,
+                    place, order, lambda s, grad=grad: grad.at[place.toggled("dp", s)], scr,
                     (send_sem, recv_sem), base,
                 )
             )
@@ -862,7 +876,7 @@
     def add(ref, first, value):
         ref[...] = value if first else ref[...] + value
 
-    upto = {0: 5, 1: 4, 2: 3, 3: 2}
+    upto = {0: 4, 1: 3, 2: 1, 3: 1}
 
     def step(f, i):
         for flow in flows[f]:
@@ -870,12 +884,6 @@
                 flow.arrive(i - 1)
             if i < upto[f]:
                 flow.start(i)
-
-    def at(c, *steps):
-        @pl.when(chunk == c)
-        def _():
-            for f, i in steps:
-                step(f, i)
 
     @pl.when(chunk == 0)
     def _():
@@ -942,13 +950,6 @@
         add(acc_u, m == 0, dot_nn(normed_t[m], g_pre))
         bias_rows = bias_rows + row_sum(g_pre_f)
         gn2_s[m] += dot_nt(g_pre, wu_c[...])
-        if m == 0:
-            at(2, (0, 2))
-            at(3, (0, 3), (1, 2))
-        if m == 1:
-            at(1, (0, 1))
-            at(2, (1, 1))
-            at(3, (2, 1))
     row = lax.broadcasted_iota(jnp.int32, (8, width), 0)
     small_out[8:16, :] += jnp.where(row == chunk, jnp.broadcast_to(bias_rows, (8, width)), 0.0)
     up, down = acc_u[...].astype(BF16), acc_d[...].T.astype(BF16)
@@ -958,17 +959,14 @@
         def _():
             grads[f][0][...] = up.reshape(grads[f][0].shape)
             grads[f][1][...] = down.reshape(grads[f][1].shape)
-            step(f, 0)
+            for k in range(f + 1):
+                if f - k < upto[k]:
+                    step(k, f - k)
 
     @pl.when(chunk == last)
     def _():
-        step(0, 4)
-        step(1, 3)
-        step(2, 2)
         outs = []
         for m in range(micro):
-            if m == 2:
-                step(3, 1)
             act_s[m] = out_s[m].astype(BF16)
             unit, g_norm = unit_s[m], gn2_s[m]
             g_out_f = cot_s[m].astype(F32)
@@ -987,10 +985,11 @@
         for f in range(CHUNKS):
             step(f, upto[f])
         for i in range(2):
-            part_outs[0][i][...] = flows[0][i].full[...]
-            part_outs[1][i][...] = flows[1][i].full[place.me["table"]]
-            part_outs[2][i][...] = flows[2][i].dp_total()[...]
-            part_outs[3][i][...] = flows[3][i].dp.bufs[1][...]
+            side = slice(i * width, (i + 1) * width)
+            part_outs[3][:, side] = flows[0][i].full[place.me["table"]]
+            part_outs[2][:, :, side] = flows[1][i].dp_total()[...]
+            part_outs[i][:, :, :, :width] = flows[2][i].dp.bufs[0][...]
+            part_outs[i][:, :, :, width:] = flows[3][i].dp.bufs[0][...]
         for f in range(CHUNKS):
             for flow in flows[f]:
                 flow.done = upto[f]
@@ -1007,7 +1006,8 @@
     far = pl.BlockSpec(memory_space=pl.ANY)
     whole = pl.BlockSpec(memory_space=pltpu.VMEM)
     block = (table_size, width // dp_size // table_size, width)
-    parts = [block, block[1:], block, (2,) + block]
+    two = block[:2] + (2 * width,)
+    parts = [(4,) + two, (4,) + two, two, two[1:]]
     hops = len(hops_of(dp_size))
 
     def per_micro(dtype):
@@ -1032,10 +1032,10 @@
         functools.partial(mlp_reduce_kernel, dp_size, table_size),
         grid=(CHUNKS,),
         in_specs=[far] * 6 + [whole] * 2,
-        out_specs=[far] * 3 + [whole] * (2 + 2 * CHUNKS),
+        out_specs=[far] * 3 + [whole] * 6,
         out_shape=[jax.ShapeDtypeStruct((micro, rows, width), d) for d in (BF16, F32, BF16)]
-        + [jax.ShapeDtypeStruct((dp_size,) + block, BF16), jax.ShapeDtypeStruct((16, width), F32)]
-        + [jax.ShapeDtypeStruct(p, BF16) for p in parts for _ in range(2)],
+        + [jax.ShapeDtypeStruct((dp_size, width // dp_size, width), BF16), jax.ShapeDtypeStruct((16, width), F32)]
+        + [jax.ShapeDtypeStruct(p, BF16) for p in parts],
         scratch_shapes=scratch,
         compiler_params=vmem(60, collective_id=2, has_side_effects=True),
         name="mlp_both_reduce",
@@ -1306,16 +1306,17 @@
 
     ins = take(15)
     vec_ref, wq_ref, wk_ref, wv_ref = ins[11:15]
-    parts = take(7)
+    parts = take(5)
     (small_in,) = take(1)
-    ig_out, small_out, embed_out = take(3)
-    totals = take(11)
+    ig_out, small_out, embed_out, dwo_out = take(4)
+    totals = take(8)
     core = take(8)
     sums_ref, acc_e, acc_q, acc_kv = core[0], *core[5:8]
     bufs = take(6)
     place = Place(dp_size, table_size)
     hops = place.hops["dp"]
-    part_scratch = [take(n) for n in [len(hops) + 2] + [3] * 2 + [2] * 2 + [1] * 2]
+    out_scratch = take(3)
+    part_scratch = [take(n) for n in (4, 4, 2, 1)]
     tail_grads = take(4)
     tail_scratch = [take(len(hops) + 2) for _ in range(4)]
     embed_grad, small_grad = take(2)
@@ -1334,31 +1335,28 @@
         base += n
         return base - n
 
-    def quick(order, blocks, scratch, back_only=False):
+    def quick(order, blocks, scratch, back_only=False, array=None):
         at = count_up(quick_sems(len(order), table_size, back_only))
-        return QuickShard(place, order, blocks, scratch, sems, at, back_only)
-
-    def by_owner(grad):
-        return lambda s: grad.at[toggled_by(place.me["dp"], s)]
-
-    out_flow = quick(forth, by_owner(parts[0]), part_scratch[0])
-    thirds = [
-        quick(order[-1:], lambda s, p=p: p.at[len(s)], scr)
-        for order, p, scr in zip((forth, back), parts[1:3], part_scratch[1:3])
-    ]
-    seconds = [quick([], lambda s, p=p: p, scr) for p, scr in zip(parts[3:5], part_scratch[3:5])]
-    firsts = [quick([], lambda s, p=p: p, scr, True) for p, scr in zip(parts[5:], part_scratch[5:])]
-    mlp = [out_flow] + thirds + seconds + firsts
+        return QuickShard(place, order, blocks, scratch, sems, at, back_only, array)
+
+    mlp = []
+    for order, back_only, part, scr in zip((forth[1:], back[1:], [], []), (False,) * 3 + (True,), parts[1:], part_scratch):
+        mlp.append(quick(order, None, scr, back_only, part))
+    others = dp_size + table_size - 2
+    mlp_out = Small(place, lambda d: parts[0].at[d], *out_scratch, sems, count_up(others), dwo_out)
     tail = [
         [
-            quick(order, by_owner(tail_grads[2 * g + i]), tail_scratch[2 * g + i])
+            quick(
+                order,
+                lambda s, grad=tail_grads[2 * g + i]: grad.at[place.toggled("dp", s)],
+                tail_scratch[2 * g + i],
+            )
             for i, order in enumerate((forth, back))
         ]
         for g in range(2)
     ]
-    others = dp_size + table_size - 2
-    embed = Small(place, lambda d: embed_grad.at[d], *embed_scratch, sems, count_up(others))
-    small = Small(place, lambda d: small_grad.at[d // 2], *small_scratch_, sems, count_up(others))
+    embed = Small(place, lambda d: embed_grad.at[d], *embed_scratch, sems, count_up(others), embed_out)
+    small = Small(place, lambda d: small_grad.at[d // 2], *small_scratch_, sems, count_up(others), small_out)
     igs = []
     for m in range(micro):
         igs.append(
@@ -1394,39 +1392,43 @@
 
     last = micro - 1
     hooks.at(0, 0, lambda: place.greet(True)())
-    for i, (m, k) in enumerate(((0, 0), (0, 1), (0, 2), (1, 0), (1, 1), (1, 2))):
+    for i, (m, k) in enumerate(((0, 0), (0, 2), (1, 1), (2, 0), (2, 2))):
         hooks.at(m, k, hooks.step([f for f in mlp if i <= f.steps], i))
-    hooks.at(1, 2, hooks.ig_finish(0))
-    hooks.at(2, 1, hooks.step(tail[0], 1))
-    hooks.at(2, 2, hooks.step(tail[0], 2))
-    hooks.at(2, 3, hooks.ig_finish(1))
-    hooks.at(2, 3, hooks.step(tail[1], 1))
-    hooks.at(2, 4, hooks.step(tail[0], 3))
-    hooks.at(2, 5, hooks.step(tail[1], 2))
-
-    def finish():
-        embed_grad[...] = acc_e[...].T.astype(BF16).reshape(embed_grad.shape)
-        hooks.step([embed], 0)()
+    for i, (m, k) in enumerate(((0, 0), (0, 2), (1, 1))):
+        hooks.at(m, k, hooks.step([mlp_out], i))
+
+    def start_small():
         d_gain, d_shift = norm_one_grads(vec_ref, wq_ref, wk_ref, wv_ref, sums_ref, acc_q, acc_kv)
         for t in range(dp_size // 2):
             cols = slice(t * LANES, (t + 1) * LANES)
             small_grad[t] = small_in[:, cols]
             small_grad[t, 1:2, :] = d_gain[:, cols]
             small_grad[t, 2:3, :] = d_shift[:, cols]
-        ends = [embed, small]
         hooks.step([small], 0)()
+
+    hooks.at(2, 0, hooks.ig_finish(0))
+    hooks.at(2, 2, hooks.step(tail[0], 1))
+    hooks.at(2, 2, start_small)
+    hooks.at(2, 5, hooks.step(tail[1], 1))
+
+    def finish():
+        embed_grad[...] = acc_e[...].T.astype(BF16).reshape(embed_grad.shape)
+        hooks.step([embed], 0)()
+        hooks.step([small], 1)()
+        hooks.step(tail[0], 2)()
+        hooks.step(tail[1], 2)()
+        hooks.step(tail[0], 3)()
         hooks.step(tail[1], 3)()
+        hooks.ig_finish(1)()
+        hooks.step([embed], 1)()
         hooks.step(tail[0], 4)()
-        hooks.step(ends, 1)()
         hooks.step(tail[1], 4)()
+        hooks.ig_finish(last)()
+        hooks.step([small, embed], 2)()
         hooks.step(tail[0], 5)()
-        hooks.ig_finish(last)()
-        hooks.step(ends, 2)()
         hooks.step(tail[1], 5)()
-        for flow in mlp + tail[0] + tail[1] + ends + igs:
+        for flow in mlp + [mlp_out, small, embed] + tail[0] + tail[1] + igs:
             flow.sent()
-        embed_out[...] = embed.total
-        small_out[...] = small.total
         for flow, out in zip(mlp + tail[0] + tail[1], totals):
             out[...] = flow.full[...]
 
@@ -1491,12 +1493,14 @@
     shard = width // dp_size
     block = (table_size, shard // table_size, width)
     tail = (dp_size, table_size, shard // table_size, 3 * HEAD_DIM)
-    blocks = [block] * 7 + [tail[1:]] * 4
+    two = block[:2] + (2 * width,)
+    blocks = [two] * 4 + [tail[1:]] * 4
     hops = len(hops_of(dp_size))
-    kinds = [(hops, False)] + [(1, False)] * 2 + [(0, False)] * 2 + [(0, True)] * 2
+    kinds = [(2, False)] * 2 + [(0, False), (0, True)]
     scratch = back_scratch(length, rows, width) + back_buffers(rows, width)
+    scratch += small_scratch(dp_size, table_size, (shard, width), BF16)
     for n, back_only in kinds:
-        scratch += quick_scratch(n, table_size, block, BF16, back_only)
+        scratch += quick_scratch(n, table_size, two, BF16, back_only)
     scratch += [pltpu.VMEM(tail, BF16)] * 4
     for _ in range(4):
         scratch += quick_scratch(hops, table_size, tail[1:], BF16)
@@ -1508,15 +1512,15 @@
     scratch += [pltpu.VMEM((table_size - 1, rows, LANES), BF16)] * micro
     scratch += [pltpu.VMEM((rows, LANES), F32)]
     count = sum(quick_sems(n, table_size, back_only) for n, back_only in kinds + [(hops, False)] * 4)
-    count += 2 * (dp_size + table_size - 2) + micro * (table_size - 1)
+    count += 3 * (dp_size + table_size - 2) + micro * (table_size - 1)
     scratch += [pltpu.SemaphoreType.DMA((count,))] * 2
-    outs = [((micro, rows, LANES), F32), (tile, F32), ((shard, LANES), F32)]
+    outs = [((micro, rows, LANES), F32), (tile, F32), ((shard, LANES), F32), ((shard, width), F32)]
     outs += [(b, BF16) for b in blocks]
     return pl.pallas_call(
         functools.partial(attend_back_reduce_kernel, dp_size, table_size),
         grid=(micro, PAIRS),
         in_specs=back_specs((p, linv), (k, v, q, gmix, mixed), varied, fixed)
-        + [whole] * 7
+        + [whole] * 5
         + [const_spec(small.shape)],
         out_specs=[const_spec(shape) for shape, _ in outs],
         out_shape=[jax.ShapeDtypeStruct(shape, dtype) for shape, dtype in outs],
@@ -1527,23 +1531,30 @@
 
 
 def finish_kernel(feat, shard, mask_ref, ig_in, small_in, embed_in, *refs):
-    chunk_ins, out_in, pair_ins, outs = refs[: 2 * CHUNKS], refs[2 * CHUNKS], refs[2 * CHUNKS + 1 : 2 * CHUNKS + 5], refs[2 * CHUNKS + 5 :]
+    chunk_ins, out_in, pair_ins, outs = refs[:4], refs[4], refs[5:9], refs[9:]
     ig_out, dwe, dwq, dwk, dwv, dwo, dwu, dwd = outs[:8]
     vecs, bu = outs[8:14], outs[14]
     half = LANES // 2
     for m in range(ig_in.shape[0]):
-        ig_out[m] = ig_in[m].T[:feat, :] * mask_ref[m].astype(F32)
+        ig_out[m] = (ig_in[m] * mask_ref[m][:1]).T[:feat, :]
     dwe[...] = embed_in[:, :feat]
-    dwo[...] = out_in[...].astype(F32)
+    dwo[...] = out_in[...]
     lane = lax.broadcasted_iota(jnp.int32, (shard, LANES), 1)
-    ups, downs = chunk_ins[::2], chunk_ins[1::2]
-    for f in range(CHUNKS):
-        dwd[f * half : (f + 1) * half, :] = downs[f][...].astype(F32)
+    width = dwo.shape[1]
+    ups = [(3, 0), (2, 0), (0, 0), (0, width)]
+    downs = [(3, width), (2, width), (1, 0), (1, width)]
+    for f, (ref, side) in enumerate(downs):
+        dwd[f * half : (f + 1) * half, :] = chunk_ins[ref][:, side : side + width].astype(F32)
+
+    def up_tile(f, o):
+        ref, side = ups[f]
+        at = side + o // 2 * LANES
+        return chunk_ins[ref][:, at : at + LANES].astype(F32)
+
     per_owner = bu.shape[1]
     for o in range(dwu.shape[1] // per_owner):
         for f in range(0, CHUNKS, 2):
-            tile = slice(o // 2 * LANES, (o // 2 + 1) * LANES)
-            low, high = ups[f][:, tile].astype(F32), ups[f + 1][:, tile].astype(F32)
+            low, high = up_tile(f, o), up_tile(f + 1, o)
             at = o * per_owner + f * half
             dwu[:, at : at + LANES] = halves(lane, o % 2 * half, low, high)
     for g in range(HEADS // 2):
@@ -1605,18 +1616,15 @@
         q, k, v, n, emb, mixed, mixed_low, p, linv, x = got[:10]
         wet, wq, wk, wv = (g.reshape(-1, g.shape[-1]) for g in got[10:14])
         vec, bu = got[14:16]
-        wo, wu, wd = (g.reshape(-1, g.shape[-1]) for g in got[16:])
+        wo, wu, wd = (g.reshape(-1, g.shape[-1]) for g in got[16:19])
         activations, ghid, gmix, dwo, small, *parts = mlp_both_reduce(
             dp_size, table_size, mixed_low, emb, cotangent, wo, wu, wd, vec, bu
         )
-        ig, small, embed, *totals = attend_backward_reduce(
-            dp_size, table_size, [dwo] + parts[6:] + parts[4:6] + parts[2:4], small,
-            p, linv, k, v, q, gmix, mixed, n, x, ghid, wet, vec, wq, wk, wv,
+        ig, small, embed, dwo, *totals = attend_backward_reduce(
+            dp_size, table_size, [dwo] + parts, small, p, linv, k, v, q, gmix, mixed, n, x, ghid, wet, vec, wq, wk, wv
         )
         totals = [t.reshape(-1, t.shape[-1]) for t in totals]
-        chunks = [t.reshape(-1, t.shape[-1]) for t in parts[:2]] + totals[5:7] + totals[3:5] + totals[1:3]
-        mask = feature_mask.reshape(micro, feat, 1)
-        out = finish(feat, ff_shard, mask, ig, small, embed, chunks, totals[:1] + totals[7:])
+        out = finish(feat, ff_shard, got[-1], ig, small, embed, totals[:4], [dwo] + totals[4:])
         ig, dwe, dwq, dwk, dwv, dwo, dwu, dwd = out[:8]
         ig, dwe = ig.transpose(0, 2, 1), dwe.T
         smalls = [o.reshape(-1) for o in out[8:14]]

time: 205 us -> 201 us (0.980)
  Pallas kernels: 199 us -> 196 us
    pallas_call x1, Pallas kernels: 44.4 us -> 38.4 us  [mlp_both_reduce(): pl.pallas_call(functools.partial(mlp_reduce_kernel, dp_size, table_size),...]
    pallas_call x1, Pallas kernels: 91 us -> 93.9 us  [attend_backward_reduce(): pl.pallas_call(functools.partial(attend_back_reduce_kernel, dp_size, tabl...]
where the time goes in v4:
time: 201 us
  Pallas kernels  196 us (98%)
  local copies, waits for them, and re-layouts  3.68 us (2%)
    pallas_call x1, Pallas kernels, attend_backward_reduce(): pl.pallas_call(functools.partial(attend_back_reduce_kernel, dp_size, tabl...  93.9 us
    pallas_call x1, Pallas kernels, attend_forward_gather(): pl.pallas_call(functools.partial(attend_gather_kernel, dp_size, table_siz...  60.5 us
    pallas_call x1, Pallas kernels, mlp_both_reduce(): pl.pallas_call(functools.partial(mlp_reduce_kernel, dp_size, table_size),...  38.4 us

profile of v4, /device:TPU:0, one launch (start us, length us, event | category | flops | bytes accessed | tf_op | source)
XLA Modules:
  0.0 200.6 jit_solution(11891087343824909761)
XLA Ops:
  0.7 60.5 %attend_forward_gather.1 = (bf16[3,512,512]{2,1,0:T(8,128)(2,1)}, bf16[3,2048,512]{2,1,0:T(8,128)(2,1)}, bf16[3,2048,512]{2,1,0:T(8,128)(2,1)}, bf16[3,2048,512]...) custom-call(s32[3]{0:T(128)} %bitcast.60, ...), custom_call_target="tpu_custom_call" | custom-call | tf_op jit(solution)/shard_map/attend_forward_gather/pallas_call | solution.py:657
  61.2 38.4 %mlp_both_reduce.1 = (bf16[3,512,512]{2,1,0:T(8,128)(2,1)}, f32[3,512,512]{2,1,0:T(8,128)}, bf16[3,512,512]{2,1,0:T(8,128)(2,1)}, bf16[8,64,512]{2,1,0:T(8,128)(...) custom-call(bf16[3,512,512]{2,1,0:T(8,128)(2,1)} %get-tuple-element., ...), custom_call_target="tpu_custom_call" | custom-call | tf_op jit(solution)/shard_map/mlp_both_reduce/pallas_call | solution.py:1031
  99.6 93.9 %attend_backward_reduce.1 = (f32[3,512,128]{2,1,0:T(8,128)}, f32[16,128]{1,0:T(8,128)}, f32[64,128]{1,0:T(8,128)}, f32[64,512]{1,0:T(8,128)}, bf16[4,16,1024]{2,...) custom-call(bf16[3,4,512,2048]{3,2,1,0:T(8,128)(2,1)} %get-tuple-ele, ...), custom_call_target="tpu_custom_call" | custom-call | tf_op jit(solution)/shard_map/attend_backward_reduce/pallas_call | solution.py:1519
  193.5 0.0 copy-start
  193.5 3.5 %finish.1 = (f32[3,100,512]{2,1,0:T(8,128)}, f32[64,100]{1,0:T(8,128)}, f32[64,512]{1,0:T(8,128)}, f32[64,512]{1,0:T(8,128)}, f32[64,512]{1,0:T(8,128)}, /*index...) custom-call(f32[3,8,128]{2,1,0:T(8,128)} %get-tuple-element.80.mask_, ...), custom_call_target="tpu_custom_call" | custom-call | tf_op jit(solution)/shard_map/finish/pallas_call | solution.py:1591
  196.9 2.5 %copy.35 = f32[3,1,512,100]{2,1,3,0:T(1,128)} copy(f32[3,1,512,100]{2,3,0,1:T(8,128)} %bitcast.44) | data formatting | bytes 1228800
  199.5 0.0 copy-done
  199.5 1.1 copy.37
Async XLA Ops:
  193.5 6.0 %copy-start = (bf16[3,512,512]{2,1,0:T(8,128)(2,1)S(1)}, bf16[3,512,512]{2,1,0:T(8,128)(2,1)}, u32[]{:S(2)}) copy-start(bf16[3,512,512]{2,1,0:T(8,128)(2,1)} %get-tuple-element.79) | copy-start | bytes 4718596
